TPU v7x, 32 devices: a whole 2x2x4 slice. The times are simulated.
32 devices in a mesh: groups: 2 (over y), dp: 4 (over z), seq: 2 (over x), head: 2 (over core).
Axes of the slice: x: 2, y: 2, z: 4, core: 2. Of those that a mesh axis runs over, the one named last changes fastest.
Arguments:
- tokens: bfloat16 [8, 768, 6144], P(('groups', 'dp'), 'seq'), parts along dimension 0, may hold values from -8 to 8
- ln_gain: float32 [6144], replicated, may hold values from 0.1 to 1.9
- qkv_weight: bfloat16 [6144, 24, 384], P('dp', ('seq', 'head')), may hold values from -8 to 8
Outputs:
- attended: bfloat16 [8, 768, 3072], P(('groups', 'dp'), 'seq', 'head'), parts along dimension 0
There are 2 independent parts, one for each index of `groups`. A program takes and returns all parts, laid end to end along the dimension named above; an argument that names none is the same for every part. Nothing has to cross between parts.
All inputs are finite; a program needn't handle non-finite values.
Results may differ from a plain program's by a relative error of at most 0.012.
Values may be sent and summed in bfloat16 or wider, within the bound.
No kernel may reach another device: no remote copies, remote signals or barrier semaphores. Data moves between devices by JAX's collectives and lax.ppermute only.
A program may use at most 128 MiB of HBM per device.

v0:
```python
import math

import jax
import jax.numpy as jnp
from jax import lax
from jax.sharding import PartitionSpec as P


def normalize(array, gain):
    widened = array.astype(jnp.float32)
    centered = widened - jnp.mean(widened, axis=-1, keepdims=True)
    variance = jnp.mean(centered * centered, axis=-1, keepdims=True)
    return (centered * lax.rsqrt(variance + 1e-06) * gain).astype(jnp.bfloat16)


def attend(projected):
    width = projected.shape[2] // 3
    queries = projected[:, :, :width]
    key_rows = projected[:, :, width : 2 * width]
    value_rows = projected[:, :, 2 * width :]
    scores = jnp.einsum("qhd,khd->hqk", queries, key_rows, preferred_element_type=jnp.float32) * (
        1.0 / math.sqrt(width)
    )
    highest = jnp.max(scores, axis=-1, keepdims=True)
    expo = jnp.exp(scores - highest)
    probs = (expo / jnp.sum(expo, axis=-1, keepdims=True)).astype(jnp.bfloat16)
    mixed = jnp.einsum("hqk,khd->qhd", probs, value_rows, preferred_element_type=jnp.float32)
    return mixed.astype(jnp.bfloat16).reshape(projected.shape[0], -1)


def per_device(tokens, ln_gain, qkv_weight):
    images = tokens.shape[0]
    width = tokens.shape[2]
    heads_here = qkv_weight.shape[1]
    columns = heads_here * qkv_weight.shape[2]
    source = normalize(tokens, ln_gain)
    half_width = width // lax.axis_size("head")
    core_index = lax.axis_index("head")
    own_half = lax.dynamic_slice_in_dim(source, core_index * half_width, half_width, 2)
    fetched = lax.all_gather(own_half, "seq", axis=1, tiled=True)
    gathered = lax.all_gather(fetched, "head", axis=2, tiled=True)
    full_tokens = gathered.shape[1]
    features = gathered.reshape(images * full_tokens, width)
    piece = lax.all_gather(qkv_weight, "dp", axis=0, tiled=True)
    projected = jnp.dot(
        features, piece.reshape(piece.shape[0], columns), preferred_element_type=jnp.float32
    )
    projected = projected.astype(jnp.bfloat16).reshape(
        images, full_tokens, heads_here, qkv_weight.shape[2]
    )
    mixed = lax.map(attend, projected)
    return lax.all_to_all(mixed, "seq", split_axis=1, concat_axis=2, tiled=True)


def solution(mesh):
    return jax.shard_map(
        per_device,
        mesh=mesh,
        in_specs=(P(("groups", "dp"), "seq", None), P(), P("dp", ("seq", "head"), None)),
        out_specs=P(("groups", "dp"), "seq", "head"),
        check_vma=False,
    )
```

profile of v0, /device:TPU:0, one launch (start us, length us, event | category | flops | bytes accessed | tf_op | source)
XLA Modules:
  0.0 679.9 jit_solution(12576983428977995891)
XLA Ops:
  6.5 0.0 all-gather.4.cloned.1.call-start
  6.5 0.0 copy-start
  6.5 3.2 convert_reduce_fusion
  9.7 0.6 copy-done
  10.3 0.0 copy-start.1
  10.3 4.9 multiply_reduce_fusion.1
  15.2 0.0 copy-done.1
  15.2 4.5 fusion.12
  19.7 0.0 all-gather.4.cloned.1.call-update
  19.7 0.0 all-gather.6.cloned.1.call-start
  19.8 65.5 %all-gather.4.cloned.1.call-done = bf16[1,768,3072]{2,1,0:T(8,128)(2,1)} async-done(((bf16[1,384,3072]{2,1,0:T(8,128)(2,1)}), bf16[1,768,3072]{2,1,0:T(8,128)(2,1)}) %all-gather.4.cloned.1.call-update) | async-done | bytes 4718608 | tf_op jit(solution)/shard_map/all_gather | solution.py:40
  85.2 0.0 all-gather.6.cloned.1.call-update
  85.2 0.2 all-gather.8.cloned.1.call-start
  85.5 10.4 %copy.28 = bf16[1536,6,384]{0,2,1:T(8,128)(2,1)} copy(bf16[1536,6,384]{2,0,1:T(8,128)(2,1)} %param.5) | data formatting | bytes 14155776 | tf_op args[2]
  95.8 0.0 all-gather.8.cloned.1.call-update
  95.9 12.8 %all-gather.6.cloned.1.call-done = bf16[1,768,6144]{2,1,0:T(8,128)(2,1)} async-done(((bf16[1,768,3072]{2,1,0:T(8,128)(2,1)}), bf16[1,768,6144]{2,1,0:T(8,128)(2,1)}) %all-gather.6.cloned.1.call-update) | async-done | bytes 9437200 | tf_op jit(solution)/shard_map/all_gather | solution.py:41
  108.6 478.9 %all-gather.8.cloned.1.call-done = bf16[6144,6,384]{0,2,1:T(8,128)(2,1)} async-done(((bf16[1536,6,384]{0,2,1:T(8,128)(2,1)}), bf16[6144,6,384]{0,2,1:T(8,128)(2,1)}) %all-gather.8.cloned.1.call-update) | async-done | bytes 28311568 | tf_op jit(solution)/shard_map/all_gather | solution.py:44
  587.6 29.9 %fusion.8 = bf16[768,2304]{1,0:T(8,128)(2,1)} fusion(bf16[6144,2304]{0,1:T(8,128)(2,1)} %bitcast.24, bf16[1,768,6144]{2,1,0:T(8,128)(2,1)} %all-gather.6.cloned.1.call-done), kind=kOutput, calls=%fused_computation.12 | convolution fusion | flops 21745041408 | bytes 41287680 | tf_op jit(solution)/shard_map/dot_general | solution.py:45
  617.5 4.5 copy.29
  622.0 8.2 %fusion.29 = (f32[6,768]{1,0:T(8,128)}, f32[6,768,768]{1,2,0:T(8,128)}) fusion(bf16[768,6,384]{0,2,1:T(8,128)(2,1)S(1)} %bitcast.21), kind=kOutput, calls=%fused_computation.27 | convolution fusion | flops 916587264 | bytes 16533504 | tf_op jit(solution)/shard_map/while/body/eval_jaxpr/sub | solution.py:25
  630.2 7.1 %fusion.15 = bf16[6,128,768]{2,1,0:T(8,128)(2,1)} fusion(f32[6,768,768]{1,2,0:T(8,128)} %get-tuple-element.17, f32[6,768]{1,0:T(8,128)} %get-tuple-element.16, bf16[768,6,384]{0,2,1:T(8,128)(2,1)S(1)} %bitcast.22), kind=kOutput, calls=%fused_computation.17 | convolution fusion | flops 913637376 | bytes 16533504 | tf_op jit(solution)/shard_map/while/body/eval_jaxpr/hqk,khd->qhd/dot_general | solution.py:27
  637.3 6.0 copy.33
  643.3 0.5 broadcast.41
  643.8 7.8 %reduce.2 = bf16[768,768]{1,0:T(8,128)(2,1)S(1)} reduce(bf16[768,1,768]{2,1,0:T(2,128)(2,1)S(1)} %bitcast.17, bf16[]{:T(256)} %broadcast.41), dimensions={1}, to_apply=%bitcast.14.reduce_sub_computation | reduce | bytes 2359298
  651.7 0.3 reshape.40
  652.0 18.0 %all_to_all.18 = bf16[2,2,147456]{2,1,0:T(2,128)(2,1)S(1)} all-to-all(bf16[2,2,147456]{2,1,0:T(2,128)(2,1)S(1)} %reshape.40), channel_id=1, replica_groups=mesh['groups'=2,'dp'=4,'seq'=2,'head'=2] {'seq'}, dimensions={0} | all-to-all | bytes 2359296 | tf_op jit(solution)/shard_map/all_to_all | solution.py:52
  670.0 1.0 reshape.41
  671.0 0.2 copy.37
  671.2 0.7 copy.34
  671.9 1.5 copy.35
  (3 shorter events, 0.0 us)
Async XLA Ops:
  6.5 78.7 %all-gather.4.cloned.1.call-start = ((), (), s32[]{:S(2)}) async-start(), calls=%async_computation.1 | async-start | bytes 7077888 | tf_op jit(solution)/shard_map/all_gather | solution.py:40
  6.5 3.8 copy-start
  10.3 4.9 copy-start.1
  19.7 88.9 %all-gather.6.cloned.1.call-start = ((), (), s32[]{:S(2)}) async-start(), calls=%async_computation.2 | async-start | bytes 14155776 | tf_op jit(solution)/shard_map/all_gather | solution.py:41
  85.2 502.3 %all-gather.8.cloned.1.call-start = ((), (), s32[]{:S(2)}) async-start(), calls=%async_computation.3 | async-start | bytes 35389440 | tf_op jit(solution)/shard_map/all_gather | solution.py:44
Sparse Core Ops, SparseCore 0:
  19.8 65.3 all-gather.3
  86.8 21.8 all-gather.5
  110.2 477.2 all-gather.7
where the time goes:
time: 680 us
  waiting for transfers between devices  557 us (82%)
  matrix products  45.2 us (7%)
  local copies, waits for them, and re-layouts  25.6 us (4%)
  other arithmetic  20.4 us (3%)
  blocking collectives  18 us (3%)
  between operations  13.2 us (2%)
    all_gather x1, waiting for transfers between devices, per_device(): piece = lax.all_gather(qkv_weight, 'dp', axis=0, tiled=True)  479 us
    all_gather x1, waiting for transfers between devices, per_device(): fetched = lax.all_gather(own_half, 'seq', axis=1, tiled=True)  65.5 us
    dot_general x1, matrix products, per_device(): jnp.dot(features, piece.reshape(piece.shape[0], columns), preferred_eleme...  29.9 us
    all_to_all x1, blocking collectives, per_device(): return lax.all_to_all(mixed, 'seq', split_axis=1, concat_axis=2, tiled=True)  18 us
  transfers between devices with their start and end apart: 3, of which 3 were waited for; matrix products, arithmetic and copies ran while one was open for 2% of the time, Pallas kernels for 0%

commit v1 on v0

--- a/solution.py
+++ b/solution.py
@@ -28,7 +28,7 @@
     return mixed.astype(jnp.bfloat16).reshape(projected.shape[0], -1)
 
 
-def per_device(tokens, ln_gain, qkv_weight):
+def plain(tokens, ln_gain, qkv_weight):
     images = tokens.shape[0]
     width = tokens.shape[2]
     heads_here = qkv_weight.shape[1]
@@ -52,6 +52,36 @@
     return lax.all_to_all(mixed, "seq", split_axis=1, concat_axis=2, tiled=True)
 
 
+def shared(tokens, ln_gain, qkv_weight):
+    groups, seqs, cores = (lax.axis_size(a) for a in ("groups", "seq", "head"))
+    _, rows, width = tokens.shape
+    heads, head_cols = qkv_weight.shape[1] // groups, qkv_weight.shape[2]
+    depth = head_cols // 3
+    part = rows // cores
+    own = lax.dynamic_slice_in_dim(tokens[0], lax.axis_index("head") * part, part, 0)
+    normed = normalize(own, ln_gain)
+    features = lax.all_gather(normed, ("groups", "seq", "head"), axis=0, tiled=True)
+    first = lax.axis_index("groups") * heads
+    mixed = []
+    for j in range(heads):
+        piece = lax.dynamic_slice_in_dim(qkv_weight, first + j, 1, 1)[:, 0]
+        weight = lax.all_gather(piece, "dp", axis=0, tiled=True)
+        projected = jnp.dot(features, weight, preferred_element_type=jnp.float32)
+        projected = projected.astype(jnp.bfloat16).reshape(groups, seqs * rows, 1, head_cols)
+        mixed.append(jnp.stack([attend(projected[g]) for g in range(groups)]))
+    out = jnp.concatenate(mixed, axis=-1).reshape(groups * seqs, rows, heads * depth)
+    out = lax.all_to_all(out, ("groups", "seq"), split_axis=0, concat_axis=0, tiled=True)
+    out = out.reshape(groups, seqs, rows, heads * depth).transpose(2, 1, 0, 3)
+    return out.reshape(1, rows, seqs * groups * heads * depth)
+
+
+def per_device(tokens, ln_gain, qkv_weight):
+    groups, cores = lax.axis_size("groups"), lax.axis_size("head")
+    if tokens.shape[0] == 1 and qkv_weight.shape[1] % groups == 0 and tokens.shape[1] % cores == 0:
+        return shared(tokens, ln_gain, qkv_weight)
+    return plain(tokens, ln_gain, qkv_weight)
+
+
 def solution(mesh):
     return jax.shard_map(
         per_device,

time: 680 us -> 436 us (0.64)
  waiting for transfers between devices: 557 us -> 334 us
  local copies, waits for them, and re-layouts: 25.6 us -> 7.22 us
  other arithmetic: 20.4 us -> 9.62 us
  matrix products: 45.2 us -> 52.2 us
    all_gather x3 -> x4, waiting for transfers between devices: 557 us -> 333 us  [the longest x3 234 us: shared(): weight = lax.all_gather(piece, 'dp', axis=0, tiled=True)]
    dot_general x1 -> x9, matrix products: 29.9 us -> 48.3 us  [the longest x3 45.5 us: shared(): projected = jnp.dot(features, weight, preferred_element_type=jnp.float32)]
    unnamed x9 -> x4, local copies, waits for them, and re-layouts: 13 us -> 0.01 us
    sub x1 -> x0, matrix products: 8.18 us -> none  [attend(): expo = jnp.exp(scores - highest)]
    unnamed x1 -> x0, other arithmetic: 7.83 us -> none
  transfers between devices with their start and end apart: 3 -> 4, of which waited for: 3 -> 4; matrix products, arithmetic and copies ran while one was open for 2% -> 9% of each run, Pallas kernels for 0% -> 0%
where the time goes in v1:
time: 436 us; the launch traced here: 435 us
  waiting for transfers between devices  334 us (77%)
  matrix products  52.2 us (12%)
  blocking collectives  19.1 us (4%)
  between operations  13.3 us (3%)
  other arithmetic  9.62 us (2%)
  local copies, waits for them, and re-layouts  7.22 us (2%)
    all_gather x3, waiting for transfers between devices, shared(): weight = lax.all_gather(piece, 'dp', axis=0, tiled=True)  234 us
    all_gather x1, waiting for transfers between devices, shared(): lax.all_gather(normed, ('groups', 'seq', 'head'), axis=0, tiled=True)  99.1 us
    dot_general x3, matrix products, shared(): projected = jnp.dot(features, weight, preferred_element_type=jnp.float32)  45.5 us
    all_to_all x1, blocking collectives, shared(): lax.all_to_all(out, ('groups', 'seq'), split_axis=0, concat_axis=0, tiled...  19.1 us
  transfers between devices with their start and end apart: 4, of which 4 were waited for; matrix products, arithmetic and copies ran while one was open for 9% of the time, Pallas kernels for 0%

profile of v1, /device:TPU:0, one launch (start us, length us, event | category | flops | bytes accessed | tf_op | source)
XLA Modules:
  0.0 435.5 jit_solution(16913165070813163666)
XLA Ops:
  6.5 0.0 all-gather.10.cloned.1.call-start
  6.5 3.9 constant_dynamic-slice_fusion.2
  10.4 0.0 copy-start.1
  10.4 0.0 all-gather.10.cloned.1.call-update
  10.4 0.0 all-gather.8.cloned.1.call-start
  10.5 0.0 copy-start
  10.5 2.2 convert_reduce_fusion
  12.7 2.4 fusion.3
  15.2 0.0 copy-done.1
  15.2 0.0 copy-done
  15.2 2.3 fusion.5
  17.5 0.0 all-gather.8.cloned.1.call-update
  17.5 0.0 all-gather.14.cloned.1.call-start
  17.6 0.7 all-gather.14.cloned.1.call-update
  18.3 0.0 all-gather.12.cloned.1.call-start
  18.3 0.5 all-gather.12.cloned.1.call-update
  18.9 83.9 %all-gather.10.cloned.1.call-done = bf16[6144,1,384]{2,0,1:T(8,128)(2,1)} async-done(((bf16[1536,1,384]{2,0,1:T(8,128)(2,1)}), bf16[6144,1,384]{2,0,1:T(8,128)(2,1)}) %all-gather.10.cloned.1.call-update) | async-done | bytes 4718608 | tf_op jit(solution)/shard_map/all_gather | solution.py:68
  102.7 99.1 %all-gather.8.cloned.1.call-done = bf16[1536,6144]{1,0:T(8,128)(2,1)} async-done(((bf16[192,6144]{1,0:T(8,128)(2,1)}), bf16[1536,6144]{1,0:T(8,128)(2,1)}) %all-gather.8.cloned.1.call-update) | async-done | bytes 18874384 | tf_op jit(solution)/shard_map/all_gather | solution.py:63
  201.8 15.2 %fusion.12 = bf16[1536,384]{1,0:T(8,128)(2,1)S(1)} fusion(bf16[1536,6144]{1,0:T(8,128)(2,1)} %all-gather.8.cloned.1.call-done, bf16[6144,1,384]{2,0,1:T(8,128)(2,1)} %all-gather.10.cloned.1.call-done), kind=kOutput, calls=%fused_computation.14 | convolution fusion | flops 7248347136 | bytes 24772608 | tf_op jit(solution)/shard_map/dot_general | solution.py:69
  217.0 0.1 slice_bitcast_fusion.5
  217.1 75.7 %all-gather.14.cloned.1.call-done = bf16[6144,1,384]{2,0,1:T(8,128)(2,1)} async-done(((bf16[1536,1,384]{2,0,1:T(8,128)(2,1)}), bf16[6144,1,384]{2,0,1:T(8,128)(2,1)}) %all-gather.14.cloned.1.call-update) | async-done | bytes 4718608 | tf_op jit(solution)/shard_map/all_gather | solution.py:68
  292.8 15.1 %fusion.18 = bf16[1536,384]{1,0:T(8,128)(2,1)S(1)} fusion(bf16[1536,6144]{1,0:T(8,128)(2,1)} %all-gather.8.cloned.1.call-done, bf16[6144,1,384]{2,0,1:T(8,128)(2,1)} %all-gather.14.cloned.1.call-done), kind=kOutput, calls=%fused_computation.16 | convolution fusion | flops 7248347136 | bytes 24772608 | tf_op jit(solution)/shard_map/dot_general | solution.py:69
  307.9 0.1 slice_bitcast_fusion.1
  308.1 74.1 %all-gather.12.cloned.1.call-done = bf16[6144,1,384]{2,0,1:T(8,128)(2,1)} async-done(((bf16[1536,1,384]{2,0,1:T(8,128)(2,1)}), bf16[6144,1,384]{2,0,1:T(8,128)(2,1)}) %all-gather.12.cloned.1.call-update) | async-done | bytes 4718608 | tf_op jit(solution)/shard_map/all_gather | solution.py:68
  382.1 15.3 %fusion.15 = bf16[1536,384]{1,0:T(8,128)(2,1)S(1)} fusion(bf16[1536,6144]{1,0:T(8,128)(2,1)} %all-gather.8.cloned.1.call-done, bf16[6144,1,384]{2,0,1:T(8,128)(2,1)} %all-gather.12.cloned.1.call-done), kind=kOutput, calls=%fused_computation.15 | convolution fusion | flops 7248347136 | bytes 24772608 | tf_op jit(solution)/shard_map/dot_general | solution.py:69
  397.4 0.1 slice_bitcast_fusion.3
  397.6 0.5 multiply_reduce_fusion.3
  398.0 0.4 fusion.23
  398.5 0.6 fusion.41
  399.1 0.5 multiply_reduce_fusion.2
  399.6 0.4 fusion.24
  400.0 0.6 fusion.42
  400.6 0.5 multiply_reduce_fusion.1
  401.1 0.4 fusion.25
  401.5 0.6 fusion.43
  402.2 0.5 multiply_reduce_fusion
  402.6 0.4 fusion.26
  403.1 0.6 fusion.44
  403.7 0.5 multiply_reduce_fusion.5
  404.2 0.4 fusion.21
  404.6 0.6 fusion.39
  405.3 0.5 multiply_reduce_fusion.4
  405.7 0.4 fusion.22
  406.2 0.6 fusion.40
  406.8 0.1 maximum_maximum_fusion
  406.9 0.7 copy.5
  407.6 19.1 %all_to_all.5 = bf16[4,384,384]{2,1,0:T(8,128)(2,1)S(1)} all-to-all(bf16[4,384,384]{2,1,0:T(8,128)(2,1)S(1)} %bitcast.163), channel_id=1, replica_groups=mesh['groups'=2,'dp'=4,'seq'=2,'head'=2] {'groups','seq'}, dimensions={0} | all-to-all | bytes 2359296 | tf_op jit(solution)/shard_map/all_to_all | solution.py:73
  426.7 0.8 copy.6
  427.5 1.5 copy.7
  (2 shorter events, 0.0 us)
Async XLA Ops:
  6.5 96.2 %all-gather.10.cloned.1.call-start = ((), (), s32[]{:S(2)}) async-start(), calls=%async_computation.2 | async-start | bytes 5898240 | tf_op jit(solution)/shard_map/all_gather | solution.py:68
  10.4 4.8 %copy-start.1 = (f32[6144]{0:T(1024)S(1)}, f32[6144]{0:T(1024)}, u32[]{:S(2)}) copy-start(f32[6144]{0:T(1024)} %param.4) | copy-start | bytes 73732
  10.4 191.4 %all-gather.8.cloned.1.call-start = ((), (), s32[]{:S(2)}) async-start(), calls=%async_computation.1 | async-start | bytes 21233664 | tf_op jit(solution)/shard_map/all_gather | solution.py:63
  10.5 4.7 %copy-start = (bf16[1,384,6144]{2,1,0:T(8,128)(2,1)S(1)}, bf16[1,384,6144]{2,1,0:T(8,128)(2,1)}, u32[]{:S(2)}) copy-start(bf16[1,384,6144]{2,1,0:T(8,128)(2,1)} %param.3) | copy-start | bytes 14155780
  17.5 275.3 %all-gather.14.cloned.1.call-start = ((), (), s32[]{:S(2)}) async-start(), calls=%async_computation.4 | async-start | bytes 5898240 | tf_op jit(solution)/shard_map/all_gather | solution.py:68
  18.3 363.9 %all-gather.12.cloned.1.call-start = ((), (), s32[]{:S(2)}) async-start(), calls=%async_computation.3 | async-start | bytes 5898240 | tf_op jit(solution)/shard_map/all_gather | solution.py:68
Sparse Core Ops, SparseCore 0:
  10.6 92.1 all-gather.9
  104.6 97.1 all-gather.7
  203.4 89.4 all-gather.13
  294.2 87.8 all-gather.11

commit v2 on v1

--- a/solution.py
+++ b/solution.py
@@ -3,6 +3,8 @@
 import jax
 import jax.numpy as jnp
 from jax import lax
+from jax.experimental import pallas as pl
+from jax.experimental.pallas import tpu as pltpu
 from jax.sharding import PartitionSpec as P
 
 
@@ -52,32 +54,118 @@
     return lax.all_to_all(mixed, "seq", split_axis=1, concat_axis=2, tiled=True)
 
 
+def attend_kernel(projected_ref, mixed_ref):
+    tokens, columns = projected_ref.shape
+    width = columns // 3
+    step = 256 if tokens % 256 == 0 else tokens
+    key_rows = projected_ref[:, width : 2 * width]
+    value_rows = projected_ref[:, 2 * width :]
+    for begin in range(0, tokens, step):
+        queries = projected_ref[begin : begin + step, :width]
+        scores = lax.dot_general(
+            queries, key_rows, (((1,), (1,)), ((), ())), preferred_element_type=jnp.float32
+        ) * (1.0 / math.sqrt(width))
+        expo = jnp.exp(scores - jnp.max(scores, axis=-1, keepdims=True))
+        probs = (expo / jnp.sum(expo, axis=-1, keepdims=True)).astype(jnp.bfloat16)
+        mixed = jnp.dot(probs, value_rows, preferred_element_type=jnp.float32)
+        mixed_ref[begin : begin + step, :] = mixed.astype(jnp.bfloat16)
+
+
+def attend_images(projected, images):
+    tokens, columns = projected.shape[0] // images, projected.shape[1]
+    width = columns // 3
+    return pl.pallas_call(
+        attend_kernel,
+        grid=(images,),
+        out_shape=jax.ShapeDtypeStruct((images * tokens, width), jnp.bfloat16),
+        in_specs=[pl.BlockSpec((tokens, columns), lambda i: (i, 0))],
+        out_specs=pl.BlockSpec((tokens, width), lambda i: (i, 0)),
+        compiler_params=pltpu.CompilerParams(vmem_limit_bytes=32 << 20),
+        cost_estimate=pl.CostEstimate(
+            flops=4 * images * tokens * tokens * width,
+            bytes_accessed=2 * images * tokens * (columns + width),
+            transcendentals=images * tokens * tokens,
+        ),
+    )(projected)
+
+
 def shared(tokens, ln_gain, qkv_weight):
     groups, seqs, cores = (lax.axis_size(a) for a in ("groups", "seq", "head"))
+    group, seq, core, plane = (lax.axis_index(a) for a in ("groups", "seq", "head", "dp"))
     _, rows, width = tokens.shape
     heads, head_cols = qkv_weight.shape[1] // groups, qkv_weight.shape[2]
     depth = head_cols // 3
+    slab = qkv_weight.shape[0]
+    inner = (plane == 1) | (plane == 2)
+
+    order = (plane, plane ^ 1, 2 - plane // 2, 3 - 3 * (plane // 2))
     part = rows // cores
-    own = lax.dynamic_slice_in_dim(tokens[0], lax.axis_index("head") * part, part, 0)
+    own = lax.dynamic_slice_in_dim(tokens[0], core * part, part, 0)
     normed = normalize(own, ln_gain)
+    normed = jnp.concatenate(
+        [lax.dynamic_slice_in_dim(normed, k * slab, slab, 1) for k in order], axis=1
+    )
     features = lax.all_gather(normed, ("groups", "seq", "head"), axis=0, tiled=True)
-    first = lax.axis_index("groups") * heads
-    mixed = []
+
+    pairs = [(0, 1), (1, 0), (2, 3), (3, 2)]
+    middle = [(1, 2), (2, 1)]
+    ends = [(1, 0), (2, 3)]
+    pieces, after = [], None
     for j in range(heads):
-        piece = lax.dynamic_slice_in_dim(qkv_weight, first + j, 1, 1)[:, 0]
-        weight = lax.all_gather(piece, "dp", axis=0, tiled=True)
-        projected = jnp.dot(features, weight, preferred_element_type=jnp.float32)
-        projected = projected.astype(jnp.bfloat16).reshape(groups, seqs * rows, 1, head_cols)
-        mixed.append(jnp.stack([attend(projected[g]) for g in range(groups)]))
-    out = jnp.concatenate(mixed, axis=-1).reshape(groups * seqs, rows, heads * depth)
-    out = lax.all_to_all(out, ("groups", "seq"), split_axis=0, concat_axis=0, tiled=True)
-    out = out.reshape(groups, seqs, rows, heads * depth).transpose(2, 1, 0, 3)
-    return out.reshape(1, rows, seqs * groups * heads * depth)
+        piece = lax.dynamic_slice_in_dim(qkv_weight, group * heads + j, 1, 1)[:, 0]
+        if after is not None:
+            piece, after = lax.optimization_barrier((piece, after))
+        near = lax.ppermute(piece, "dp", pairs)
+        over = lax.ppermute(piece, "dp", middle)
+        far = lax.ppermute(near, "dp", middle)
+        over_end = lax.ppermute(over, "dp", ends)
+        far_end = lax.ppermute(far, "dp", ends)
+        after = over
+        pieces.append((piece, near, jnp.where(inner, over, over_end), jnp.where(inner, far, far_end)))
+
+    received = []
+    for j in range(heads):
+        total = None
+        for i, weight in enumerate(pieces[j]):
+            term = jnp.dot(
+                features[:, i * slab : (i + 1) * slab], weight, preferred_element_type=jnp.float32
+            )
+            total = term if total is None else total + term
+        mixed = attend_images(total.astype(jnp.bfloat16), groups)
+        mixed = mixed.reshape(groups, seqs, rows, depth)
+        got = []
+        for a in range(groups):
+            for b in range(seqs):
+                to_group, to_seq = (group + a) % groups, (seq + b) % seqs
+                sent = lax.dynamic_slice(
+                    mixed, (to_group, to_seq, 0, 0), (1, 1, rows, depth)
+                )[0, 0]
+                if a or b:
+                    sent = lax.ppermute(
+                        sent,
+                        ("groups", "seq"),
+                        [
+                            (g * seqs + s, (g + a) % groups * seqs + (s + b) % seqs)
+                            for g in range(groups)
+                            for s in range(seqs)
+                        ],
+                    )
+                got.append(sent)
+        received.append(jnp.stack(got))
+    received = jnp.stack(received)
+    blocks = []
+    for s in range(seqs):
+        for g in range(groups):
+            index = (group - g) % groups * seqs + (seq - s) % seqs
+            chosen = lax.dynamic_index_in_dim(received, index, 1, keepdims=False)
+            blocks.extend(chosen[j] for j in range(heads))
+    return jnp.concatenate(blocks, axis=1)[None]
 
 
 def per_device(tokens, ln_gain, qkv_weight):
     groups, cores = lax.axis_size("groups"), lax.axis_size("head")
-    if tokens.shape[0] == 1 and qkv_weight.shape[1] % groups == 0 and tokens.shape[1] % cores == 0:
+    fits = tokens.shape[0] == 1 and qkv_weight.shape[1] % groups == 0
+    if fits and tokens.shape[1] % cores == 0 and lax.axis_size("dp") == 4:
         return shared(tokens, ln_gain, qkv_weight)
     return plain(tokens, ln_gain, qkv_weight)
 

time: 436 us -> 289 us (0.66); the launches traced: 435 us -> 284 us
  waiting for transfers between devices: 334 us -> 110 us
  starting transfers between devices: 0.12 us -> 90.4 us
  blocking collectives: 19.1 us -> 0 us
  Pallas kernels: 0 us -> 11.5 us
  matrix products: 52.2 us -> 41.9 us
    all_gather x3 -> x0, waiting for transfers between devices: 234 us -> none  [shared(): weight = lax.all_gather(piece, 'dp', axis=0, tiled=True)]
    ppermute x0 -> x24, waiting for transfers between devices: none -> 105 us  [the longest x3 53.4 us: shared(): far_end = lax.ppermute(far, 'dp', ends)]
    all_gather x1, waiting for transfers between devices: 99.1 us -> 5.03 us  [shared(): lax.all_gather(normed, ('groups', 'seq', 'head'), axis=0, tiled=True)]
    ppermute x0 -> x24, starting transfers between devices: none -> 90.4 us  [the longest x3 60.2 us: shared(): near = lax.ppermute(piece, 'dp', pairs)]
    all_to_all x1 -> x0, blocking collectives: 19.1 us -> none  [shared(): lax.all_to_all(out, ('groups', 'seq'), split_axis=0, concat_axis=0, tiled...]
    pallas_call x0 -> x3, Pallas kernels: none -> 11.5 us  [attend_images(): pl.pallas_call(attend_kernel, grid=(images,), out_shape=jax.ShapeDtypeStr...]
    dot_general x15 -> x12, matrix products: 52.2 us -> 41.9 us  [shared(): jnp.dot(features[:, i * slab:(i + 1) * slab], weight, preferred_element_t...]
  transfers between devices with their start and end apart: 4 -> 25, of which waited for: 4 -> 12; matrix products, arithmetic and copies ran while one was open for 9% -> 16% of each run, Pallas kernels for 0% -> 4%
where the time goes in v2:
time: 289 us; the launch traced here: 284 us
  waiting for transfers between devices  110 us (38%)
  starting transfers between devices  90.4 us (31%)
  matrix products  41.9 us (14%)
  between operations  14.1 us (5%)
  Pallas kernels  11.5 us (4%)
  other arithmetic  9.07 us (3%)
  local copies, waits for them, and re-layouts  6.12 us (2%)
    ppermute x3, starting transfers between devices, shared(): near = lax.ppermute(piece, 'dp', pairs)  60.2 us
    ppermute x3, waiting for transfers between devices, shared(): far_end = lax.ppermute(far, 'dp', ends)  53.4 us
    dot_general x12, matrix products, shared(): jnp.dot(features[:, i * slab:(i + 1) * slab], weight, preferred_element_t...  41.9 us
    ppermute x3, waiting for transfers between devices, shared(): over_end = lax.ppermute(over, 'dp', ends)  27 us
    ppermute x3, waiting for transfers between devices, shared(): near = lax.ppermute(piece, 'dp', pairs)  21 us
    ppermute x9, starting transfers between devices, shared(): lax.ppermute(sent, ('groups', 'seq'), [(g * seqs + s, (g + a) % groups *...  13.6 us
    pallas_call x3, Pallas kernels, attend_images(): pl.pallas_call(attend_kernel, grid=(images,), out_shape=jax.ShapeDtypeStr...  11.5 us
  transfers between devices with their start and end apart: 25, of which 12 were waited for; matrix products, arithmetic and copies ran while one was open for 16% of the time, Pallas kernels for 4%

profile of v2, /device:TPU:0, one launch (start us, length us, event | category | flops | bytes accessed | tf_op | source)
XLA Modules:
  0.0 283.6 jit_solution(1503603942425137594)
XLA Ops:
  6.5 2.1 convert_reduce_fusion
  8.6 2.4 fusion.3
  11.1 2.6 fusion.5
  13.7 0.2 constant_dynamic-slice_fusion.3
  13.9 1.7 pad_maximum_fusion
  15.6 2.3 dynamic-slice_bitcast_fusion.2
  17.9 0.7 collective-permute-start.1
  18.7 5.8 %collective-permute-start = (bf16[1536,384]{1,0:T(8,128)(2,1)S(1)}, bf16[1536,384]{1,0:T(8,128)(2,1)}, u32[]{:S(2)}, u32[]{:S(2)}) collective-permute-start(bf16[1536,384]{1,0:T(8,128)(2,1)S(1)} %get-tuple-element.9), channel_id=1, source_target_pairs={{0,4},{4,0},{8,12},{12,8},{1,5},{5,1},{9,13},{13,9},{2,6},{6,2},{1... | collective-permute-start | bytes 3538952 | tf_op jit(solution)/shard_map/ppermute | solution.py:118
  24.5 1.0 copy-done.5
  25.6 0.7 collective-permute-start.9
  26.3 28.9 %collective-permute-start.8 = (bf16[1536,384]{1,0:T(8,128)(2,1)S(1)}, bf16[1536,384]{1,0:T(8,128)(2,1)}, u32[]{:S(2)}, u32[]{:S(2)}) collective-permute-start(bf16[1536,384]{1,0:T(8,128)(2,1)S(1)} %get-tuple-element.7), channel_id=1, source_target_pairs={{0,4},{4,0},{8,12},{12,8},{1,5},{5,1},{9,13},{13,9},{2,6},{6,2},{1... | collective-permute-start | bytes 3538952 | tf_op jit(solution)/shard_map/ppermute | solution.py:118
  55.1 1.7 collective-permute-start.3
  56.8 1.0 copy-done.3
  57.8 25.6 %collective-permute-start.16 = (bf16[1536,384]{1,0:T(8,128)(2,1)S(1)}, bf16[1536,384]{1,0:T(8,128)(2,1)}, u32[]{:S(2)}, u32[]{:S(2)}) collective-permute-start(bf16[1536,384]{1,0:T(8,128)(2,1)S(1)} %get-tuple-element.8), channel_id=1, source_target_pairs={{0,4},{4,0},{8,12},{12,8},{1,5},{5,1},{9,13},{13,9},{2,6},{6,2},{1... | collective-permute-start | bytes 3538952 | tf_op jit(solution)/shard_map/ppermute | solution.py:118
  83.4 1.3 collective-permute-start.2
  84.7 1.7 collective-permute-start.17
  86.4 1.3 collective-permute-start.4
  87.7 1.7 collective-permute-start.11
  89.4 21.0 %collective-permute-done.16 = bf16[1536,384]{1,0:T(8,128)(2,1)} collective-permute-done((bf16[1536,384]{1,0:T(8,128)(2,1)S(1)}, bf16[1536,384]{1,0:T(8,128)(2,1)}, u32[]{:S(2)}, u32[]{:S(2)}) %collective-permute-start.16) | collective-permute-done | bytes 1179680 | tf_op jit(solution)/shard_map/ppermute | solution.py:118
  110.4 1.7 collective-permute-start.19
  112.1 5.0 %all-gather.2.cloned.1.call-done = bf16[1536,6144]{1,0:T(8,128)(2,1)} async-done(((bf16[192,6144]{1,0:T(8,128)(2,1)}), bf16[1536,6144]{1,0:T(8,128)(2,1)}) %all-gather.2.cloned.1.call-update) | async-done | bytes 18874384 | tf_op jit(solution)/shard_map/all_gather | solution.py:108
  117.2 4.6 %fusion.28 = f32[1536,384]{1,0:T(8,128)S(1)} fusion(bf16[1536,384]{1,0:T(8,128)(2,1)S(1)} %get-tuple-element.9, bf16[1536,6144]{1,0:T(8,128)(2,1)} %all-gather.2.cloned.1.call-done), kind=kOutput, calls=%fused_computation.30 | convolution fusion | flops 1811939328 | bytes 8257536 | tf_op jit(solution)/shard_map/dot_general | solution.py:130
  121.8 5.9 %fusion.36 = f32[1536,384]{1,0:T(8,128)S(1)} fusion(f32[1536,384]{1,0:T(8,128)S(1)} %fusion.28, bf16[1536,384]{1,0:T(8,128)(2,1)} %collective-permute-done, bf16[1536,6144]{1,0:T(8,128)(2,1)} %all-gather.2.cloned.1.call-done), kind=kOutput, calls=%fused_computation.34 | convolution fusion | flops 1812529152 | bytes 10616832 | tf_op jit(solution)/shard_map/dot_general | solution.py:130
  127.7 8.0 %collective-permute-done.2 = bf16[1536,384]{1,0:T(8,128)(2,1)} collective-permute-done((bf16[1536,384]{1,0:T(8,128)(2,1)}, bf16[1536,384]{1,0:T(8,128)(2,1)}, u32[]{:S(2)}, u32[]{:S(2)}) %collective-permute-start.2) | collective-permute-done | bytes 1179680 | tf_op jit(solution)/shard_map/ppermute | solution.py:121
  135.7 1.3 collective-permute-start.10
  137.0 1.3 collective-permute-start.12
  138.3 1.3 collective-permute-start.18
  139.6 1.8 collective-permute-start.20
  141.4 3.9 %fusion.39 = f32[1536,384]{1,0:T(8,128)S(1)} fusion(f32[1536,384]{1,0:T(8,128)S(1)} %fusion.36, bf16[1536,6144]{1,0:T(8,128)(2,1)S(1)} %copy-done.2, bf16[1536,384]{1,0:T(8,128)(2,1)S(1)} %copy-done.6, bf16[1536,384]{1,0:T(8,128)(2,1)} %collective-permute-done.2, pred[]{:T(512)S(6)} %or.3), kind=kOutput, calls=%fused_computation.35 | convolution fusion | flops 1813118976 | bytes 11796481 | tf_op jit(solution)/shard_map/dot_general | solution.py:130
  145.3 15.6 %collective-permute-done.4 = bf16[1536,384]{1,0:T(8,128)(2,1)} collective-permute-done((bf16[1536,384]{1,0:T(8,128)(2,1)}, bf16[1536,384]{1,0:T(8,128)(2,1)}, u32[]{:S(2)}, u32[]{:S(2)}) %collective-permute-start.4) | collective-permute-done | bytes 1179680 | tf_op jit(solution)/shard_map/ppermute | solution.py:122
  160.9 3.9 %fusion.63.projected_ref = bf16[1536,384]{1,0:T(8,128)(2,1)S(1)} fusion(f32[1536,384]{1,0:T(8,128)S(1)} %fusion.39, bf16[1536,6144]{1,0:T(8,128)(2,1)S(1)} %copy-done.2, bf16[1536,384]{1,0:T(8,128)(2,1)} %collective-permute-done.3, bf16[1536,384]{1,0:T(8,128)(2,1)} %collective-permute-done.4, pred[]{:T(512)S(6)} %or.3), kind=kOutput, calls=%fused_computation.43 | convolution fusion | flops 1813708800 | bytes 10616833 | tf_op jit(solution)/shard_map/dot_general | solution.py:130
  164.9 3.8 %shard_map.37 = bf16[1536,128]{1,0:T(8,128)(2,1)S(1)} custom-call(bf16[1536,384]{1,0:T(8,128)(2,1)S(1)} %fusion.63.projected_ref), custom_call_target="tpu_custom_call" | custom-call | flops 603979776 | bytes 1572864 | tf_op jit(solution)/shard_map/pallas_call | solution.py:77
  168.7 1.5 collective-permute-start.5
  170.3 3.9 %fusion.20 = f32[1536,384]{1,0:T(8,128)S(1)} fusion(bf16[1536,384]{1,0:T(8,128)(2,1)} %collective-permute-done.8, bf16[1536,6144]{1,0:T(8,128)(2,1)S(1)} %copy-done.2), kind=kOutput, calls=%fused_computation.22 | convolution fusion | flops 1811939328 | bytes 8257536 | tf_op jit(solution)/shard_map/dot_general | solution.py:130
  174.2 2.7 fusion.30
  176.8 9.3 %collective-permute-done.10 = bf16[1536,384]{1,0:T(8,128)(2,1)S(1)} collective-permute-done((bf16[1536,384]{1,0:T(8,128)(2,1)S(1)}, bf16[1536,384]{1,0:T(8,128)(2,1)S(1)}, u32[]{:S(2)}, u32[]{:S(2)}) %collective-permute-start.10) | collective-permute-done | bytes 1179680 | tf_op jit(solution)/shard_map/ppermute | solution.py:121
  186.1 1.5 collective-permute-start.6
  187.6 2.6 fusion.42
  190.3 21.1 %collective-permute-done.12 = bf16[1536,384]{1,0:T(8,128)(2,1)S(1)} collective-permute-done((bf16[1536,384]{1,0:T(8,128)(2,1)}, bf16[1536,384]{1,0:T(8,128)(2,1)S(1)}, u32[]{:S(2)}, u32[]{:S(2)}) %collective-permute-start.12) | collective-permute-done | bytes 1179680 | tf_op jit(solution)/shard_map/ppermute | solution.py:122
  211.4 2.4 collective-permute-start.7
  213.8 2.6 fusion.60.projected_ref
  216.5 3.9 %shard_map.38 = bf16[1536,128]{1,0:T(8,128)(2,1)S(1)} custom-call(bf16[1536,384]{1,0:T(8,128)(2,1)S(1)} %fusion.60.projected_ref), custom_call_target="tpu_custom_call" | custom-call | flops 603979776 | bytes 1572864 | tf_op jit(solution)/shard_map/pallas_call | solution.py:77
  220.4 3.9 %fusion.18 = f32[1536,384]{1,0:T(8,128)S(1)} fusion(bf16[1536,384]{1,0:T(8,128)(2,1)} %collective-permute-done.16, bf16[1536,6144]{1,0:T(8,128)(2,1)S(1)} %copy-done.2), kind=kOutput, calls=%fused_computation.20 | convolution fusion | flops 1811939328 | bytes 8257536 | tf_op jit(solution)/shard_map/dot_general | solution.py:130
  224.3 2.6 fusion.33
  226.9 9.8 %collective-permute-done.18 = bf16[1536,384]{1,0:T(8,128)(2,1)S(1)} collective-permute-done((bf16[1536,384]{1,0:T(8,128)(2,1)}, bf16[1536,384]{1,0:T(8,128)(2,1)S(1)}, u32[]{:S(2)}, u32[]{:S(2)}) %collective-permute-start.18) | collective-permute-done | bytes 1179680 | tf_op jit(solution)/shard_map/ppermute | solution.py:121
  236.7 1.5 collective-permute-start.13
  238.2 2.6 fusion.45
  240.8 16.7 %collective-permute-done.20 = bf16[1536,384]{1,0:T(8,128)(2,1)S(1)} collective-permute-done((bf16[1536,384]{1,0:T(8,128)(2,1)}, bf16[1536,384]{1,0:T(8,128)(2,1)S(1)}, u32[]{:S(2)}, u32[]{:S(2)}) %collective-permute-start.20) | collective-permute-done | bytes 1179680 | tf_op jit(solution)/shard_map/ppermute | solution.py:122
  257.5 1.5 collective-permute-start.14
  259.0 2.6 fusion.57.projected_ref
  261.7 3.9 %shard_map.39 = bf16[1536,128]{1,0:T(8,128)(2,1)S(1)} custom-call(bf16[1536,384]{1,0:T(8,128)(2,1)S(1)} %fusion.57.projected_ref), custom_call_target="tpu_custom_call" | custom-call | flops 603979776 | bytes 1572864 | tf_op jit(solution)/shard_map/pallas_call | solution.py:77
  265.6 1.5 collective-permute-start.15
  267.1 0.5 collective-permute-start.21
  267.7 1.5 collective-permute-start.22
  269.2 0.1 maximum_bitcast_fusion
  269.2 1.5 collective-permute-start.23
  270.7 0.5 collective-permute-done.15
  271.2 0.1 maximum_bitcast_fusion.1
  271.2 0.5 collective-permute-done.21
  271.7 0.5 collective-permute-done.22
  272.3 2.5 collective-permute-done.23
  274.8 0.1 maximum_bitcast_fusion.2
  274.9 0.1 pad_maximum_fusion.1
  275.5 1.0 copy-done.1
  (43 shorter events, 0.6 us)
Async XLA Ops:
  6.5 110.6 %all-gather.2.cloned.1.call-start = ((), (), s32[]{:S(2)}) async-start(), calls=%async_computation | async-start | bytes 21233664 | tf_op jit(solution)/shard_map/all_gather | solution.py:108
  8.6 2.5 copy-start
  17.9 6.6 %collective-permute-start.1 = (bf16[1536,384]{1,0:T(8,128)(2,1)S(1)}, bf16[1536,384]{1,0:T(8,128)(2,1)S(1)}, u32[]{:S(2)}, u32[]{:S(2)}) collective-permute-start(bf16[1536,384]{1,0:T(8,128)(2,1)S(1)} %get-tuple-element.9), channel_id=1, source_target_pairs={{4,8},{8,4},{5,9},{9,5},{6,10},{10,6},{7,11},{11,7},{20,24},{24,20... | collective-permute-start | bytes 3538952 | tf_op jit(solution)/shard_map/ppermute | solution.py:119
  18.7 36.5 %collective-permute-start = (bf16[1536,384]{1,0:T(8,128)(2,1)S(1)}, bf16[1536,384]{1,0:T(8,128)(2,1)}, u32[]{:S(2)}, u32[]{:S(2)}) collective-permute-start(bf16[1536,384]{1,0:T(8,128)(2,1)S(1)} %get-tuple-element.9), channel_id=1, source_target_pairs={{0,4},{4,0},{8,12},{12,8},{1,5},{5,1},{9,13},{13,9},{2,6},{6,2},{1... | collective-permute-start | bytes 3538952 | tf_op jit(solution)/shard_map/ppermute | solution.py:118
  24.5 1.0 copy-start.5
  25.6 31.3 %collective-permute-start.9 = (bf16[1536,384]{1,0:T(8,128)(2,1)S(1)}, bf16[1536,384]{1,0:T(8,128)(2,1)S(1)}, u32[]{:S(2)}, u32[]{:S(2)}) collective-permute-start(bf16[1536,384]{1,0:T(8,128)(2,1)S(1)} %get-tuple-element.7), channel_id=1, source_target_pairs={{4,8},{8,4},{5,9},{9,5},{6,10},{10,6},{7,11},{11,7},{20,24},{24,20... | collective-permute-start | bytes 3538952 | tf_op jit(solution)/shard_map/ppermute | solution.py:119
  26.3 61.4 %collective-permute-start.8 = (bf16[1536,384]{1,0:T(8,128)(2,1)S(1)}, bf16[1536,384]{1,0:T(8,128)(2,1)}, u32[]{:S(2)}, u32[]{:S(2)}) collective-permute-start(bf16[1536,384]{1,0:T(8,128)(2,1)S(1)} %get-tuple-element.7), channel_id=1, source_target_pairs={{0,4},{4,0},{8,12},{12,8},{1,5},{5,1},{9,13},{13,9},{2,6},{6,2},{1... | collective-permute-start | bytes 3538952 | tf_op jit(solution)/shard_map/ppermute | solution.py:118
  55.1 31.3 %collective-permute-start.3 = (bf16[1536,384]{1,0:T(8,128)(2,1)}, bf16[1536,384]{1,0:T(8,128)(2,1)}, u32[]{:S(2)}, u32[]{:S(2)}) collective-permute-start(bf16[1536,384]{1,0:T(8,128)(2,1)} %collective-permute-done), channel_id=1, source_target_pairs={{4,8},{8,4},{5,9},{9,5},{6,10},{10,6},{7,11},{11,7},{20,24},{24,20... | collective-permute-start | bytes 3538952 | tf_op jit(solution)/shard_map/ppermute | solution.py:120
  56.8 1.0 copy-start.3
  57.8 52.5 %collective-permute-start.16 = (bf16[1536,384]{1,0:T(8,128)(2,1)S(1)}, bf16[1536,384]{1,0:T(8,128)(2,1)}, u32[]{:S(2)}, u32[]{:S(2)}) collective-permute-start(bf16[1536,384]{1,0:T(8,128)(2,1)S(1)} %get-tuple-element.8), channel_id=1, source_target_pairs={{0,4},{4,0},{8,12},{12,8},{1,5},{5,1},{9,13},{13,9},{2,6},{6,2},{1... | collective-permute-start | bytes 3538952 | tf_op jit(solution)/shard_map/ppermute | solution.py:118
  83.4 52.3 %collective-permute-start.2 = (bf16[1536,384]{1,0:T(8,128)(2,1)}, bf16[1536,384]{1,0:T(8,128)(2,1)}, u32[]{:S(2)}, u32[]{:S(2)}) collective-permute-start(bf16[1536,384]{1,0:T(8,128)(2,1)} %copy-done.5), channel_id=1, source_target_pairs={{4,0},{8,12},{5,1},{9,13},{6,2},{10,14},{7,3},{11,15},{20,16},{24,... | collective-permute-start | bytes 3538952 | tf_op jit(solution)/shard_map/ppermute | solution.py:121
  84.7 53.6 %collective-permute-start.17 = (bf16[1536,384]{1,0:T(8,128)(2,1)S(1)}, bf16[1536,384]{1,0:T(8,128)(2,1)}, u32[]{:S(2)}, u32[]{:S(2)}) collective-permute-start(bf16[1536,384]{1,0:T(8,128)(2,1)S(1)} %get-tuple-element.8), channel_id=1, source_target_pairs={{4,8},{8,4},{5,9},{9,5},{6,10},{10,6},{7,11},{11,7},{20,24},{24,20... | collective-permute-start | bytes 3538952 | tf_op jit(solution)/shard_map/ppermute | solution.py:119
  86.4 74.5 %collective-permute-start.4 = (bf16[1536,384]{1,0:T(8,128)(2,1)}, bf16[1536,384]{1,0:T(8,128)(2,1)}, u32[]{:S(2)}, u32[]{:S(2)}) collective-permute-start(bf16[1536,384]{1,0:T(8,128)(2,1)} %collective-permute-done.3), channel_id=1, source_target_pairs={{4,0},{8,12},{5,1},{9,13},{6,2},{10,14},{7,3},{11,15},{20,16},{24,... | collective-permute-start | bytes 3538952 | tf_op jit(solution)/shard_map/ppermute | solution.py:122
  87.7 49.2 %collective-permute-start.11 = (bf16[1536,384]{1,0:T(8,128)(2,1)}, bf16[1536,384]{1,0:T(8,128)(2,1)}, u32[]{:S(2)}, u32[]{:S(2)}) collective-permute-start(bf16[1536,384]{1,0:T(8,128)(2,1)} %collective-permute-done.8), channel_id=1, source_target_pairs={{4,8},{8,4},{5,9},{9,5},{6,10},{10,6},{7,11},{11,7},{20,24},{24,20... | collective-permute-start | bytes 3538952 | tf_op jit(solution)/shard_map/ppermute | solution.py:120
  110.4 29.2 %collective-permute-start.19 = (bf16[1536,384]{1,0:T(8,128)(2,1)}, bf16[1536,384]{1,0:T(8,128)(2,1)}, u32[]{:S(2)}, u32[]{:S(2)}) collective-permute-start(bf16[1536,384]{1,0:T(8,128)(2,1)} %collective-permute-done.16), channel_id=1, source_target_pairs={{4,8},{8,4},{5,9},{9,5},{6,10},{10,6},{7,11},{11,7},{20,24},{24,20... | collective-permute-start | bytes 3538952 | tf_op jit(solution)/shard_map/ppermute | solution.py:120
  117.2 24.2 %copy-start.2 = (bf16[1536,6144]{1,0:T(8,128)(2,1)S(1)}, bf16[1536,6144]{1,0:T(8,128)(2,1)}, u32[]{:S(2)}) copy-start(bf16[1536,6144]{1,0:T(8,128)(2,1)} %all-gather.2.cloned.1.call-done) | copy-start | bytes 56623108
  121.8 13.9 %copy-start.4 = (bf16[1536,384]{1,0:T(8,128)(2,1)S(1)}, bf16[1536,384]{1,0:T(8,128)(2,1)}, u32[]{:S(2)}) copy-start(bf16[1536,384]{1,0:T(8,128)(2,1)} %copy-done.3) | copy-start | bytes 3538948
  121.8 19.6 %copy-start.6 = (bf16[1536,384]{1,0:T(8,128)(2,1)S(1)}, bf16[1536,384]{1,0:T(8,128)(2,1)}, u32[]{:S(2)}) copy-start(bf16[1536,384]{1,0:T(8,128)(2,1)} %copy-done.5) | copy-start | bytes 3538948
  135.7 50.5 %collective-permute-start.10 = (bf16[1536,384]{1,0:T(8,128)(2,1)S(1)}, bf16[1536,384]{1,0:T(8,128)(2,1)S(1)}, u32[]{:S(2)}, u32[]{:S(2)}) collective-permute-start(bf16[1536,384]{1,0:T(8,128)(2,1)S(1)} %copy-done.4), channel_id=1, source_target_pairs={{4,0},{8,12},{5,1},{9,13},{6,2},{10,14},{7,3},{11,15},{20,16},{24,... | collective-permute-start | bytes 3538952 | tf_op jit(solution)/shard_map/ppermute | solution.py:121
  137.0 74.4 %collective-permute-start.12 = (bf16[1536,384]{1,0:T(8,128)(2,1)}, bf16[1536,384]{1,0:T(8,128)(2,1)S(1)}, u32[]{:S(2)}, u32[]{:S(2)}) collective-permute-start(bf16[1536,384]{1,0:T(8,128)(2,1)} %collective-permute-done.11), channel_id=1, source_target_pairs={{4,0},{8,12},{5,1},{9,13},{6,2},{10,14},{7,3},{11,15},{20,16},{24,... | collective-permute-start | bytes 3538952 | tf_op jit(solution)/shard_map/ppermute | solution.py:122
  138.3 98.4 %collective-permute-start.18 = (bf16[1536,384]{1,0:T(8,128)(2,1)}, bf16[1536,384]{1,0:T(8,128)(2,1)S(1)}, u32[]{:S(2)}, u32[]{:S(2)}) collective-permute-start(bf16[1536,384]{1,0:T(8,128)(2,1)} %collective-permute-done.17), channel_id=1, source_target_pairs={{4,0},{8,12},{5,1},{9,13},{6,2},{10,14},{7,3},{11,15},{20,16},{24,... | collective-permute-start | bytes 3538952 | tf_op jit(solution)/shard_map/ppermute | solution.py:121
  139.6 117.9 %collective-permute-start.20 = (bf16[1536,384]{1,0:T(8,128)(2,1)}, bf16[1536,384]{1,0:T(8,128)(2,1)S(1)}, u32[]{:S(2)}, u32[]{:S(2)}) collective-permute-start(bf16[1536,384]{1,0:T(8,128)(2,1)} %collective-permute-done.19), channel_id=1, source_target_pairs={{4,0},{8,12},{5,1},{9,13},{6,2},{10,14},{7,3},{11,15},{20,16},{24,... | collective-permute-start | bytes 3538952 | tf_op jit(solution)/shard_map/ppermute | solution.py:122
  168.7 96.9 %collective-permute-start.5 = (bf16[384,128]{1,0:T(8,128)(2,1)S(1)}, bf16[384,128]{1,0:T(8,128)(2,1)S(1)}, u32[]{:S(2)}, u32[]{:S(2)}) collective-permute-start(bf16[384,128]{1,0:T(8,128)(2,1)S(1)} %get-tuple-element.19), channel_id=1, source_target_pairs={{0,2},{2,0},{16,18},{18,16},{1,3},{3,1},{17,19},{19,17},{4,6},{6,4... | collective-permute-start | bytes 294920 | tf_op jit(solution)/shard_map/ppermute | solution.py:144
  186.1 81.0 %collective-permute-start.6 = (bf16[384,128]{1,0:T(8,128)(2,1)S(1)}, bf16[384,128]{1,0:T(8,128)(2,1)S(1)}, u32[]{:S(2)}, u32[]{:S(2)}) collective-permute-start(bf16[384,128]{1,0:T(8,128)(2,1)S(1)} %get-tuple-element.18), channel_id=1, source_target_pairs={{0,16},{2,18},{16,0},{18,2},{1,17},{3,19},{17,1},{19,3},{4,20},{6,... | collective-permute-start | bytes 294920 | tf_op jit(solution)/shard_map/ppermute | solution.py:144
  211.4 56.3 %collective-permute-start.7 = (bf16[384,128]{1,0:T(8,128)(2,1)S(1)}, bf16[384,128]{1,0:T(8,128)(2,1)S(1)}, u32[]{:S(2)}, u32[]{:S(2)}) collective-permute-start(bf16[384,128]{1,0:T(8,128)(2,1)S(1)} %get-tuple-element.17), channel_id=1, source_target_pairs={{0,18},{2,16},{16,2},{18,0},{1,19},{3,17},{17,3},{19,1},{4,22},{6,... | collective-permute-start | bytes 294920 | tf_op jit(solution)/shard_map/ppermute | solution.py:144
  236.7 32.5 %collective-permute-start.13 = (bf16[384,128]{1,0:T(8,128)(2,1)S(1)}, bf16[384,128]{1,0:T(8,128)(2,1)S(1)}, u32[]{:S(2)}, u32[]{:S(2)}) collective-permute-start(bf16[384,128]{1,0:T(8,128)(2,1)S(1)} %get-tuple-element.23), channel_id=1, source_target_pairs={{0,2},{2,0},{16,18},{18,16},{1,3},{3,1},{17,19},{19,17},{4,6},{6,4... | collective-permute-start | bytes 294920 | tf_op jit(solution)/shard_map/ppermute | solution.py:144
  257.5 13.2 %collective-permute-start.14 = (bf16[384,128]{1,0:T(8,128)(2,1)S(1)}, bf16[384,128]{1,0:T(8,128)(2,1)S(1)}, u32[]{:S(2)}, u32[]{:S(2)}) collective-permute-start(bf16[384,128]{1,0:T(8,128)(2,1)S(1)} %get-tuple-element.22), channel_id=1, source_target_pairs={{0,16},{2,18},{16,0},{18,2},{1,17},{3,19},{17,1},{19,3},{4,20},{6,... | collective-permute-start | bytes 294920 | tf_op jit(solution)/shard_map/ppermute | solution.py:144
  265.6 5.6 %collective-permute-start.15 = (bf16[384,128]{1,0:T(8,128)(2,1)S(1)}, bf16[384,128]{1,0:T(8,128)(2,1)S(1)}, u32[]{:S(2)}, u32[]{:S(2)}) collective-permute-start(bf16[384,128]{1,0:T(8,128)(2,1)S(1)} %get-tuple-element.21), channel_id=1, source_target_pairs={{0,18},{2,16},{16,2},{18,0},{1,19},{3,17},{17,3},{19,1},{4,22},{6,... | collective-permute-start | bytes 294920 | tf_op jit(solution)/shard_map/ppermute | solution.py:144
  267.1 4.6 %collective-permute-start.21 = (bf16[384,128]{1,0:T(8,128)(2,1)S(1)}, bf16[384,128]{1,0:T(8,128)(2,1)S(1)}, u32[]{:S(2)}, u32[]{:S(2)}) collective-permute-start(bf16[384,128]{1,0:T(8,128)(2,1)S(1)} %get-tuple-element.27), channel_id=1, source_target_pairs={{0,2},{2,0},{16,18},{18,16},{1,3},{3,1},{17,19},{19,17},{4,6},{6,4... | collective-permute-start | bytes 294920 | tf_op jit(solution)/shard_map/ppermute | solution.py:144
  267.7 4.6 %collective-permute-start.22 = (bf16[384,128]{1,0:T(8,128)(2,1)S(1)}, bf16[384,128]{1,0:T(8,128)(2,1)S(1)}, u32[]{:S(2)}, u32[]{:S(2)}) collective-permute-start(bf16[384,128]{1,0:T(8,128)(2,1)S(1)} %get-tuple-element.26), channel_id=1, source_target_pairs={{0,16},{2,18},{16,0},{18,2},{1,17},{3,19},{17,1},{19,3},{4,20},{6,... | collective-permute-start | bytes 294920 | tf_op jit(solution)/shard_map/ppermute | solution.py:144
  269.2 5.6 %collective-permute-start.23 = (bf16[384,128]{1,0:T(8,128)(2,1)S(1)}, bf16[384,128]{1,0:T(8,128)(2,1)S(1)}, u32[]{:S(2)}, u32[]{:S(2)}) collective-permute-start(bf16[384,128]{1,0:T(8,128)(2,1)S(1)} %get-tuple-element.25), channel_id=1, source_target_pairs={{0,18},{2,16},{16,2},{18,0},{1,19},{3,17},{17,3},{19,1},{4,22},{6,... | collective-permute-start | bytes 294920 | tf_op jit(solution)/shard_map/ppermute | solution.py:144
  275.5 1.0 copy-start.1
Sparse Core Ops, SparseCore 0:
  15.7 101.4 all-gather.1

commit v3 on v0

--- a/solution.py
+++ b/solution.py
@@ -1,8 +1,11 @@
+import functools
 import math
 
 import jax
 import jax.numpy as jnp
 from jax import lax
+from jax.experimental import pallas as pl
+from jax.experimental.pallas import tpu as pltpu
 from jax.sharding import PartitionSpec as P
 
 
@@ -28,7 +31,7 @@
     return mixed.astype(jnp.bfloat16).reshape(projected.shape[0], -1)
 
 
-def per_device(tokens, ln_gain, qkv_weight):
+def plain(tokens, ln_gain, qkv_weight):
     images = tokens.shape[0]
     width = tokens.shape[2]
     heads_here = qkv_weight.shape[1]
@@ -52,6 +55,353 @@
     return lax.all_to_all(mixed, "seq", split_axis=1, concat_axis=2, tiled=True)
 
 
+CHAINS = 1
+
+
+def normalize_kernel(place_ref, tokens_ref, gain_ref, *normed_refs):
+    widened = tokens_ref[0].astype(jnp.float32)
+    mean = jnp.mean(widened, axis=-1, keepdims=True)
+    centered = widened - mean
+    scale = lax.rsqrt(jnp.mean(centered * centered, axis=-1, keepdims=True) + 1e-06)
+    slab = widened.shape[1] // 4
+    span = normed_refs[0].shape[1]
+    for i in range(4):
+        columns = pl.ds(pl.multiple_of(place_ref[i + 1] * slab, 128), slab)
+        part = (tokens_ref[0, :, columns].astype(jnp.float32) - mean) * scale * gain_ref[:, columns]
+        begin = i * slab % span
+        normed_refs[i * slab // span][:, begin : begin + slab] = part.astype(jnp.bfloat16)
+
+
+def normalize_part(tokens, ln_gain, part, core, order):
+    width = tokens.shape[2]
+    step, count = 32, 2 * CHAINS
+    steps = part // step
+    place = jnp.stack([jnp.asarray(v, jnp.int32) for v in (core, *order)])
+    return pl.pallas_call(
+        normalize_kernel,
+        out_shape=[jax.ShapeDtypeStruct((part, width // count), jnp.bfloat16)] * count,
+        grid_spec=pltpu.PrefetchScalarGridSpec(
+            num_scalar_prefetch=1,
+            grid=(steps,),
+            in_specs=[
+                pl.BlockSpec((1, step, width), lambda i, place: (0, place[0] * steps + i, 0)),
+                pl.BlockSpec((1, width), lambda i, place: (0, 0)),
+            ],
+            out_specs=[pl.BlockSpec((step, width // count), lambda i, place: (i, 0))] * count,
+        ),
+        compiler_params=pltpu.CompilerParams(vmem_limit_bytes=56 << 20),
+        cost_estimate=pl.CostEstimate(
+            flops=8 * part * width, bytes_accessed=4 * part * width, transcendentals=part
+        ),
+    )(place, tokens, ln_gain[None])
+
+
+def attend_rows(projected_ref, mixed_ref, base):
+    tokens, columns = projected_ref.shape
+    width = columns // 3
+    step = 256
+    key_rows = projected_ref[:, width : 2 * width]
+    value_rows = projected_ref[:, 2 * width :]
+    for begin in range(0, tokens, step):
+        queries = projected_ref[begin : begin + step, :width]
+        scores = lax.dot_general(
+            queries, key_rows, (((1,), (1,)), ((), ())), preferred_element_type=jnp.float32
+        ) * (1.0 / math.sqrt(width))
+        expo = jnp.exp(scores - jnp.max(scores, axis=-1, keepdims=True))
+        probs = (expo / jnp.sum(expo, axis=-1, keepdims=True)).astype(jnp.bfloat16)
+        mixed = jnp.dot(probs, value_rows, preferred_element_type=jnp.float32)
+        mixed_ref[base + begin : base + begin + step, :] = mixed.astype(jnp.bfloat16)
+
+
+def job_kernel(images, slots, finish, add, role_ref, *refs):
+    count = 2 * CHAINS
+    refs = list(refs)
+    take = lambda n: [refs.pop(0) for _ in range(n)]
+    pieces = [[[take(count) for _ in range(2)] for _ in range(2)] for _ in range(images)]
+    weights = [(take(CHAINS), take(CHAINS)) for _ in slots]
+    partial_ref = refs.pop(0) if add else None
+    out_ref, features_ref, weight_ref, total_ref, projected_ref, sems, weight_sems = take(7)
+    core, inner = role_ref[0], role_ref[1]
+    part, span = pieces[0][0][0][0].shape
+    columns = weight_ref.shape[1]
+    slab = weight_ref.shape[0] // len(slots)
+    tokens = 4 * part
+    blocks = span // columns
+
+    def token_copies(image, n):
+        begin = slots[n] * slab
+        for place in range(2):
+            for owner in range(2):
+                row = image * tokens + (2 * place + (1 - core if owner else core)) * part
+                yield pltpu.make_async_copy(
+                    pieces[image][place][owner][begin // span].at[:, pl.ds(begin % span, slab)],
+                    features_ref.at[pl.ds(pl.multiple_of(row, 32), part), pl.ds(n * slab, slab)],
+                    sems.at[(image * len(slots) + n) * 4 + place * 2 + owner],
+                )
+
+    def weight_copies(n, role):
+        for i in range(CHAINS):
+            for b in range(blocks):
+                row = n * slab + (i * blocks + b) * part
+                yield pltpu.make_async_copy(
+                    weights[n][role][i].at[:, pl.ds(b * columns, columns)],
+                    weight_ref.at[pl.ds(row, part)],
+                    weight_sems.at[(n * CHAINS + i) * blocks + b],
+                )
+
+    for n in range(len(slots)):
+
+        @pl.when(inner == 1)
+        def _():
+            for copy in weight_copies(n, 0):
+                copy.start()
+
+        @pl.when(inner != 1)
+        def _():
+            for copy in weight_copies(n, 1):
+                copy.start()
+
+        for copy in token_copies(0, n):
+            copy.start()
+    for image in range(1, images):
+        for n in range(len(slots)):
+            for copy in token_copies(image, n):
+                copy.start()
+
+    step = 256
+    for image in range(images):
+        for n in range(len(slots)):
+            if image == 0:
+                for copy in weight_copies(n, 0):
+                    copy.wait()
+            for copy in token_copies(image, n):
+                copy.wait()
+
+            @pl.loop(0, tokens // step)
+            def _(i):
+                rows = pl.ds(pl.multiple_of(i * step, step), step)
+                from_rows = pl.ds(pl.multiple_of(image * tokens + i * step, step), step)
+                term = jnp.dot(
+                    features_ref[from_rows, n * slab : (n + 1) * slab],
+                    weight_ref[n * slab : (n + 1) * slab, :],
+                    preferred_element_type=jnp.float32,
+                )
+                if n:
+                    term += total_ref[rows, :]
+                elif add:
+                    term += partial_ref[from_rows, :]
+                if n < len(slots) - 1:
+                    total_ref[rows, :] = term
+                elif finish:
+                    projected_ref[rows, :] = term.astype(jnp.bfloat16)
+                else:
+                    out_ref[from_rows, :] = term
+
+        if finish:
+            attend_rows(projected_ref, out_ref, image * tokens)
+
+
+def run_job(core, inner, columns, images, weights, slots=(0, 1, 2, 3), partial=None, finish=True):
+    part, span = images[0][0][0][0].shape
+    slab = span * CHAINS // 2
+    tokens = 4 * part
+    total = len(images) * tokens
+    width = columns // 3
+    anywhere, vmem = pl.BlockSpec(memory_space=pl.ANY), pl.BlockSpec(memory_space=pltpu.VMEM)
+    pieces = [x for image in images for place in image for owner in place for x in owner]
+    pieces += [x for slot in slots for role in weights[slot] for x in role]
+    operands = pieces + ([partial] if partial is not None else [])
+    depth = len(slots) * slab
+    shape = (total, width) if finish else (total, columns)
+    return pl.pallas_call(
+        functools.partial(job_kernel, len(images), slots, finish, partial is not None),
+        out_shape=jax.ShapeDtypeStruct(shape, jnp.bfloat16 if finish else jnp.float32),
+        in_specs=[pl.BlockSpec(memory_space=pltpu.SMEM)]
+        + [anywhere] * len(pieces)
+        + [vmem] * (len(operands) - len(pieces)),
+        out_specs=vmem,
+        scratch_shapes=[
+            pltpu.VMEM((total, depth), jnp.bfloat16),
+            pltpu.VMEM((depth, columns), jnp.bfloat16),
+            pltpu.VMEM((tokens, columns), jnp.float32),
+            pltpu.VMEM((tokens, columns), jnp.bfloat16),
+            pltpu.SemaphoreType.DMA((len(images) * len(slots) * 4,)),
+            pltpu.SemaphoreType.DMA((depth // part,)),
+        ],
+        compiler_params=pltpu.CompilerParams(vmem_limit_bytes=56 << 20),
+        cost_estimate=pl.CostEstimate(
+            flops=2 * total * depth * columns + (4 * total * tokens * width if finish else 0),
+            bytes_accessed=2 * total * depth + 2 * depth * columns,
+            transcendentals=total * tokens if finish else 0,
+        ),
+    )(jnp.stack([core, inner]).astype(jnp.int32), *operands)
+
+
+def shared(tokens, ln_gain, qkv_weight):
+    groups, planes, seqs, cores = (lax.axis_size(a) for a in ("groups", "dp", "seq", "head"))
+    group, plane, seq, core = (lax.axis_index(a) for a in ("groups", "dp", "seq", "head"))
+    _, rows, width = tokens.shape
+    slab, heads, columns = qkv_weight.shape
+    heads, part, depth = heads // groups, rows // cores, columns // 3
+    inner = (plane == 1) | (plane == 2)
+    chains = range(CHAINS)
+    wait = lax.optimization_barrier
+
+    def fold(piece):
+        piece = piece.reshape(-1, part, columns).transpose(1, 0, 2)
+        return piece.reshape(part, -1)
+
+    own = []
+    for j in range(heads):
+        piece = lax.dynamic_slice_in_dim(qkv_weight, group * heads + j, 1, 1)[:, 0]
+        own.append([fold(p) for p in jnp.split(piece, CHAINS)])
+
+    order = (plane, plane ^ 1, 2 - plane // 2, 3 - 3 * (plane // 2))
+    normed = normalize_part(tokens, ln_gain, part, core, order)
+
+    def pick(for_inner, for_ends):
+        return jnp.where(inner, for_inner, for_ends)
+
+    def pair(value):
+        return lax.ppermute(value, "dp", [(0, 1), (1, 0), (2, 3), (3, 2)])
+
+    def outward(value):
+        return lax.ppermute(value, "dp", [(1, 0), (2, 3)])
+
+    def middle(value):
+        return lax.ppermute(value, "dp", [(1, 2), (2, 1)])
+
+    swap = [(0, 1), (1, 0)]
+    beside = lambda value: lax.ppermute(value, "seq", swap)
+    across = lambda value: lax.ppermute(value, "groups", swap)
+    other = lambda value: lax.ppermute(value, "head", swap)
+
+    pairs, middles, xs, ys = [], [], [], []
+    tokens_later = tokens
+    for t in range(6):
+        now = []
+        for i in chains:
+            give = {
+                0: lambda: pick(own[0][i], normed[i]),
+                1: lambda: pick(middles[0][i], normed[CHAINS + i]),
+                2: lambda: pick(own[1][i], own[0][i]),
+                3: lambda: pick(middles[1][i], own[1][i]),
+                4: lambda: pick(middles[3][i], own[2][i]),
+                5: lambda: middles[4][i],
+            }[t]()
+            give_middle = own[t][i] if t < 3 else pairs[t - 1][i]
+            if t < 2:
+                give_x = give_y = normed[t * CHAINS + i]
+            elif t == 2:
+                give_x, give_y = ys[0][i], xs[1][i]
+            elif t < 5:
+                give_x = give_y = pairs[t - 3][i]
+            else:
+                give_x, give_y = ys[3][i], xs[4][i]
+            now.append((give, give_middle, give_x, give_y))
+        got = [
+            (pair(a) if t < 5 else outward(a), middle(b), beside(c), across(d))
+            for a, b, c, d in now
+        ]
+        if t < 5:
+            got, own, normed, tokens_later = wait((got, own, normed, tokens_later))
+        pairs.append([g[0] for g in got])
+        middles.append([g[1] for g in got])
+        xs.append([g[2] for g in got])
+        ys.append([g[3] for g in got])
+        if t == 0:
+            normed_other = normalize_part(tokens_later, ln_gain, part, 1 - core, order)
+
+    def with_other(values):
+        return (values, [other(v) for v in values])
+
+    own_images = (
+        ((normed, normed_other), with_other(xs[0] + xs[1])),
+        (with_other(ys[0] + ys[1]), with_other(xs[2] + ys[2])),
+    )
+    lent_images = (
+        (with_other(pairs[0] + pairs[1]), with_other(xs[3] + xs[4])),
+        (with_other(ys[3] + ys[4]), with_other(xs[5] + ys[5])),
+    )
+
+    def exchange(mixed):
+        got = []
+        for a in range(groups):
+            for b in range(seqs):
+                sent = mixed[(a * seqs + b) * rows : (a * seqs + b + 1) * rows]
+                if a or b:
+                    steps = [
+                        (g * seqs + s, (g + a) % groups * seqs + (s + b) % seqs)
+                        for g in range(groups)
+                        for s in range(seqs)
+                    ]
+                    sent = lax.ppermute(sent, ("groups", "seq"), steps)
+                got.append(sent)
+        return got
+
+    def hand_back(mixed):
+        got = []
+        for a in range(groups):
+            for b in range(seqs):
+                steps = [
+                    (
+                        (g * planes + z) * seqs + s,
+                        ((g + a) % groups * planes + (z ^ 1)) * seqs + (s + b) % seqs,
+                    )
+                    for g in range(groups)
+                    for z in (1, 2)
+                    for s in range(seqs)
+                ]
+                sent = mixed[(a * seqs + b) * rows : (a * seqs + b + 1) * rows]
+                got.append(lax.ppermute(sent, ("groups", "dp", "seq"), steps))
+        return got
+
+    inner_heads = (
+        (own[0], pairs[2], middles[0], middles[3]),
+        (own[1], pairs[3], middles[1], middles[4]),
+        (own[2], pairs[4], middles[2], middles[5]),
+    )
+    end_heads = (
+        (own[0], pairs[0], pairs[1], pairs[4]),
+        (own[1], pairs[2], pairs[3], pairs[5]),
+    )
+    jobs = (
+        tuple(zip(inner_heads[0], inner_heads[0])),
+        tuple(zip(inner_heads[1], end_heads[0])),
+        tuple(zip(inner_heads[2], end_heads[1])),
+    )
+    lent = inner_heads[2]
+    lent = tuple((w, w) for w in (lent[1], lent[0], lent[2], lent[3]))
+
+    results = [exchange(run_job(core, inner, columns, own_images, job)) for job in jobs]
+    results.append(hand_back(run_job(core, inner, columns, lent_images, lent)))
+    results = wait(results)
+
+    received = jnp.stack([
+        jnp.concatenate(
+            [pick(results[j][i], results[j + 1][i]) for j in range(heads)], axis=1
+        )
+        for i in range(groups * seqs)
+    ])
+    blocks = []
+    for s in range(seqs):
+        for g in range(groups):
+            index = (group - g) % groups * seqs + (seq - s) % seqs
+            blocks.append(lax.dynamic_index_in_dim(received, index, 0, keepdims=False))
+    return jnp.concatenate(blocks, axis=1)[None]
+
+
+def per_device(tokens, ln_gain, qkv_weight):
+    groups, planes, seqs, cores = (lax.axis_size(a) for a in ("groups", "dp", "seq", "head"))
+    images, rows, width = tokens.shape
+    slab, heads, _ = qkv_weight.shape
+    if (groups, planes, seqs, cores) == (2, 4, 2, 2) and images == 1 and heads == 3 * groups:
+        part = rows // cores
+        if rows % (32 * cores) == 0 and slab % part == 0 and 2 * slab == qkv_weight.shape[2] * slab // part:
+            return shared(tokens, ln_gain, qkv_weight)
+    return plain(tokens, ln_gain, qkv_weight)
+
+
 def solution(mesh):
     return jax.shard_map(
         per_device,

time: 680 us -> 304 us (0.45)
  waiting for transfers between devices: 557 us -> 127 us
  Pallas kernels: 0 us -> 102 us
  starting transfers between devices: 0.26 us -> 52.2 us
  matrix products: 45.2 us -> 0 us
  blocking collectives: 18 us -> 0 us
  other arithmetic: 20.4 us -> 4.23 us
  local copies, waits for them, and re-layouts: 25.6 us -> 11.7 us
  between operations: 13.2 us -> 1.1 us
    all_gather x3 -> x0, waiting for transfers between devices: 557 us -> none  [the longest x1 479 us: per_device(): piece = lax.all_gather(qkv_weight, 'dp', axis=0, tiled=True)]
    ppermute x0 -> x51, waiting for transfers between devices: none -> 127 us  [the longest x6 64.8 us: shared(): beside = lambda value: lax.ppermute(value, 'seq', swap)]
    pallas_call x0 -> x6, Pallas kernels: none -> 102 us  [the longest x4 88.4 us: run_job(): pl.pallas_call(functools.partial(job_kernel, len(images), slots, finish,...]
    ppermute x0 -> x51, starting transfers between devices: none -> 52.2 us  [the longest x5 12.5 us: pair(): return lax.ppermute(value, 'dp', [(0, 1), (1, 0), (2, 3), (3, 2)])]
    dot_general x2 -> x0, matrix products: 37.1 us -> none  [the longest x1 29.9 us: per_device(): jnp.dot(features, piece.reshape(piece.shape[0], columns), preferred_eleme...]
    all_to_all x1 -> x0, blocking collectives: 18 us -> none  [per_device(): return lax.all_to_all(mixed, 'seq', split_axis=1, concat_axis=2, tiled=True)]
    unnamed x9 -> x56, local copies, waits for them, and re-layouts: 13 us -> 1.93 us
    sub x1 -> x0, matrix products: 8.18 us -> none  [attend(): expo = jnp.exp(scores - highest)]
  transfers between devices with their start and end apart: 3 -> 51, of which waited for: 3 -> 16; matrix products, arithmetic and copies ran while one was open for 2% -> 2% of each run, Pallas kernels for 0% -> 32%
where the time goes in v3:
time: 304 us; the launch traced here: 298 us
  waiting for transfers between devices  127 us (42%)
  Pallas kernels  102 us (34%)
  starting transfers between devices  52.2 us (17%)
  local copies, waits for them, and re-layouts  11.7 us (4%)
  other arithmetic  4.23 us (1%)
    pallas_call x4, Pallas kernels, run_job(): pl.pallas_call(functools.partial(job_kernel, len(images), slots, finish,...  88.4 us
    ppermute x6, waiting for transfers between devices, shared(): beside = lambda value: lax.ppermute(value, 'seq', swap)  64.8 us
    ppermute x5, waiting for transfers between devices, pair(): return lax.ppermute(value, 'dp', [(0, 1), (1, 0), (2, 3), (3, 2)])  42.7 us
    pallas_call x2, Pallas kernels, normalize_part(): pl.pallas_call(normalize_kernel, out_shape=[jax.ShapeDtypeStruct((part, w...  13.2 us
    ppermute x5, starting transfers between devices, pair(): return lax.ppermute(value, 'dp', [(0, 1), (1, 0), (2, 3), (3, 2)])  12.5 us
    ppermute x4, waiting for transfers between devices, hand_back(): got.append(lax.ppermute(sent, ('groups', 'dp', 'seq'), steps))  12 us
    ppermute x9, starting transfers between devices, exchange(): sent = lax.ppermute(sent, ('groups', 'seq'), steps)  10.7 us
    ppermute x6, starting transfers between devices, shared(): across = lambda value: lax.ppermute(value, 'groups', swap)  8.83 us
  transfers between devices with their start and end apart: 51, of which 16 were waited for; matrix products, arithmetic and copies ran while one was open for 2% of the time, Pallas kernels for 32%

profile of v3, /device:TPU:0, one launch (start us, length us, event | category | flops | bytes accessed | tf_op | source)
XLA Modules:
  0.0 298.2 jit_solution(17800798954848041491)
XLA Ops:
  0.0 3.4 %constant_dynamic-slice_fusion = (bf16[1536,1,384]{2,0,1:T(8,128)(2,1)}, bf16[1536,1,384]{2,0,1:T(8,128)(2,1)S(1)}, bf16[1536,1,384]{2,0,1:T(8,128)(2,1)S(1)}) fusion(bf16[1536,6,384]{2,0,1:T(8,128)(2,1)} %param.5, s32[]{:T(128)S(6)} %select_n.136, s32[]{:T(128)S(6)} %select_n.132, s32[]{:T(128)S(6)} %select_n.135), kind=kLoop, calls=%fused_computation.27 | loop fusion | bytes 7077900 | tf_op jit(solution)/shard_map/dynamic_slice | solution.py:256
  3.6 0.8 stack.70.place_ref
  4.4 6.5 %shard_map.37 = (bf16[192,3072]{1,0:T(8,128)(2,1)}, bf16[192,3072]{1,0:T(8,128)(2,1)}) custom-call(s32[5]{0:T(128)} %stack.70.place_ref, bf16[1,384,6144]{2,1,0:T(8,128)(2,1)} %tokens_ref.2, f32[1,6144]{1,0:T(1,128)} %bitcast.60), custom_call_target="tpu_custom_call" | custom-call | flops 9437184 | bytes 4718592 | tf_op jit(solution)/shard_map/pallas_call | solution.py:80
  10.9 1.5 broadcast_select_fusion.4
  12.4 1.7 collective-permute-start
  14.1 0.7 collective-permute-start.1
  14.9 1.6 collective-permute-start.2
  16.4 1.5 collective-permute-start.3
  18.2 1.4 copy-done.3
  19.8 21.0 %collective-permute-done.refs_19_.refs_0_ = bf16[192,3072]{1,0:T(8,128)(2,1)S(1)} collective-permute-done((bf16[192,3072]{1,0:T(8,128)(2,1)S(1)}, bf16[192,3072]{1,0:T(8,128)(2,1)S(1)}, u32[]{:S(2)}, u32[]{:S(2)}) %collective-permute-start) | collective-permute-done | bytes 1179680 | tf_op jit(solution)/shard_map/ppermute | solution.py:266
  40.8 1.6 collective-permute-done.2.refs_4_
  42.4 1.3 collective-permute-done.3.refs_8_
  43.8 5.4 %collective-permute-start.4 = (bf16[192,3072]{1,0:T(8,128)(2,1)S(1)}, bf16[192,3072]{1,0:T(8,128)(2,1)S(1)}, u32[]{:S(2)}, u32[]{:S(2)}) collective-permute-start(bf16[192,3072]{1,0:T(8,128)(2,1)S(1)} %broadcast_select_fusion.3), channel_id=1, source_target_pairs={{0,4},{4,0},{8,12},{12,8},{1,5},{5,1},{9,13},{13,9},{2,6},{6,2},{1... | collective-permute-start | bytes 3538952 | tf_op jit(solution)/shard_map/ppermute | solution.py:266
  49.2 0.7 collective-permute-start.5
  50.5 1.5 collective-permute-start.7
  52.1 1.5 collective-permute-start.10
  53.5 19.9 %collective-permute-done.4.refs_21_.refs_1_ = bf16[192,3072]{1,0:T(8,128)(2,1)S(1)} collective-permute-done((bf16[192,3072]{1,0:T(8,128)(2,1)S(1)}, bf16[192,3072]{1,0:T(8,128)(2,1)S(1)}, u32[]{:S(2)}, u32[]{:S(2)}) %collective-permute-start.4) | collective-permute-done | bytes 1179680 | tf_op jit(solution)/shard_map/ppermute | solution.py:266
  73.4 5.6 %collective-permute-done.6.refs_5_ = bf16[192,3072]{1,0:T(8,128)(2,1)} collective-permute-done((bf16[192,3072]{1,0:T(8,128)(2,1)S(1)}, bf16[192,3072]{1,0:T(8,128)(2,1)}, u32[]{:S(2)}, u32[]{:S(2)}) %collective-permute-start.6) | collective-permute-done | bytes 1179680 | tf_op jit(solution)/shard_map/ppermute | solution.py:275
  79.2 1.6 collective-permute-start.8
  81.5 1.6 collective-permute-start.11
  83.0 0.9 collective-permute-start.14
  84.0 20.3 %collective-permute-done.10.refs_12_ = bf16[192,3072]{1,0:T(8,128)(2,1)} collective-permute-done((bf16[192,3072]{1,0:T(8,128)(2,1)S(1)}, bf16[192,3072]{1,0:T(8,128)(2,1)}, u32[]{:S(2)}, u32[]{:S(2)}) %collective-permute-start.10) | collective-permute-done | bytes 1179680 | tf_op jit(solution)/shard_map/ppermute | solution.py:275
  104.3 1.5 collective-permute-start.15
  105.8 2.7 collective-permute-done.11.refs_13_
  108.7 1.5 collective-permute-start.12
  110.2 0.7 collective-permute-start.13
  111.0 15.3 %collective-permute-done.14.refs_4_ = bf16[192,3072]{1,0:T(8,128)(2,1)} collective-permute-done((bf16[192,3072]{1,0:T(8,128)(2,1)S(1)}, bf16[192,3072]{1,0:T(8,128)(2,1)}, u32[]{:S(2)}, u32[]{:S(2)}) %collective-permute-start.14) | collective-permute-done | bytes 1179680 | tf_op jit(solution)/shard_map/ppermute | solution.py:275
  126.3 3.5 %collective-permute-done.15.refs_8_ = bf16[192,3072]{1,0:T(8,128)(2,1)} collective-permute-done((bf16[192,3072]{1,0:T(8,128)(2,1)S(1)}, bf16[192,3072]{1,0:T(8,128)(2,1)}, u32[]{:S(2)}, u32[]{:S(2)}) %collective-permute-start.15) | collective-permute-done | bytes 1179680 | tf_op jit(solution)/shard_map/ppermute | solution.py:276
  130.5 1.5 collective-permute-start.19
  132.2 2.4 collective-permute-start.16
  134.6 1.7 collective-permute-start.17
  136.3 22.0 %collective-permute-done.18.refs_5_ = bf16[192,3072]{1,0:T(8,128)(2,1)S(1)} collective-permute-done((bf16[192,3072]{1,0:T(8,128)(2,1)S(1)}, bf16[192,3072]{1,0:T(8,128)(2,1)S(1)}, u32[]{:S(2)}, u32[]{:S(2)}) %collective-permute-start.18) | collective-permute-done | bytes 1179680 | tf_op jit(solution)/shard_map/ppermute | solution.py:275
  158.9 1.8 collective-permute-done.16.refs_23_.refs_18_.refs_16_.refs_17_
  162.6 6.7 %shard_map.38 = (bf16[192,3072]{1,0:T(8,128)(2,1)}, bf16[192,3072]{1,0:T(8,128)(2,1)}) custom-call(s32[5]{0:T(128)} %stack.72.place_ref, bf16[1,384,6144]{2,1,0:T(8,128)(2,1)} %tokens_ref.2, f32[1,6144]{1,0:T(1,128)} %bitcast.61), custom_call_target="tpu_custom_call" | custom-call | flops 9437184 | bytes 4718592 | tf_op jit(solution)/shard_map/pallas_call | solution.py:80
  169.4 1.0 collective-permute-start.43
  170.3 0.7 collective-permute-start.32
  171.1 1.3 collective-permute-start.33
  172.4 1.2 collective-permute-start.44
  173.6 22.0 %shard_map.39 = bf16[1536,128]{1,0:T(8,128)(2,1)} custom-call(s32[2]{0:T(128)} %pad_add_fusion.role_ref, bf16[192,3072]{1,0:T(8,128)(2,1)} %get-tuple-element.103.refs_0_, bf16[192,3072]{1,0:T(8,128)(2,1)} %get-tuple-element.104.refs_1_, bf16[192,3072]{1,0:T(8,128)(2,1)} %get-tuple-element.105.refs_2_, bf16[192,3072]{1,0:T(8,128)(2,1)} %get-tuple-element.106.refs_3_, ...), custom_call_target="tpu_custom_call" | custom-call | flops 7851737088 | bytes 23592960 | tf_op jit(solution)/shard_map/pallas_call | solution.py:216
  195.6 1.1 fusion.3
  196.7 22.3 %shard_map.40 = bf16[1536,128]{1,0:T(8,128)(2,1)} custom-call(s32[2]{0:T(128)} %pad_add_fusion.role_ref, bf16[192,3072]{1,0:T(8,128)(2,1)} %get-tuple-element.103.refs_0_, bf16[192,3072]{1,0:T(8,128)(2,1)} %get-tuple-element.104.refs_1_, bf16[192,3072]{1,0:T(8,128)(2,1)} %get-tuple-element.105.refs_2_, bf16[192,3072]{1,0:T(8,128)(2,1)} %get-tuple-element.106.refs_3_, ...), custom_call_target="tpu_custom_call" | custom-call | flops 7851737088 | bytes 23592960 | tf_op jit(solution)/shard_map/pallas_call | solution.py:216
  220.8 1.1 fusion.2
  221.8 21.9 %shard_map.41 = bf16[1536,128]{1,0:T(8,128)(2,1)} custom-call(s32[2]{0:T(128)} %pad_add_fusion.role_ref, bf16[192,3072]{1,0:T(8,128)(2,1)} %get-tuple-element.103.refs_0_, bf16[192,3072]{1,0:T(8,128)(2,1)} %get-tuple-element.104.refs_1_, bf16[192,3072]{1,0:T(8,128)(2,1)} %get-tuple-element.105.refs_2_, bf16[192,3072]{1,0:T(8,128)(2,1)} %get-tuple-element.106.refs_3_, ...), custom_call_target="tpu_custom_call" | custom-call | flops 7851737088 | bytes 23592960 | tf_op jit(solution)/shard_map/pallas_call | solution.py:216
  243.8 1.1 fusion.1
  244.8 1.2 collective-permute-start.26
  246.0 0.9 collective-permute-start.27
  247.0 1.4 collective-permute-start.28
  248.4 1.1 collective-permute-start.29
  249.5 0.9 collective-permute-start.30
  250.5 22.1 %shard_map.42 = bf16[1536,128]{1,0:T(8,128)(2,1)} custom-call(s32[2]{0:T(128)} %pad_add_fusion.role_ref, bf16[192,3072]{1,0:T(8,128)(2,1)} %copy-done.9, bf16[192,3072]{1,0:T(8,128)(2,1)} %copy-done.10, bf16[192,3072]{1,0:T(8,128)(2,1)} %copy-done.14, bf16[192,3072]{1,0:T(8,128)(2,1)} %copy-done.22, bf16[192,3072]{1,0:T(8,128)(2,1)} %collective-permute-done.14.refs_4_, ...), custom_call_target="tpu_custom_call" | custom-call | flops 7851737088 | bytes 23592960 | tf_op jit(solution)/shard_map/pallas_call | solution.py:216
  272.6 1.5 collective-permute-start.31
  274.1 1.1 collective-permute-start.34
  275.2 0.9 collective-permute-start.35
  276.2 1.1 fusion
  277.2 1.5 collective-permute-start.36
  278.8 1.3 collective-permute-start.47
  280.1 1.3 collective-permute-start.48
  281.4 1.3 collective-permute-start.49
  282.7 1.3 collective-permute-start.50
  284.1 7.5 %collective-permute-done.47 = bf16[384,128]{1,0:T(8,128)(2,1)S(1)} collective-permute-done((bf16[384,128]{1,0:T(8,128)(2,1)S(1)}, bf16[384,128]{1,0:T(8,128)(2,1)S(1)}, u32[]{:S(2)}, u32[]{:S(2)}) %collective-permute-start.47) | collective-permute-done | bytes 98336 | tf_op jit(solution)/shard_map/ppermute | solution.py:356
  291.6 2.1 collective-permute-done.48
  293.7 1.3 collective-permute-done.49
  295.0 1.1 collective-permute-done.50
  296.7 1.1 maximum_bitcast_fusion
  (125 shorter events, 8.1 us)
Async XLA Ops:
  3.6 75.4 %copy-start.1 = (bf16[8,24,8,384]{3,2,0,1:T(8,128)(2,1)}, bf16[8,24,8,384]{3,2,0,1:T(8,128)(2,1)S(1)}, u32[]{:S(2)}) copy-start(bf16[8,24,8,384]{3,2,0,1:T(8,128)(2,1)S(1)} %copy.7) | copy-start | bytes 3538948
  12.4 28.4 %collective-permute-start = (bf16[192,3072]{1,0:T(8,128)(2,1)S(1)}, bf16[192,3072]{1,0:T(8,128)(2,1)S(1)}, u32[]{:S(2)}, u32[]{:S(2)}) collective-permute-start(bf16[192,3072]{1,0:T(8,128)(2,1)S(1)} %broadcast_select_fusion.4), channel_id=1, source_target_pairs={{0,4},{4,0},{8,12},{12,8},{1,5},{5,1},{9,13},{13,9},{2,6},{6,2},{1... | collective-permute-start | bytes 3538952 | tf_op jit(solution)/shard_map/ppermute | solution.py:266
  14.1 26.7 %collective-permute-start.1 = (bf16[192,3072]{1,0:T(8,128)(2,1)S(1)}, bf16[192,3072]{1,0:T(8,128)(2,1)S(1)}, u32[]{:S(2)}, u32[]{:S(2)}) collective-permute-start(bf16[192,3072]{1,0:T(8,128)(2,1)S(1)} %bitcast.47), channel_id=1, source_target_pairs={{4,8},{8,4},{5,9},{9,5},{6,10},{10,6},{7,11},{11,7},{20,24},{24,20... | collective-permute-start | bytes 3538952 | tf_op jit(solution)/shard_map/ppermute | solution.py:272
  14.9 27.5 %collective-permute-start.2 = (bf16[192,3072]{1,0:T(8,128)(2,1)S(1)}, bf16[192,3072]{1,0:T(8,128)(2,1)S(1)}, u32[]{:S(2)}, u32[]{:S(2)}) collective-permute-start(bf16[192,3072]{1,0:T(8,128)(2,1)S(1)} %copy-done.4), channel_id=1, source_target_pairs={{0,2},{2,0},{1,3},{3,1},{4,6},{6,4},{5,7},{7,5},{8,10},{10,8},{9,1... | collective-permute-start | bytes 3538952 | tf_op jit(solution)/shard_map/ppermute | solution.py:275
  16.4 27.2 %collective-permute-start.3 = (bf16[192,3072]{1,0:T(8,128)(2,1)S(1)}, bf16[192,3072]{1,0:T(8,128)(2,1)S(1)}, u32[]{:S(2)}, u32[]{:S(2)}) collective-permute-start(bf16[192,3072]{1,0:T(8,128)(2,1)S(1)} %copy-done.4), channel_id=1, source_target_pairs={{0,16},{16,0},{1,17},{17,1},{2,18},{18,2},{3,19},{19,3},{4,20},{20... | collective-permute-start | bytes 3538952 | tf_op jit(solution)/shard_map/ppermute | solution.py:276
  18.2 90.4 %copy-start = (bf16[8,24,8,384]{3,2,0,1:T(8,128)(2,1)}, bf16[8,24,8,384]{3,2,0,1:T(8,128)(2,1)S(1)}, u32[]{:S(2)}) copy-start(bf16[8,24,8,384]{3,2,0,1:T(8,128)(2,1)S(1)} %copy.8) | copy-start | bytes 3538948
  19.8 112.3 %copy-start.2 = (bf16[8,24,8,384]{3,2,0,1:T(8,128)(2,1)}, bf16[8,24,8,384]{3,2,0,1:T(8,128)(2,1)S(1)}, u32[]{:S(2)}) copy-start(bf16[8,24,8,384]{3,2,0,1:T(8,128)(2,1)S(1)} %copy.9) | copy-start | bytes 3538948
  40.8 89.1 %copy-start.9 = (bf16[192,3072]{1,0:T(8,128)(2,1)}, bf16[192,3072]{1,0:T(8,128)(2,1)S(1)}, u32[]{:S(2)}) copy-start(bf16[192,3072]{1,0:T(8,128)(2,1)S(1)} %collective-permute-done.refs_19_.refs_0_) | copy-start | bytes 3538948
  42.4 68.5 %copy-start.11 = (bf16[192,3072]{1,0:T(8,128)(2,1)}, bf16[192,3072]{1,0:T(8,128)(2,1)S(1)}, u32[]{:S(2)}) copy-start(bf16[192,3072]{1,0:T(8,128)(2,1)S(1)} %collective-permute-done.2.refs_4_) | copy-start | bytes 3538948
  43.7 82.7 %copy-start.12 = (bf16[192,3072]{1,0:T(8,128)(2,1)}, bf16[192,3072]{1,0:T(8,128)(2,1)S(1)}, u32[]{:S(2)}) copy-start(bf16[192,3072]{1,0:T(8,128)(2,1)S(1)} %collective-permute-done.3.refs_8_) | copy-start | bytes 3538948
  43.8 29.6 %collective-permute-start.4 = (bf16[192,3072]{1,0:T(8,128)(2,1)S(1)}, bf16[192,3072]{1,0:T(8,128)(2,1)S(1)}, u32[]{:S(2)}, u32[]{:S(2)}) collective-permute-start(bf16[192,3072]{1,0:T(8,128)(2,1)S(1)} %broadcast_select_fusion.3), channel_id=1, source_target_pairs={{0,4},{4,0},{8,12},{12,8},{1,5},{5,1},{9,13},{13,9},{2,6},{6,2},{1... | collective-permute-start | bytes 3538952 | tf_op jit(solution)/shard_map/ppermute | solution.py:266
  49.2 24.2 %collective-permute-start.5 = (bf16[192,3072]{1,0:T(8,128)(2,1)S(1)}, bf16[192,3072]{1,0:T(8,128)(2,1)S(1)}, u32[]{:S(2)}, u32[]{:S(2)}) collective-permute-start(bf16[192,3072]{1,0:T(8,128)(2,1)S(1)} %bitcast.41), channel_id=1, source_target_pairs={{4,8},{8,4},{5,9},{9,5},{6,10},{10,6},{7,11},{11,7},{20,24},{24,20... | collective-permute-start | bytes 3538952 | tf_op jit(solution)/shard_map/ppermute | solution.py:272
  49.9 29.1 %collective-permute-start.6 = (bf16[192,3072]{1,0:T(8,128)(2,1)S(1)}, bf16[192,3072]{1,0:T(8,128)(2,1)}, u32[]{:S(2)}, u32[]{:S(2)}) collective-permute-start(bf16[192,3072]{1,0:T(8,128)(2,1)S(1)} %copy-done.5), channel_id=1, source_target_pairs={{0,2},{2,0},{1,3},{3,1},{4,6},{6,4},{5,7},{7,5},{8,10},{10,8},{9,1... | collective-permute-start | bytes 3538952 | tf_op jit(solution)/shard_map/ppermute | solution.py:275
  50.5 28.5 %collective-permute-start.7 = (bf16[192,3072]{1,0:T(8,128)(2,1)S(1)}, bf16[192,3072]{1,0:T(8,128)(2,1)}, u32[]{:S(2)}, u32[]{:S(2)}) collective-permute-start(bf16[192,3072]{1,0:T(8,128)(2,1)S(1)} %copy-done.5), channel_id=1, source_target_pairs={{0,16},{16,0},{1,17},{17,1},{2,18},{18,2},{3,19},{19,3},{4,20},{20... | collective-permute-start | bytes 3538952 | tf_op jit(solution)/shard_map/ppermute | solution.py:276
  52.1 52.2 %collective-permute-start.10 = (bf16[192,3072]{1,0:T(8,128)(2,1)S(1)}, bf16[192,3072]{1,0:T(8,128)(2,1)}, u32[]{:S(2)}, u32[]{:S(2)}) collective-permute-start(bf16[192,3072]{1,0:T(8,128)(2,1)S(1)} %collective-permute-done.3.refs_8_), channel_id=1, source_target_pairs={{0,2},{2,0},{1,3},{3,1},{4,6},{6,4},{5,7},{7,5},{8,10},{10,8},{9,1... | collective-permute-start | bytes 3538952 | tf_op jit(solution)/shard_map/ppermute | solution.py:275
  73.4 85.2 %copy-start.10 = (bf16[192,3072]{1,0:T(8,128)(2,1)}, bf16[192,3072]{1,0:T(8,128)(2,1)S(1)}, u32[]{:S(2)}) copy-start(bf16[192,3072]{1,0:T(8,128)(2,1)S(1)} %collective-permute-done.4.refs_21_.refs_1_) | copy-start | bytes 3538948
  73.4 35.1 %copy-start.7 = (bf16[192,3072]{1,0:T(8,128)(2,1)}, bf16[192,3072]{1,0:T(8,128)(2,1)S(1)}, u32[]{:S(2)}) copy-start(bf16[192,3072]{1,0:T(8,128)(2,1)S(1)} %collective-permute-done.5.refs_20_) | copy-start | bytes 3538948
  79.2 26.6 %collective-permute-start.8 = (bf16[192,3072]{1,0:T(8,128)(2,1)S(1)}, bf16[192,3072]{1,0:T(8,128)(2,1)S(1)}, u32[]{:S(2)}, u32[]{:S(2)}) collective-permute-start(bf16[192,3072]{1,0:T(8,128)(2,1)S(1)} %broadcast_select_fusion.2), channel_id=1, source_target_pairs={{0,4},{4,0},{8,12},{12,8},{1,5},{5,1},{9,13},{13,9},{2,6},{6,2},{1... | collective-permute-start | bytes 3538952 | tf_op jit(solution)/shard_map/ppermute | solution.py:266
  80.7 25.1 %collective-permute-start.9 = (bf16[192,3072]{1,0:T(8,128)(2,1)S(1)}, bf16[192,3072]{1,0:T(8,128)(2,1)S(1)}, u32[]{:S(2)}, u32[]{:S(2)}) collective-permute-start(bf16[192,3072]{1,0:T(8,128)(2,1)S(1)} %bitcast.52), channel_id=1, source_target_pairs={{4,8},{8,4},{5,9},{9,5},{6,10},{10,6},{7,11},{11,7},{20,24},{24,20... | collective-permute-start | bytes 3538952 | tf_op jit(solution)/shard_map/ppermute | solution.py:272
  81.5 27.1 %collective-permute-start.11 = (bf16[192,3072]{1,0:T(8,128)(2,1)}, bf16[192,3072]{1,0:T(8,128)(2,1)}, u32[]{:S(2)}, u32[]{:S(2)}) collective-permute-start(bf16[192,3072]{1,0:T(8,128)(2,1)} %collective-permute-done.6.refs_5_), channel_id=1, source_target_pairs={{0,16},{16,0},{1,17},{17,1},{2,18},{18,2},{3,19},{19,3},{4,20},{20... | collective-permute-start | bytes 3538952 | tf_op jit(solution)/shard_map/ppermute | solution.py:276
  83.0 43.3 %collective-permute-start.14 = (bf16[192,3072]{1,0:T(8,128)(2,1)S(1)}, bf16[192,3072]{1,0:T(8,128)(2,1)}, u32[]{:S(2)}, u32[]{:S(2)}) collective-permute-start(bf16[192,3072]{1,0:T(8,128)(2,1)S(1)} %collective-permute-done.refs_19_.refs_0_), channel_id=1, source_target_pairs={{0,2},{2,0},{1,3},{3,1},{4,6},{6,4},{5,7},{7,5},{8,10},{10,8},{9,1... | collective-permute-start | bytes 3538952 | tf_op jit(solution)/shard_map/ppermute | solution.py:275
  104.3 25.6 %collective-permute-start.15 = (bf16[192,3072]{1,0:T(8,128)(2,1)S(1)}, bf16[192,3072]{1,0:T(8,128)(2,1)}, u32[]{:S(2)}, u32[]{:S(2)}) collective-permute-start(bf16[192,3072]{1,0:T(8,128)(2,1)S(1)} %collective-permute-done.refs_19_.refs_0_), channel_id=1, source_target_pairs={{0,16},{16,0},{1,17},{17,1},{2,18},{18,2},{3,19},{19,3},{4,20},{20... | collective-permute-start | bytes 3538952 | tf_op jit(solution)/shard_map/ppermute | solution.py:276
  108.7 21.2 %collective-permute-start.12 = (bf16[192,3072]{1,0:T(8,128)(2,1)S(1)}, bf16[192,3072]{1,0:T(8,128)(2,1)S(1)}, u32[]{:S(2)}, u32[]{:S(2)}) collective-permute-start(bf16[192,3072]{1,0:T(8,128)(2,1)S(1)} %broadcast_select_fusion.1), channel_id=1, source_target_pairs={{0,4},{4,0},{8,12},{12,8},{1,5},{5,1},{9,13},{13,9},{2,6},{6,2},{1... | collective-permute-start | bytes 3538952 | tf_op jit(solution)/shard_map/ppermute | solution.py:266
  110.2 20.4 %collective-permute-start.13 = (bf16[192,3072]{1,0:T(8,128)(2,1)S(1)}, bf16[192,3072]{1,0:T(8,128)(2,1)S(1)}, u32[]{:S(2)}, u32[]{:S(2)}) collective-permute-start(bf16[192,3072]{1,0:T(8,128)(2,1)S(1)} %collective-permute-done.8.refs_18_.refs_19_), channel_id=1, source_target_pairs={{4,8},{8,4},{5,9},{9,5},{6,10},{10,6},{7,11},{11,7},{20,24},{24,20... | collective-permute-start | bytes 3538952 | tf_op jit(solution)/shard_map/ppermute | solution.py:272
  110.9 21.3 %collective-permute-start.20 = (bf16[192,3072]{1,0:T(8,128)(2,1)S(1)}, bf16[192,3072]{1,0:T(8,128)(2,1)S(1)}, u32[]{:S(2)}, u32[]{:S(2)}) collective-permute-start(bf16[192,3072]{1,0:T(8,128)(2,1)S(1)} %collective-permute-done.2.refs_4_), channel_id=1, source_target_pairs={{0,1},{1,0},{2,3},{3,2},{4,5},{5,4},{6,7},{7,6},{8,9},{9,8},{10,11... | collective-permute-start | bytes 3538952 | tf_op jit(solution)/shard_map/ppermute | solution.py:277
  126.3 8.2 %collective-permute-start.22 = (bf16[192,3072]{1,0:T(8,128)(2,1)S(1)}, bf16[192,3072]{1,0:T(8,128)(2,1)S(1)}, u32[]{:S(2)}, u32[]{:S(2)}) collective-permute-start(bf16[192,3072]{1,0:T(8,128)(2,1)S(1)} %collective-permute-done.3.refs_8_), channel_id=1, source_target_pairs={{0,1},{1,0},{2,3},{3,2},{4,5},{5,4},{6,7},{7,6},{8,9},{9,8},{10,11... | collective-permute-start | bytes 3538952 | tf_op jit(solution)/shard_map/ppermute | solution.py:277
  129.9 6.4 %collective-permute-start.37 = (bf16[192,3072]{1,0:T(8,128)(2,1)S(1)}, bf16[192,3072]{1,0:T(8,128)(2,1)S(1)}, u32[]{:S(2)}, u32[]{:S(2)}) collective-permute-start(bf16[192,3072]{1,0:T(8,128)(2,1)S(1)} %collective-permute-done.refs_19_.refs_0_), channel_id=1, source_target_pairs={{0,1},{1,0},{2,3},{3,2},{4,5},{5,4},{6,7},{7,6},{8,9},{9,8},{10,11... | collective-permute-start | bytes 3538952 | tf_op jit(solution)/shard_map/ppermute | solution.py:277
  129.9 28.4 %collective-permute-start.18 = (bf16[192,3072]{1,0:T(8,128)(2,1)S(1)}, bf16[192,3072]{1,0:T(8,128)(2,1)S(1)}, u32[]{:S(2)}, u32[]{:S(2)}) collective-permute-start(bf16[192,3072]{1,0:T(8,128)(2,1)S(1)} %collective-permute-done.4.refs_21_.refs_1_), channel_id=1, source_target_pairs={{0,2},{2,0},{1,3},{3,1},{4,6},{6,4},{5,7},{7,5},{8,10},{10,8},{9,1... | collective-permute-start | bytes 3538952 | tf_op jit(solution)/shard_map/ppermute | solution.py:275
  130.5 28.0 %collective-permute-start.19 = (bf16[192,3072]{1,0:T(8,128)(2,1)S(1)}, bf16[192,3072]{1,0:T(8,128)(2,1)S(1)}, u32[]{:S(2)}, u32[]{:S(2)}) collective-permute-start(bf16[192,3072]{1,0:T(8,128)(2,1)S(1)} %collective-permute-done.4.refs_21_.refs_1_), channel_id=1, source_target_pairs={{0,16},{16,0},{1,17},{17,1},{2,18},{18,2},{3,19},{19,3},{4,20},{20... | collective-permute-start | bytes 3538952 | tf_op jit(solution)/shard_map/ppermute | solution.py:276
  132.2 28.5 %copy-start.21 = (bf16[192,3072]{1,0:T(8,128)(2,1)}, bf16[192,3072]{1,0:T(8,128)(2,1)S(1)}, u32[]{:S(2)}) copy-start(bf16[192,3072]{1,0:T(8,128)(2,1)S(1)} %collective-permute-done.20.refs_6_) | copy-start | bytes 3538948
  132.2 28.5 %collective-permute-start.16 = (bf16[192,3072]{1,0:T(8,128)(2,1)S(1)}, bf16[192,3072]{1,0:T(8,128)(2,1)}, u32[]{:S(2)}, u32[]{:S(2)}) collective-permute-start(bf16[192,3072]{1,0:T(8,128)(2,1)S(1)} %broadcast_select_fusion), channel_id=1, source_target_pairs={{0,4},{4,0},{8,12},{12,8},{1,5},{5,1},{9,13},{13,9},{2,6},{6,2},{1... | collective-permute-start | bytes 3538952 | tf_op jit(solution)/shard_map/ppermute | solution.py:266
  134.6 26.2 %copy-start.23 = (bf16[192,3072]{1,0:T(8,128)(2,1)}, bf16[192,3072]{1,0:T(8,128)(2,1)S(1)}, u32[]{:S(2)}) copy-start(bf16[192,3072]{1,0:T(8,128)(2,1)S(1)} %collective-permute-done.22.refs_10_) | copy-start | bytes 3538948
  134.6 26.1 %collective-permute-start.17 = (bf16[192,3072]{1,0:T(8,128)(2,1)S(1)}, bf16[192,3072]{1,0:T(8,128)(2,1)}, u32[]{:S(2)}, u32[]{:S(2)}) collective-permute-start(bf16[192,3072]{1,0:T(8,128)(2,1)S(1)} %collective-permute-done.12.refs_18_.refs_21_), channel_id=1, source_target_pairs={{4,8},{8,4},{5,9},{9,5},{6,10},{10,6},{7,11},{11,7},{20,24},{24,20... | collective-permute-start | bytes 3538952 | tf_op jit(solution)/shard_map/ppermute | solution.py:272
  136.3 24.4 %copy-start.14 = (bf16[192,3072]{1,0:T(8,128)(2,1)}, bf16[192,3072]{1,0:T(8,128)(2,1)S(1)}, u32[]{:S(2)}) copy-start(bf16[192,3072]{1,0:T(8,128)(2,1)S(1)} %collective-permute-done.37.refs_2_) | copy-start | bytes 3538948
  136.3 33.0 %collective-permute-start.21 = (bf16[192,3072]{1,0:T(8,128)(2,1)}, bf16[192,3072]{1,0:T(8,128)(2,1)S(1)}, u32[]{:S(2)}, u32[]{:S(2)}) collective-permute-start(bf16[192,3072]{1,0:T(8,128)(2,1)} %collective-permute-done.6.refs_5_), channel_id=1, source_target_pairs={{0,1},{1,0},{2,3},{3,2},{4,5},{5,4},{6,7},{7,6},{8,9},{9,8},{10,11... | collective-permute-start | bytes 3538952 | tf_op jit(solution)/shard_map/ppermute | solution.py:277
  158.3 11.1 %collective-permute-start.23 = (bf16[192,3072]{1,0:T(8,128)(2,1)}, bf16[192,3072]{1,0:T(8,128)(2,1)}, u32[]{:S(2)}, u32[]{:S(2)}) collective-permute-start(bf16[192,3072]{1,0:T(8,128)(2,1)} %collective-permute-done.7.refs_9_), channel_id=1, source_target_pairs={{0,1},{1,0},{2,3},{3,2},{4,5},{5,4},{6,7},{7,6},{8,9},{9,8},{10,11... | collective-permute-start | bytes 3538952 | tf_op jit(solution)/shard_map/ppermute | solution.py:277
  158.6 11.8 %collective-permute-start.38 = (bf16[192,3072]{1,0:T(8,128)(2,1)S(1)}, bf16[192,3072]{1,0:T(8,128)(2,1)S(1)}, u32[]{:S(2)}, u32[]{:S(2)}) collective-permute-start(bf16[192,3072]{1,0:T(8,128)(2,1)S(1)} %collective-permute-done.4.refs_21_.refs_1_), channel_id=1, source_target_pairs={{0,1},{1,0},{2,3},{3,2},{4,5},{5,4},{6,7},{7,6},{8,9},{9,8},{10,11... | collective-permute-start | bytes 3538952 | tf_op jit(solution)/shard_map/ppermute | solution.py:277
  160.7 10.4 %collective-permute-start.24 = (bf16[192,3072]{1,0:T(8,128)(2,1)}, bf16[192,3072]{1,0:T(8,128)(2,1)}, u32[]{:S(2)}, u32[]{:S(2)}) collective-permute-start(bf16[192,3072]{1,0:T(8,128)(2,1)} %collective-permute-done.10.refs_12_), channel_id=1, source_target_pairs={{0,1},{1,0},{2,3},{3,2},{4,5},{5,4},{6,7},{7,6},{8,9},{9,8},{10,11... | collective-permute-start | bytes 3538952 | tf_op jit(solution)/shard_map/ppermute | solution.py:277
  160.7 11.6 %collective-permute-start.25 = (bf16[192,3072]{1,0:T(8,128)(2,1)}, bf16[192,3072]{1,0:T(8,128)(2,1)}, u32[]{:S(2)}, u32[]{:S(2)}) collective-permute-start(bf16[192,3072]{1,0:T(8,128)(2,1)} %collective-permute-done.11.refs_13_), channel_id=1, source_target_pairs={{0,1},{1,0},{2,3},{3,2},{4,5},{5,4},{6,7},{7,6},{8,9},{9,8},{10,11... | collective-permute-start | bytes 3538952 | tf_op jit(solution)/shard_map/ppermute | solution.py:277
  169.3 49.8 %collective-permute-start.39 = (bf16[192,3072]{1,0:T(8,128)(2,1)}, bf16[192,3072]{1,0:T(8,128)(2,1)S(1)}, u32[]{:S(2)}, u32[]{:S(2)}) collective-permute-start(bf16[192,3072]{1,0:T(8,128)(2,1)} %collective-permute-done.14.refs_4_), channel_id=1, source_target_pairs={{0,1},{1,0},{2,3},{3,2},{4,5},{5,4},{6,7},{7,6},{8,9},{9,8},{10,11... | collective-permute-start | bytes 3538952 | tf_op jit(solution)/shard_map/ppermute | solution.py:277
  169.4 49.8 %collective-permute-start.43 = (bf16[192,3072]{1,0:T(8,128)(2,1)}, bf16[192,3072]{1,0:T(8,128)(2,1)}, u32[]{:S(2)}, u32[]{:S(2)}) collective-permute-start(bf16[192,3072]{1,0:T(8,128)(2,1)} %collective-permute-done.15.refs_8_), channel_id=1, source_target_pairs={{0,2},{2,0},{1,3},{3,1},{4,6},{6,4},{5,7},{7,5},{8,10},{10,8},{9,1... | collective-permute-start | bytes 3538952 | tf_op jit(solution)/shard_map/ppermute | solution.py:275
  170.3 25.3 %copy-start.22 = (bf16[192,3072]{1,0:T(8,128)(2,1)}, bf16[192,3072]{1,0:T(8,128)(2,1)S(1)}, u32[]{:S(2)}) copy-start(bf16[192,3072]{1,0:T(8,128)(2,1)S(1)} %collective-permute-done.38.refs_3_) | copy-start | bytes 3538948
  170.3 49.3 %collective-permute-start.32 = (bf16[192,3072]{1,0:T(8,128)(2,1)}, bf16[192,3072]{1,0:T(8,128)(2,1)S(1)}, u32[]{:S(2)}, u32[]{:S(2)}) collective-permute-start(bf16[192,3072]{1,0:T(8,128)(2,1)} %collective-permute-done.16.refs_23_.refs_18_.refs_16_.refs_17_), channel_id=1, source_target_pairs={{4,8},{8,4},{5,9},{9,5},{6,10},{10,6},{7,11},{11,7},{20,24},{24,20... | collective-permute-start | bytes 3538952 | tf_op jit(solution)/shard_map/ppermute | solution.py:272
  171.1 48.7 %collective-permute-start.33 = (bf16[192,3072]{1,0:T(8,128)(2,1)}, bf16[192,3072]{1,0:T(8,128)(2,1)}, u32[]{:S(2)}, u32[]{:S(2)}) collective-permute-start(bf16[192,3072]{1,0:T(8,128)(2,1)} %collective-permute-done.17.refs_22_), channel_id=1, source_target_pairs={{4,0},{8,12},{5,1},{9,13},{6,2},{10,14},{7,3},{11,15},{20,16},{24,... | collective-permute-start | bytes 3538952 | tf_op jit(solution)/shard_map/ppermute | solution.py:269
  172.4 47.8 %collective-permute-start.44 = (bf16[192,3072]{1,0:T(8,128)(2,1)S(1)}, bf16[192,3072]{1,0:T(8,128)(2,1)}, u32[]{:S(2)}, u32[]{:S(2)}) collective-permute-start(bf16[192,3072]{1,0:T(8,128)(2,1)S(1)} %copy-done.17), channel_id=1, source_target_pairs={{0,16},{16,0},{1,17},{17,1},{2,18},{18,2},{3,19},{19,3},{4,20},{20... | collective-permute-start | bytes 3538952 | tf_op jit(solution)/shard_map/ppermute | solution.py:276
  219.1 24.7 %copy-start.24 = (bf16[192,3072]{1,0:T(8,128)(2,1)}, bf16[192,3072]{1,0:T(8,128)(2,1)S(1)}, u32[]{:S(2)}) copy-start(bf16[192,3072]{1,0:T(8,128)(2,1)S(1)} %collective-permute-done.39.refs_6_) | copy-start | bytes 3538948
  219.1 25.8 %collective-permute-start.41 = (bf16[192,3072]{1,0:T(8,128)(2,1)}, bf16[192,3072]{1,0:T(8,128)(2,1)S(1)}, u32[]{:S(2)}, u32[]{:S(2)}) collective-permute-start(bf16[192,3072]{1,0:T(8,128)(2,1)} %collective-permute-done.15.refs_8_), channel_id=1, source_target_pairs={{0,1},{1,0},{2,3},{3,2},{4,5},{5,4},{6,7},{7,6},{8,9},{9,8},{10,11... | collective-permute-start | bytes 3538952 | tf_op jit(solution)/shard_map/ppermute | solution.py:277
  219.2 26.9 %collective-permute-start.40 = (bf16[192,3072]{1,0:T(8,128)(2,1)S(1)}, bf16[192,3072]{1,0:T(8,128)(2,1)}, u32[]{:S(2)}, u32[]{:S(2)}) collective-permute-start(bf16[192,3072]{1,0:T(8,128)(2,1)S(1)} %copy-done.17), channel_id=1, source_target_pairs={{0,1},{1,0},{2,3},{3,2},{4,5},{5,4},{6,7},{7,6},{8,9},{9,8},{10,11... | collective-permute-start | bytes 3538952 | tf_op jit(solution)/shard_map/ppermute | solution.py:277
  219.7 27.3 %collective-permute-start.42 = (bf16[192,3072]{1,0:T(8,128)(2,1)S(1)}, bf16[192,3072]{1,0:T(8,128)(2,1)}, u32[]{:S(2)}, u32[]{:S(2)}) collective-permute-start(bf16[192,3072]{1,0:T(8,128)(2,1)S(1)} %copy-done.19), channel_id=1, source_target_pairs={{0,1},{1,0},{2,3},{3,2},{4,5},{5,4},{6,7},{7,6},{8,9},{9,8},{10,11... | collective-permute-start | bytes 3538952 | tf_op jit(solution)/shard_map/ppermute | solution.py:277
  219.8 28.6 %collective-permute-start.45 = (bf16[192,3072]{1,0:T(8,128)(2,1)}, bf16[192,3072]{1,0:T(8,128)(2,1)}, u32[]{:S(2)}, u32[]{:S(2)}) collective-permute-start(bf16[192,3072]{1,0:T(8,128)(2,1)} %collective-permute-done.43.refs_12_), channel_id=1, source_target_pairs={{0,1},{1,0},{2,3},{3,2},{4,5},{5,4},{6,7},{7,6},{8,9},{9,8},{10,11... | collective-permute-start | bytes 3538952 | tf_op jit(solution)/shard_map/ppermute | solution.py:277
  220.7 28.9 %collective-permute-start.46 = (bf16[192,3072]{1,0:T(8,128)(2,1)}, bf16[192,3072]{1,0:T(8,128)(2,1)}, u32[]{:S(2)}, u32[]{:S(2)}) collective-permute-start(bf16[192,3072]{1,0:T(8,128)(2,1)} %collective-permute-done.44.refs_13_), channel_id=1, source_target_pairs={{0,1},{1,0},{2,3},{3,2},{4,5},{5,4},{6,7},{7,6},{8,9},{9,8},{10,11... | collective-permute-start | bytes 3538952 | tf_op jit(solution)/shard_map/ppermute | solution.py:277
  244.8 27.7 %collective-permute-start.26 = (bf16[384,128]{1,0:T(8,128)(2,1)S(1)}, bf16[384,128]{1,0:T(8,128)(2,1)S(1)}, u32[]{:S(2)}, u32[]{:S(2)}) collective-permute-start(bf16[384,128]{1,0:T(8,128)(2,1)S(1)} %get-tuple-element.158), channel_id=1, source_target_pairs={{0,2},{2,0},{16,18},{18,16},{1,3},{3,1},{17,19},{19,17},{4,6},{6,4... | collective-permute-start | bytes 294920 | tf_op jit(solution)/shard_map/ppermute | solution.py:338
  246.0 28.1 %collective-permute-start.27 = (bf16[384,128]{1,0:T(8,128)(2,1)S(1)}, bf16[384,128]{1,0:T(8,128)(2,1)S(1)}, u32[]{:S(2)}, u32[]{:S(2)}) collective-permute-start(bf16[384,128]{1,0:T(8,128)(2,1)S(1)} %get-tuple-element.157), channel_id=1, source_target_pairs={{0,16},{2,18},{16,0},{18,2},{1,17},{3,19},{17,1},{19,3},{4,20},{6,... | collective-permute-start | bytes 294920 | tf_op jit(solution)/shard_map/ppermute | solution.py:338
  247.0 28.3 %collective-permute-start.28 = (bf16[384,128]{1,0:T(8,128)(2,1)S(1)}, bf16[384,128]{1,0:T(8,128)(2,1)S(1)}, u32[]{:S(2)}, u32[]{:S(2)}) collective-permute-start(bf16[384,128]{1,0:T(8,128)(2,1)S(1)} %get-tuple-element.156), channel_id=1, source_target_pairs={{0,18},{2,16},{16,2},{18,0},{1,19},{3,17},{17,3},{19,1},{4,22},{6,... | collective-permute-start | bytes 294920 | tf_op jit(solution)/shard_map/ppermute | solution.py:338
  248.4 28.8 %collective-permute-start.29 = (bf16[384,128]{1,0:T(8,128)(2,1)S(1)}, bf16[384,128]{1,0:T(8,128)(2,1)S(1)}, u32[]{:S(2)}, u32[]{:S(2)}) collective-permute-start(bf16[384,128]{1,0:T(8,128)(2,1)S(1)} %get-tuple-element.154), channel_id=1, source_target_pairs={{0,2},{2,0},{16,18},{18,16},{1,3},{3,1},{17,19},{19,17},{4,6},{6,4... | collective-permute-start | bytes 294920 | tf_op jit(solution)/shard_map/ppermute | solution.py:338
  249.5 29.2 %collective-permute-start.30 = (bf16[384,128]{1,0:T(8,128)(2,1)S(1)}, bf16[384,128]{1,0:T(8,128)(2,1)S(1)}, u32[]{:S(2)}, u32[]{:S(2)}) collective-permute-start(bf16[384,128]{1,0:T(8,128)(2,1)S(1)} %get-tuple-element.153), channel_id=1, source_target_pairs={{0,16},{2,18},{16,0},{18,2},{1,17},{3,19},{17,1},{19,3},{4,20},{6,... | collective-permute-start | bytes 294920 | tf_op jit(solution)/shard_map/ppermute | solution.py:338
  272.6 7.4 %collective-permute-start.31 = (bf16[384,128]{1,0:T(8,128)(2,1)S(1)}, bf16[384,128]{1,0:T(8,128)(2,1)S(1)}, u32[]{:S(2)}, u32[]{:S(2)}) collective-permute-start(bf16[384,128]{1,0:T(8,128)(2,1)S(1)} %get-tuple-element.152), channel_id=1, source_target_pairs={{0,18},{2,16},{16,2},{18,0},{1,19},{3,17},{17,3},{19,1},{4,22},{6,... | collective-permute-start | bytes 294920 | tf_op jit(solution)/shard_map/ppermute | solution.py:338
  274.1 7.2 %collective-permute-start.34 = (bf16[384,128]{1,0:T(8,128)(2,1)S(1)}, bf16[384,128]{1,0:T(8,128)(2,1)S(1)}, u32[]{:S(2)}, u32[]{:S(2)}) collective-permute-start(bf16[384,128]{1,0:T(8,128)(2,1)S(1)} %get-tuple-element.150), channel_id=1, source_target_pairs={{0,2},{2,0},{16,18},{18,16},{1,3},{3,1},{17,19},{19,17},{4,6},{6,4... | collective-permute-start | bytes 294920 | tf_op jit(solution)/shard_map/ppermute | solution.py:338
  275.2 7.4 %collective-permute-start.35 = (bf16[384,128]{1,0:T(8,128)(2,1)S(1)}, bf16[384,128]{1,0:T(8,128)(2,1)S(1)}, u32[]{:S(2)}, u32[]{:S(2)}) collective-permute-start(bf16[384,128]{1,0:T(8,128)(2,1)S(1)} %get-tuple-element.149), channel_id=1, source_target_pairs={{0,16},{2,18},{16,0},{18,2},{1,17},{3,19},{17,1},{19,3},{4,20},{6,... | collective-permute-start | bytes 294920 | tf_op jit(solution)/shard_map/ppermute | solution.py:338
  277.2 6.8 %collective-permute-start.36 = (bf16[384,128]{1,0:T(8,128)(2,1)S(1)}, bf16[384,128]{1,0:T(8,128)(2,1)S(1)}, u32[]{:S(2)}, u32[]{:S(2)}) collective-permute-start(bf16[384,128]{1,0:T(8,128)(2,1)S(1)} %get-tuple-element.148), channel_id=1, source_target_pairs={{0,18},{2,16},{16,2},{18,0},{1,19},{3,17},{17,3},{19,1},{4,22},{6,... | collective-permute-start | bytes 294920 | tf_op jit(solution)/shard_map/ppermute | solution.py:338
  278.8 12.8 %collective-permute-start.47 = (bf16[384,128]{1,0:T(8,128)(2,1)S(1)}, bf16[384,128]{1,0:T(8,128)(2,1)S(1)}, u32[]{:S(2)}, u32[]{:S(2)}) collective-permute-start(bf16[384,128]{1,0:T(8,128)(2,1)S(1)} %get-tuple-element.147), channel_id=1, source_target_pairs={{4,0},{6,2},{8,12},{10,14},{20,16},{22,18},{24,28},{26,30},{5,1},{... | collective-permute-start | bytes 294920 | tf_op jit(solution)/shard_map/ppermute | solution.py:356
  280.1 13.7 %collective-permute-start.48 = (bf16[384,128]{1,0:T(8,128)(2,1)S(1)}, bf16[384,128]{1,0:T(8,128)(2,1)S(1)}, u32[]{:S(2)}, u32[]{:S(2)}) collective-permute-start(bf16[384,128]{1,0:T(8,128)(2,1)S(1)} %get-tuple-element.146), channel_id=1, source_target_pairs={{4,2},{6,0},{8,14},{10,12},{20,18},{22,16},{24,30},{26,28},{5,3},{... | collective-permute-start | bytes 294920 | tf_op jit(solution)/shard_map/ppermute | solution.py:356
  281.4 13.6 %collective-permute-start.49 = (bf16[384,128]{1,0:T(8,128)(2,1)S(1)}, bf16[384,128]{1,0:T(8,128)(2,1)S(1)}, u32[]{:S(2)}, u32[]{:S(2)}) collective-permute-start(bf16[384,128]{1,0:T(8,128)(2,1)S(1)} %get-tuple-element.145), channel_id=1, source_target_pairs={{4,16},{6,18},{8,28},{10,30},{20,0},{22,2},{24,12},{26,14},{5,17},... | collective-permute-start | bytes 294920 | tf_op jit(solution)/shard_map/ppermute | solution.py:356
  282.7 13.4 %collective-permute-start.50 = (bf16[384,128]{1,0:T(8,128)(2,1)S(1)}, bf16[384,128]{1,0:T(8,128)(2,1)S(1)}, u32[]{:S(2)}, u32[]{:S(2)}) collective-permute-start(bf16[384,128]{1,0:T(8,128)(2,1)S(1)} %get-tuple-element.144), channel_id=1, source_target_pairs={{4,18},{6,16},{8,30},{10,28},{20,2},{22,0},{24,14},{26,12},{5,19},... | collective-permute-start | bytes 294920 | tf_op jit(solution)/shard_map/ppermute | solution.py:356
  (15 other events, 94.5 us)

commit v4 on v0

--- a/solution.py
+++ b/solution.py
@@ -1,8 +1,11 @@
+import functools
 import math
 
 import jax
 import jax.numpy as jnp
 from jax import lax
+from jax.experimental import pallas as pl
+from jax.experimental.pallas import tpu as pltpu
 from jax.sharding import PartitionSpec as P
 
 
@@ -28,7 +31,7 @@
     return mixed.astype(jnp.bfloat16).reshape(projected.shape[0], -1)
 
 
-def per_device(tokens, ln_gain, qkv_weight):
+def plain(tokens, ln_gain, qkv_weight):
     images = tokens.shape[0]
     width = tokens.shape[2]
     heads_here = qkv_weight.shape[1]
@@ -52,6 +55,399 @@
     return lax.all_to_all(mixed, "seq", split_axis=1, concat_axis=2, tiled=True)
 
 
+def normalize_kernel(place_ref, tokens_ref, gain_ref, *normed_refs):
+    widened = tokens_ref[0].astype(jnp.float32)
+    mean = jnp.mean(widened, axis=-1, keepdims=True)
+    centered = widened - mean
+    scale = lax.rsqrt(jnp.mean(centered * centered, axis=-1, keepdims=True) + 1e-06)
+    slab = widened.shape[1] // 4
+    span = normed_refs[0].shape[1]
+    for i in range(4):
+        columns = pl.ds(pl.multiple_of(place_ref[i + 1] * slab, 128), slab)
+        part = (tokens_ref[0, :, columns].astype(jnp.float32) - mean) * scale * gain_ref[:, columns]
+        begin = i * slab % span
+        normed_refs[i * slab // span][:, begin : begin + slab] = part.astype(jnp.bfloat16)
+
+
+def normalize_part(tokens, ln_gain, part, core, order):
+    width = tokens.shape[2]
+    step, count = 32, 2
+    steps = part // step
+    place = jnp.stack([jnp.asarray(v, jnp.int32) for v in (core, *order)])
+    return pl.pallas_call(
+        normalize_kernel,
+        out_shape=[jax.ShapeDtypeStruct((part, width // count), jnp.bfloat16)] * count,
+        grid_spec=pltpu.PrefetchScalarGridSpec(
+            num_scalar_prefetch=1,
+            grid=(steps,),
+            in_specs=[
+                pl.BlockSpec((1, step, width), lambda i, place: (0, place[0] * steps + i, 0)),
+                pl.BlockSpec((1, width), lambda i, place: (0, 0)),
+            ],
+            out_specs=[pl.BlockSpec((step, width // count), lambda i, place: (i, 0))] * count,
+        ),
+        compiler_params=pltpu.CompilerParams(vmem_limit_bytes=56 << 20),
+        cost_estimate=pl.CostEstimate(
+            flops=8 * part * width, bytes_accessed=4 * part * width, transcendentals=part
+        ),
+    )(place, tokens, ln_gain[None])
+
+
+def attend_rows(projected_ref, mixed_ref, base):
+    tokens, columns = projected_ref.shape
+    width = columns // 3
+    step = 256
+    key_rows = projected_ref[:, width : 2 * width]
+    value_rows = projected_ref[:, 2 * width :]
+    for begin in range(0, tokens, step):
+        queries = projected_ref[begin : begin + step, :width]
+        scores = lax.dot_general(
+            queries, key_rows, (((1,), (1,)), ((), ())), preferred_element_type=jnp.float32
+        )
+        highest = jnp.max(scores, axis=-1, keepdims=True)
+        expo = jnp.exp2((scores - highest) * (math.log2(math.e) / math.sqrt(width)))
+        mixed = jnp.dot(expo.astype(jnp.bfloat16), value_rows, preferred_element_type=jnp.float32)
+        mixed = mixed / jnp.sum(expo, axis=-1, keepdims=True)
+        mixed_ref[base + begin : base + begin + step, :] = mixed.astype(jnp.bfloat16)
+
+
+def job_kernel(layout, slots, counts, same, columns, finished, role_ref, *refs):
+    refs = list(refs)
+    take = lambda n: [refs.pop(0) for _ in range(n)]
+    images, jobs = len(layout), counts[0]
+    pieces = [[[take(2) for _ in range(n)] for n in places] for places in layout]
+    weights = [[take(1) * 2 if alike else take(2) for alike in row] for row in same]
+    partials = [None if at is None else take(1)[0] for at in columns]
+    outs = take(jobs)
+    features_ref, weight_ref, total_ref, projected_ref, token_sems, weight_sems, sum_sems = take(7)
+    core, inner = role_ref[0], role_ref[1]
+    span = pieces[0][0][0][0].shape[1]
+    slab = span // 2
+    tokens, wide = projected_ref.shape
+    part = tokens // 4
+
+    def features(image, n):
+        return features_ref.at[pl.ds(image * tokens, tokens), pl.ds(n * slab, slab)]
+
+    def weight(n, j):
+        return weight_ref.at[pl.ds(n * slab, slab), pl.ds(j * wide, wide)]
+
+    def total(image, j):
+        return total_ref.at[pl.ds(image * tokens, tokens), pl.ds(j * wide, wide)]
+
+    def start_tokens(image, n):
+        cut, begin = slots[n] // 2, slots[n] % 2 * slab
+        for place in range(2):
+            split = layout[image][place]
+            for owner in range(split):
+                row = image * tokens + 2 * place * part
+                if split == 2:
+                    row += (1 - core if owner else core) * part
+                rows = pl.ds(pl.multiple_of(row, 32), 2 * part // split)
+                pltpu.make_async_copy(
+                    pieces[image][place][owner][cut].at[:, pl.ds(begin, slab)],
+                    features_ref.at[rows, pl.ds(n * slab, slab)],
+                    token_sems.at[image, n],
+                ).start()
+
+    def start_weight(n, j, role):
+        source = weights[n][j][role]
+        if source.shape[0] == slab:
+            pltpu.make_async_copy(source, weight(n, j), weight_sems.at[n, j]).start()
+            return
+        for b in range(source.shape[1] // wide):
+            pltpu.make_async_copy(
+                source.at[:, pl.ds(b * wide, wide)],
+                weight_ref.at[pl.ds(n * slab + b * part, part), pl.ds(j * wide, wide)],
+                weight_sems.at[n, j],
+            ).start()
+
+    def start_weights(n):
+        for j in range(counts[n]):
+            if same[n][j]:
+                start_weight(n, j, 0)
+                continue
+
+            @pl.when(inner == 1)
+            def _():
+                start_weight(n, j, 0)
+
+            @pl.when(inner != 1)
+            def _():
+                start_weight(n, j, 1)
+
+    def partial_copy(image, j):
+        source = partials[j].at[pl.ds(image * tokens, tokens), pl.ds(columns[j], wide)]
+        return pltpu.make_async_copy(source, total(image, j), sum_sems.at[image, j])
+
+    for n in range(len(slots)):
+        start_tokens(0, n)
+        start_weights(n)
+    for image in range(images):
+        for j in range(jobs):
+            if columns[j] is not None:
+                partial_copy(image, j).start()
+        if image:
+            for n in range(len(slots)):
+                start_tokens(image, n)
+
+    for image in range(images):
+        for n in range(len(slots)):
+            pltpu.make_async_copy(
+                features(image, n), features(image, n), token_sems.at[image, n]
+            ).wait()
+            if image == 0:
+                for j in range(counts[n]):
+                    pltpu.make_async_copy(weight(n, j), weight(n, j), weight_sems.at[n, j]).wait()
+            term = jnp.dot(
+                features(image, n)[...],
+                weight_ref[n * slab : (n + 1) * slab, : counts[n] * wide],
+                preferred_element_type=jnp.float32,
+            )
+            for j in range(counts[n]):
+                value = term[:, j * wide : (j + 1) * wide]
+                if n == 0 and columns[j] is not None:
+                    partial_copy(image, j).wait()
+                if n or columns[j] is not None:
+                    value += total(image, j)[...]
+                if n + 1 < len(slots) and j < counts[n + 1]:
+                    total(image, j)[...] = value
+                elif j < finished:
+                    projected_ref[...] = value.astype(jnp.bfloat16)
+                    attend_rows(projected_ref, outs[j], image * tokens)
+                else:
+                    outs[j][image * tokens : (image + 1) * tokens, :] = value
+
+
+def run_jobs(core, inner, wide, images, slots, weights, partials=None, finished=0):
+    layout = [[len(place) for place in image] for image in images]
+    operands = [x for image in images for place in image for owner in place for x in owner]
+    span = operands[0].shape[1]
+    slab = span // 2
+    tokens = sum(owner[0].shape[0] for place in images[0] for owner in place)
+    total = len(images) * tokens
+    counts = [len(row) for row in weights]
+    jobs = counts[0]
+    same = [[not isinstance(w, tuple) for w in row] for row in weights]
+    for row in weights:
+        for w in row:
+            operands += list(w) if isinstance(w, tuple) else [w]
+    partials = partials or [None] * jobs
+    columns = [p and p[1] for p in partials]
+    operands += [p[0] for p in partials if p]
+    vmem = pl.BlockSpec(memory_space=pltpu.VMEM)
+    depth = len(slots) * slab
+    return pl.pallas_call(
+        functools.partial(job_kernel, layout, slots, counts, same, columns, finished),
+        out_shape=[
+            jax.ShapeDtypeStruct((total, wide // 3), jnp.bfloat16)
+            if j < finished
+            else jax.ShapeDtypeStruct((total, wide), jnp.float32)
+            for j in range(jobs)
+        ],
+        in_specs=[pl.BlockSpec(memory_space=pltpu.SMEM)]
+        + [pl.BlockSpec(memory_space=pl.ANY)] * len(operands),
+        out_specs=[vmem] * jobs,
+        scratch_shapes=[
+            pltpu.VMEM((total, depth), jnp.bfloat16),
+            pltpu.VMEM((depth, jobs * wide), jnp.bfloat16),
+            pltpu.VMEM((total, jobs * wide), jnp.float32),
+            pltpu.VMEM((tokens, wide), jnp.bfloat16),
+            pltpu.SemaphoreType.DMA((len(images), len(slots))),
+            pltpu.SemaphoreType.DMA((len(slots), jobs)),
+            pltpu.SemaphoreType.DMA((len(images), jobs)),
+        ],
+        compiler_params=pltpu.CompilerParams(vmem_limit_bytes=56 << 20),
+        cost_estimate=pl.CostEstimate(
+            flops=2 * total * slab * wide * sum(counts), bytes_accessed=0, transcendentals=0
+        ),
+    )(jnp.stack([core, inner]).astype(jnp.int32), *operands)
+
+
+def shared(tokens, ln_gain, qkv_weight):
+    groups, planes, seqs, cores = (lax.axis_size(a) for a in ("groups", "dp", "seq", "head"))
+    group, plane, seq, core = (lax.axis_index(a) for a in ("groups", "dp", "seq", "head"))
+    _, rows, _ = tokens.shape
+    slab, heads, columns = qkv_weight.shape
+    heads, part = heads // groups, rows // cores
+    inner = (plane == 1) | (plane == 2)
+    wait = lax.optimization_barrier
+
+    def fold(piece):
+        piece = piece.reshape(-1, part, columns).transpose(1, 0, 2)
+        return piece.reshape(part, -1)
+
+    def weight_piece(weight, j):
+        return lax.dynamic_slice_in_dim(weight, group * heads + j, 1, 1)[:, 0]
+
+    def pick(for_inner, for_ends):
+        return jnp.where(inner, for_inner, for_ends)
+
+    def pair(value):
+        return lax.ppermute(value, "dp", [(0, 1), (1, 0), (2, 3), (3, 2)])
+
+    def outward(value):
+        return lax.ppermute(value, "dp", [(1, 0), (2, 3)])
+
+    def middle(value):
+        return lax.ppermute(value, "dp", [(1, 2), (2, 1)])
+
+    swap = [(0, 1), (1, 0)]
+    beside = lambda value: lax.ppermute(value, "seq", swap)
+    across = lambda value: lax.ppermute(value, "groups", swap)
+
+    def others(*values):
+        got = []
+        for value in values:
+            if got:
+                value, got[-1] = wait((value, got[-1]))
+            got.append(lax.ppermute(value, "head", swap))
+        return got
+
+    beside_plane, far_inner = plane ^ 1, 2 - plane // 2
+    order = (
+        plane,
+        pick(beside_plane, far_inner),
+        pick(far_inner, beside_plane),
+        3 - 3 * (plane // 2),
+    )
+    run = functools.partial(run_jobs, core, inner, columns)
+
+    def exchange(mixed):
+        got = []
+        for a in range(groups):
+            for b in range(seqs):
+                sent = mixed[(a * seqs + b) * rows : (a * seqs + b + 1) * rows]
+                if a or b:
+                    steps = [
+                        (g * seqs + s, (g + a) % groups * seqs + (s + b) % seqs)
+                        for g in range(groups)
+                        for s in range(seqs)
+                    ]
+                    sent = lax.ppermute(sent, ("groups", "seq"), steps)
+                got.append(sent)
+        return got
+
+    own0 = weight_piece(qkv_weight, 0)
+    pair1, middle1 = pair(own0), middle(own0)
+    tokens, own0 = wait((tokens, own0))
+    normed = normalize_part(tokens, ln_gain, part, core, order)
+    normed, qkv_weight = wait((normed, qkv_weight))
+    cut0, cut1 = normed
+    beside1, across1 = beside(cut0), across(cut0)
+    own1, own2 = weight_piece(qkv_weight, 1), weight_piece(qkv_weight, 2)
+    pair1, middle1, beside1, across1, own1, own2, cut0, cut1, tokens = wait(
+        (pair1, middle1, beside1, across1, own1, own2, cut0, cut1, tokens)
+    )
+
+    pair2, middle2 = pair(pick(fold(middle1), cut0)), middle(own1)
+    beside2, across2 = beside(cut1), across(cut1)
+    far_normed = normalize_part(tokens, ln_gain, part, 1 - core, order)
+    far1 = others(beside1, across1)
+    pair2, middle2, beside2, across2, across1, cut1, own2, far_normed, far1 = wait(
+        (pair2, middle2, beside2, across2, across1, cut1, own2, far_normed, far1)
+    )
+
+    pair3, middle3 = pair(pick(fold(own1), cut1)), middle(own2)
+    beside3, across3 = beside(across1), across(beside2)
+    far2 = others(beside2, across2)
+    pair3, middle3, beside3, across3, middle2, pair1, pair2, far2 = wait(
+        (pair3, middle3, beside3, across3, middle2, pair1, pair2, far2)
+    )
+
+    pair4, middle4 = pair(pick(middle2, own1)), middle(pair1)
+    beside4, across4 = beside(pair2), across(pair2)
+    far3 = others(beside3, across3)
+    images = [
+        ((normed, far_normed), ((beside1, beside2), (far1[0], far2[0]))),
+        (((across1, across2), (far1[1], far2[1])), ((beside3, across3), far3)),
+    ]
+    sums = run(
+        images,
+        (0, 2),
+        [[own0, (own1, own0), (own2, own1)], [middle1, (middle2, pair1), (middle3, pair3)]],
+    )
+    pair4, middle4, beside4, across4, own2, pair3, sums = wait(
+        (pair4, middle4, beside4, across4, own2, pair3, sums)
+    )
+
+    pair5, middle5 = pair(pick(middle4, own2)), middle(pair4)
+    beside5, across5 = beside(pair3), across(pair3)
+    (mixed1,) = run(images, (1, 3), [[pair1], [middle4]], [(sums[0], 0)], 1)
+    far_lent = others(pair2, pair3, beside4, across4)
+    pair5, middle5, beside5, across5, across4, mixed1, far_lent = wait(
+        (pair5, middle5, beside5, across5, across4, mixed1, far_lent)
+    )
+
+    pair6, middle6 = outward(middle5), middle(pair5)
+    beside6, across6 = beside(across4), across(beside5)
+    far5 = others(beside5, across5)
+    mixed2, sum3 = run(
+        images,
+        (1, 3),
+        [[(pair4, pair2), (pair5, pair4)], [(middle5, pair5)]],
+        [(sums[1], 0), (sums[2], 0)],
+        1,
+    )
+    early = exchange(jnp.concatenate([mixed1, mixed2], axis=1))
+    lent0 = [
+        (((pair2, pair3), far_lent[:2]), ((beside4, beside5), (far_lent[2], far5[0])))
+    ]
+    (sum4,) = run(lent0, (0, 1, 2), [[pair5], [middle3], [own2]])
+    pair6, middle6, beside6, across6, sum3, sum4, far5 = wait(
+        (pair6, middle6, beside6, across6, sum3, sum4, far5)
+    )
+
+    far6 = [lax.ppermute(value, "head", swap) for value in (beside6, across6)]
+    (mixed3,) = run(images, (3,), [[(middle6, pair6)]], [(sum3, 0)], 1)
+    late = exchange(mixed3)
+    (mixed4,) = run(lent0, (3,), [[middle6]], [(sum4, 0)], 1)
+    lent1 = [
+        (((across4, across5), (far_lent[3], far5[1])), ((beside6, across6), far6))
+    ]
+    (mixed5,) = run(lent1, (0, 1, 2, 3), [[pair5], [middle3], [own2], [middle6]], None, 1)
+
+    def hand_back(mixed):
+        got = []
+        for a in range(groups):
+            for b in range(seqs):
+                steps = [
+                    (
+                        (g * planes + z) * seqs + s,
+                        ((g + a) % groups * planes + (z ^ 1)) * seqs + (s + b) % seqs,
+                    )
+                    for g in range(groups)
+                    for z in (1, 2)
+                    for s in range(seqs)
+                ]
+                sent = mixed[a][b * rows : (b + 1) * rows]
+                got.append(lax.ppermute(sent, ("groups", "dp", "seq"), steps))
+        return got
+
+    early, late, back = wait((early, late, hand_back((mixed4, mixed5))))
+    received = jnp.stack([
+        pick(jnp.concatenate([x, y], axis=1), jnp.concatenate([x[:, x.shape[1] // 2 :], y, z], axis=1))
+        for x, y, z in zip(early, late, back)
+    ])
+    blocks = []
+    for s in range(seqs):
+        for g in range(groups):
+            index = (group - g) % groups * seqs + (seq - s) % seqs
+            blocks.append(lax.dynamic_index_in_dim(received, index, 0, keepdims=False))
+    return jnp.concatenate(blocks, axis=1)[None]
+
+
+def per_device(tokens, ln_gain, qkv_weight):
+    groups, planes, seqs, cores = (lax.axis_size(a) for a in ("groups", "dp", "seq", "head"))
+    images, rows, width = tokens.shape
+    slab, heads, _ = qkv_weight.shape
+    if (groups, planes, seqs, cores) == (2, 4, 2, 2) and images == 1 and heads == 3 * groups:
+        part = rows // cores
+        if rows % (32 * cores) == 0 and slab % part == 0 and 2 * slab == qkv_weight.shape[2] * slab // part:
+            return shared(tokens, ln_gain, qkv_weight)
+    return plain(tokens, ln_gain, qkv_weight)
+
+
 def solution(mesh):
     return jax.shard_map(
         per_device,

time: 680 us -> 278 us (0.41)
  waiting for transfers between devices: 557 us -> 99.2 us
  Pallas kernels: 0 us -> 103 us
  starting transfers between devices: 0.26 us -> 48.8 us
  matrix products: 45.2 us -> 0 us
  blocking collectives: 18 us -> 0 us
  other arithmetic: 20.4 us -> 7.31 us
  between operations: 13.2 us -> 0.9 us
  local copies, waits for them, and re-layouts: 25.6 us -> 14.9 us
    all_gather x3 -> x0, waiting for transfers between devices: 557 us -> none  [the longest x1 479 us: per_device(): piece = lax.all_gather(qkv_weight, 'dp', axis=0, tiled=True)]
    pallas_call x0 -> x9, Pallas kernels: none -> 103 us  [the longest x7 89.5 us: run_jobs(): pl.pallas_call(functools.partial(job_kernel, layout, slots, counts, same,...]
    ppermute x0 -> x48, waiting for transfers between devices: none -> 99.2 us  [the longest x5 68.9 us: pair(): return lax.ppermute(value, 'dp', [(0, 1), (1, 0), (2, 3), (3, 2)])]
    ppermute x0 -> x48, starting transfers between devices: none -> 48.8 us  [the longest x5 13.3 us: pair(): return lax.ppermute(value, 'dp', [(0, 1), (1, 0), (2, 3), (3, 2)])]
    dot_general x2 -> x0, matrix products: 37.1 us -> none  [the longest x1 29.9 us: per_device(): jnp.dot(features, piece.reshape(piece.shape[0], columns), preferred_eleme...]
    all_to_all x1 -> x0, blocking collectives: 18 us -> none  [per_device(): return lax.all_to_all(mixed, 'seq', split_axis=1, concat_axis=2, tiled=True)]
    unnamed x9 -> x55, local copies, waits for them, and re-layouts: 13 us -> 2.57 us
    sub x1 -> x0, matrix products: 8.18 us -> none  [attend(): expo = jnp.exp(scores - highest)]
  transfers between devices with their start and end apart: 3 -> 48, of which waited for: 3 -> 17; matrix products, arithmetic and copies ran while one was open for 2% -> 7% of each run, Pallas kernels for 0% -> 37%
where the time goes in v4:
time: 278 us; the launch traced here: 274 us
  Pallas kernels  103 us (37%)
  waiting for transfers between devices  99.2 us (36%)
  starting transfers between devices  48.8 us (18%)
  local copies, waits for them, and re-layouts  14.9 us (5%)
  other arithmetic  7.31 us (3%)
    pallas_call x7, Pallas kernels, run_jobs(): pl.pallas_call(functools.partial(job_kernel, layout, slots, counts, same,...  89.5 us
    ppermute x5, waiting for transfers between devices, pair(): return lax.ppermute(value, 'dp', [(0, 1), (1, 0), (2, 3), (3, 2)])  68.9 us
    ppermute x5, starting transfers between devices, pair(): return lax.ppermute(value, 'dp', [(0, 1), (1, 0), (2, 3), (3, 2)])  13.3 us
    pallas_call x2, Pallas kernels, normalize_part(): pl.pallas_call(normalize_kernel, out_shape=[jax.ShapeDtypeStruct((part, w...  13.1 us
    ppermute x6, waiting for transfers between devices, shared(): across = lambda value: lax.ppermute(value, 'groups', swap)  12 us
    ppermute x6, starting transfers between devices, middle(): return lax.ppermute(value, 'dp', [(1, 2), (2, 1)])  8.06 us
    ppermute x4, waiting for transfers between devices, hand_back(): got.append(lax.ppermute(sent, ('groups', 'dp', 'seq'), steps))  7.79 us
    ppermute x6, starting transfers between devices, exchange(): sent = lax.ppermute(sent, ('groups', 'seq'), steps)  7.11 us
  transfers between devices with their start and end apart: 48, of which 17 were waited for; matrix products, arithmetic and copies ran while one was open for 7% of the time, Pallas kernels for 37%

profile of v4, /device:TPU:0, one launch (start us, length us, event | category | flops | bytes accessed | tf_op | source)
XLA Modules:
  0.0 273.7 jit_solution(4406642493465036827)
XLA Ops:
  0.0 1.4 dynamic-slice_bitcast_fusion.2.refs_16_.refs_18_
  1.4 1.7 collective-permute-start.1
  3.1 4.9 %collective-permute-start = (bf16[1536,384]{1,0:T(8,128)(2,1)S(1)}, bf16[1536,384]{1,0:T(8,128)(2,1)}, u32[]{:S(2)}, u32[]{:S(2)}) collective-permute-start(bf16[1536,384]{1,0:T(8,128)(2,1)S(1)} %dynamic-slice_bitcast_fusion.2.refs_16_.refs_18_), channel_id=1, source_target_pairs={{0,4},{4,0},{8,12},{12,8},{1,5},{5,1},{9,13},{13,9},{2,6},{6,2},{1... | collective-permute-start | bytes 3538952 | tf_op jit(solution)/shard_map/ppermute | solution.py:287
  8.0 0.7 stack.30.place_ref
  8.6 6.5 %shard_map.37 = (bf16[192,3072]{1,0:T(8,128)(2,1)}, bf16[192,3072]{1,0:T(8,128)(2,1)}) custom-call(s32[5]{0:T(128)} %stack.30.place_ref, bf16[1,384,6144]{2,1,0:T(8,128)(2,1)} %tokens_ref.1, f32[1,6144]{1,0:T(1,128)} %bitcast.61), custom_call_target="tpu_custom_call" | custom-call | flops 9437184 | bytes 4718592 | tf_op jit(solution)/shard_map/pallas_call | solution.py:77
  15.2 1.5 collective-permute-start.3
  16.7 1.5 collective-permute-start.2
  18.2 3.0 %dynamic-slice_bitcast_fusion = (bf16[1536,384]{1,0:T(8,128)(2,1)S(1)}, bf16[1536,384]{1,0:T(8,128)(2,1)}) fusion(bf16[1536,6,384]{2,0,1:T(8,128)(2,1)} %param.5, s32[]{:T(128)S(6)} %select_n.140, s32[]{:T(128)S(6)} %select_n.139), kind=kLoop, calls=%fused_computation.2 | loop fusion | bytes 4718600 | tf_op jit(solution)/shard_map/squeeze | solution.py:281
  21.2 12.6 %collective-permute-done.refs_23_.refs_16_ = bf16[1536,384]{1,0:T(8,128)(2,1)} collective-permute-done((bf16[1536,384]{1,0:T(8,128)(2,1)S(1)}, bf16[1536,384]{1,0:T(8,128)(2,1)}, u32[]{:S(2)}, u32[]{:S(2)}) %collective-permute-start) | collective-permute-done | bytes 1179680 | tf_op jit(solution)/shard_map/ppermute | solution.py:287
  33.8 8.8 %collective-permute-done.3.refs_8_ = bf16[192,3072]{1,0:T(8,128)(2,1)} collective-permute-done((bf16[192,3072]{1,0:T(8,128)(2,1)}, bf16[192,3072]{1,0:T(8,128)(2,1)}, u32[]{:S(2)}, u32[]{:S(2)}) %collective-permute-start.3) | collective-permute-done | bytes 1179680 | tf_op jit(solution)/shard_map/ppermute | solution.py:297
  42.6 1.2 collective-permute-done.2.refs_4_
  44.4 1.5 collective-permute-start.6
  45.9 1.6 copy.7
  47.5 1.1 broadcast_select_fusion.1
  49.0 1.7 collective-permute-start.5
  50.6 0.6 stack.32.place_ref
  51.2 6.5 %shard_map.38 = (bf16[192,3072]{1,0:T(8,128)(2,1)}, bf16[192,3072]{1,0:T(8,128)(2,1)}) custom-call(s32[5]{0:T(128)} %stack.32.place_ref, bf16[1,384,6144]{2,1,0:T(8,128)(2,1)} %tokens_ref.1, f32[1,6144]{1,0:T(1,128)} %bitcast.62), custom_call_target="tpu_custom_call" | custom-call | flops 9437184 | bytes 4718592 | tf_op jit(solution)/shard_map/pallas_call | solution.py:77
  57.8 18.9 %collective-permute-done.4.refs_17_.refs_0_ = bf16[192,3072]{1,0:T(8,128)(2,1)S(1)} collective-permute-done((bf16[192,3072]{1,0:T(8,128)(2,1)}, bf16[192,3072]{1,0:T(8,128)(2,1)S(1)}, u32[]{:S(2)}, u32[]{:S(2)}) %collective-permute-start.4) | collective-permute-done | bytes 1179680 | tf_op jit(solution)/shard_map/ppermute | solution.py:287
  76.8 1.8 copy.6
  78.6 1.6 collective-permute-start.13
  80.3 3.4 %collective-permute-start.10 = (bf16[192,3072]{1,0:T(8,128)(2,1)S(1)}, bf16[192,3072]{1,0:T(8,128)(2,1)S(1)}, u32[]{:S(2)}, u32[]{:S(2)}) collective-permute-start(bf16[192,3072]{1,0:T(8,128)(2,1)S(1)} %broadcast_select_fusion), channel_id=1, source_target_pairs={{0,4},{4,0},{8,12},{12,8},{1,5},{5,1},{9,13},{13,9},{2,6},{6,2},{1... | collective-permute-start | bytes 3538952 | tf_op jit(solution)/shard_map/ppermute | solution.py:287
  83.7 0.7 collective-permute-start.11
  84.4 0.6 collective-permute-start.12
  85.0 25.0 %collective-permute-done.10.refs_25_.refs_1_ = bf16[192,3072]{1,0:T(8,128)(2,1)S(1)} collective-permute-done((bf16[192,3072]{1,0:T(8,128)(2,1)S(1)}, bf16[192,3072]{1,0:T(8,128)(2,1)S(1)}, u32[]{:S(2)}, u32[]{:S(2)}) %collective-permute-start.10) | collective-permute-done | bytes 1179680 | tf_op jit(solution)/shard_map/ppermute | solution.py:287
  110.1 2.5 collective-permute-done.12.refs_12_
  112.6 2.8 %collective-permute-done.20.refs_14_ = bf16[192,3072]{1,0:T(8,128)(2,1)S(1)} collective-permute-done((bf16[192,3072]{1,0:T(8,128)(2,1)S(1)}, bf16[192,3072]{1,0:T(8,128)(2,1)S(1)}, u32[]{:S(2)}, u32[]{:S(2)}) %collective-permute-start.20) | collective-permute-done | bytes 1179680 | tf_op jit(solution)/shard_map/ppermute | solution.py:304
  115.7 2.7 broadcast_select_fusion.3
  118.4 1.7 collective-permute-start.16
  120.1 1.9 collective-permute-start.17
  123.1 1.0 copy-done.12
  124.7 20.6 %shard_map.39 = (f32[1536,384]{1,0:T(8,128)}, f32[1536,384]{1,0:T(8,128)}, f32[1536,384]{1,0:T(8,128)}) custom-call(s32[2]{0:T(128)} %pad_add_fusion.role_ref, bf16[192,3072]{1,0:T(8,128)(2,1)} %get-tuple-element.108.refs_0_, bf16[192,3072]{1,0:T(8,128)(2,1)} %get-tuple-element.118.refs_1_, bf16[192,3072]{1,0:T(8,128)(2,1)} %get-tuple-element.132.refs_2_, ...), custom_call_target="tpu_custom_call" | custom-call | flops 10871635968 | tf_op jit(solution)/shard_map/pallas_call | solution.py:240
  145.3 1.5 collective-permute-done.16.refs_16_.refs_19_
  146.8 3.1 %collective-permute-done.19.refs_0_ = bf16[192,3072]{1,0:T(8,128)(2,1)} collective-permute-done((bf16[192,3072]{1,0:T(8,128)(2,1)S(1)}, bf16[192,3072]{1,0:T(8,128)(2,1)}, u32[]{:S(2)}, u32[]{:S(2)}) %collective-permute-start.19) | collective-permute-done | bytes 1179680 | tf_op jit(solution)/shard_map/ppermute | solution.py:297
  150.1 2.8 %collective-permute-done.27.refs_3_ = bf16[192,3072]{1,0:T(8,128)(2,1)S(1)} collective-permute-done((bf16[192,3072]{1,0:T(8,128)(2,1)S(1)}, bf16[192,3072]{1,0:T(8,128)(2,1)S(1)}, u32[]{:S(2)}, u32[]{:S(2)}) %collective-permute-start.27) | collective-permute-done | bytes 1179680 | tf_op jit(solution)/shard_map/ppermute | solution.py:304
  153.1 1.5 collective-permute-start.25
  155.1 1.2 broadcast_select_fusion.2
  156.3 3.1 %collective-permute-start.22 = (bf16[1536,384]{1,0:T(8,128)(2,1)}, bf16[1536,384]{1,0:T(8,128)(2,1)S(1)}, u32[]{:S(2)}, u32[]{:S(2)}) collective-permute-start(bf16[1536,384]{1,0:T(8,128)(2,1)} %broadcast_select_fusion.2), channel_id=1, source_target_pairs={{0,4},{4,0},{8,12},{12,8},{1,5},{5,1},{9,13},{13,9},{2,6},{6,2},{1... | collective-permute-start | bytes 3538952 | tf_op jit(solution)/shard_map/ppermute | solution.py:287
  159.4 0.9 collective-permute-start.23
  160.4 14.1 %shard_map.40 = bf16[1536,128]{1,0:T(8,128)(2,1)} custom-call(s32[2]{0:T(128)} %pad_add_fusion.role_ref, bf16[192,3072]{1,0:T(8,128)(2,1)} %get-tuple-element.108.refs_0_, bf16[192,3072]{1,0:T(8,128)(2,1)} %get-tuple-element.118.refs_1_, bf16[192,3072]{1,0:T(8,128)(2,1)} %get-tuple-element.132.refs_2_, bf16[192,3072]{1,0:T(8,128)(2,1)} %get-tuple-element.133.refs_3_, ...), custom_call_target="tpu_custom_call" | custom-call | flops 3623878656 | tf_op jit(solution)/shard_map/pallas_call | solution.py:240
  174.6 10.9 %collective-permute-done.22.refs_18_.refs_21_.refs_8_ = bf16[1536,384]{1,0:T(8,128)(2,1)S(1)} collective-permute-done((bf16[1536,384]{1,0:T(8,128)(2,1)}, bf16[1536,384]{1,0:T(8,128)(2,1)S(1)}, u32[]{:S(2)}, u32[]{:S(2)}) %collective-permute-start.22) | collective-permute-done | bytes 1179680 | tf_op jit(solution)/shard_map/ppermute | solution.py:287
  186.2 1.3 collective-permute-start.33
  187.5 1.6 collective-permute-start.35
  189.1 1.1 collective-permute-start.34
  190.3 1.4 constant_dynamic-update-slice_fusion.1
  191.7 17.8 %shard_map.41 = (bf16[1536,128]{1,0:T(8,128)(2,1)}, f32[1536,384]{1,0:T(8,128)}) custom-call(s32[2]{0:T(128)} %pad_add_fusion.role_ref, bf16[192,3072]{1,0:T(8,128)(2,1)} %get-tuple-element.108.refs_0_, bf16[192,3072]{1,0:T(8,128)(2,1)} %get-tuple-element.118.refs_1_, bf16[192,3072]{1,0:T(8,128)(2,1)} %get-tuple-element.132.refs_2_, ...), custom_call_target="tpu_custom_call" | custom-call | flops 5435817984 | tf_op jit(solution)/shard_map/pallas_call | solution.py:240
  209.5 8.6 %shard_map.42.refs_9_ = f32[768,384]{1,0:T(8,128)} custom-call(s32[2]{0:T(128)} %pad_add_fusion.role_ref, bf16[192,3072]{1,0:T(8,128)(2,1)} %copy-done.5, bf16[192,3072]{1,0:T(8,128)(2,1)} %copy-done.13, bf16[192,3072]{1,0:T(8,128)(2,1)} %collective-permute-done.26.refs_2_, bf16[192,3072]{1,0:T(8,128)(2,1)} %copy-done.16, bf16[192,3072]{1,0:T(8,128)(2,1)} %copy-done.15, ...), custom_call_target="tpu_custom_call" | custom-call | flops 2717908992 | tf_op jit(solution)/shard_map/pallas_call | solution.py:240
  218.7 1.1 constant_dynamic-update-slice_fusion
  219.9 1.9 collective-permute-start.32
  222.3 1.1 collective-permute-start.30
  223.5 6.6 %shard_map.44 = bf16[768,128]{1,0:T(8,128)(2,1)} custom-call(s32[2]{0:T(128)} %pad_add_fusion.role_ref, bf16[192,3072]{1,0:T(8,128)(2,1)} %copy-done.5, bf16[192,3072]{1,0:T(8,128)(2,1)} %copy-done.13, bf16[192,3072]{1,0:T(8,128)(2,1)} %collective-permute-done.26.refs_2_, bf16[192,3072]{1,0:T(8,128)(2,1)} %copy-done.16, bf16[192,3072]{1,0:T(8,128)(2,1)} %copy-done.15, ...), custom_call_target="tpu_custom_call" | custom-call | flops 905969664 | tf_op jit(solution)/shard_map/pallas_call | solution.py:240
  230.1 10.5 %shard_map.43 = bf16[1536,128]{1,0:T(8,128)(2,1)} custom-call(s32[2]{0:T(128)} %pad_add_fusion.role_ref, bf16[192,3072]{1,0:T(8,128)(2,1)} %get-tuple-element.108.refs_0_, bf16[192,3072]{1,0:T(8,128)(2,1)} %get-tuple-element.118.refs_1_, bf16[192,3072]{1,0:T(8,128)(2,1)} %get-tuple-element.132.refs_2_, bf16[192,3072]{1,0:T(8,128)(2,1)} %get-tuple-element.133.refs_3_, ...), custom_call_target="tpu_custom_call" | custom-call | flops 1811939328 | tf_op jit(solution)/shard_map/pallas_call | solution.py:240
  240.6 1.1 fusion.1
  241.7 1.3 collective-permute-start.43
  243.0 1.3 collective-permute-start.42
  244.3 11.4 %shard_map.45 = bf16[768,128]{1,0:T(8,128)(2,1)} custom-call(s32[2]{0:T(128)} %pad_add_fusion.role_ref, bf16[192,3072]{1,0:T(8,128)(2,1)} %collective-permute-done.19.refs_0_, bf16[192,3072]{1,0:T(8,128)(2,1)} %collective-permute-done.25.refs_1_, bf16[192,3072]{1,0:T(8,128)(2,1)} %copy-done.23, bf16[192,3072]{1,0:T(8,128)(2,1)} %collective-permute-done.38.refs_3_, ...), custom_call_target="tpu_custom_call" | custom-call | flops 3623878656 | tf_op jit(solution)/shard_map/pallas_call | solution.py:240
  255.7 1.0 fusion.2
  256.7 1.9 collective-permute-start.41
  259.1 1.1 collective-permute-start.39
  260.2 1.3 collective-permute-start.47
  261.5 1.3 collective-permute-start.46
  263.2 0.6 collective-permute-done.40
  263.9 6.7 %collective-permute-done.47 = bf16[384,128]{1,0:T(8,128)(2,1)S(1)} collective-permute-done((bf16[384,128]{1,0:T(8,128)(2,1)S(1)}, bf16[384,128]{1,0:T(8,128)(2,1)S(1)}, u32[]{:S(2)}, u32[]{:S(2)}) %collective-permute-start.47) | collective-permute-done | bytes 98336 | tf_op jit(solution)/shard_map/ppermute | solution.py:424
  270.6 1.1 collective-permute-done.46
  272.4 1.1 maximum_bitcast_fusion
  (121 shorter events, 7.6 us)
Async XLA Ops:
  1.4 13.8 %copy-start.22 = (bf16[1536,384]{1,0:T(8,128)(2,1)}, bf16[1536,384]{1,0:T(8,128)(2,1)S(1)}, u32[]{:S(2)}) copy-start(bf16[1536,384]{1,0:T(8,128)(2,1)S(1)} %dynamic-slice_bitcast_fusion.2.refs_16_.refs_18_) | copy-start | bytes 3538948
  1.4 19.8 %collective-permute-start.1 = (bf16[1536,384]{1,0:T(8,128)(2,1)S(1)}, bf16[1536,384]{1,0:T(8,128)(2,1)}, u32[]{:S(2)}, u32[]{:S(2)}) collective-permute-start(bf16[1536,384]{1,0:T(8,128)(2,1)S(1)} %dynamic-slice_bitcast_fusion.2.refs_16_.refs_18_), channel_id=1, source_target_pairs={{4,8},{8,4},{5,9},{9,5},{6,10},{10,6},{7,11},{11,7},{20,24},{24,20... | collective-permute-start | bytes 3538952 | tf_op jit(solution)/shard_map/ppermute | solution.py:293
  3.1 30.7 %collective-permute-start = (bf16[1536,384]{1,0:T(8,128)(2,1)S(1)}, bf16[1536,384]{1,0:T(8,128)(2,1)}, u32[]{:S(2)}, u32[]{:S(2)}) collective-permute-start(bf16[1536,384]{1,0:T(8,128)(2,1)S(1)} %dynamic-slice_bitcast_fusion.2.refs_16_.refs_18_), channel_id=1, source_target_pairs={{0,4},{4,0},{8,12},{12,8},{1,5},{5,1},{9,13},{13,9},{2,6},{6,2},{1... | collective-permute-start | bytes 3538952 | tf_op jit(solution)/shard_map/ppermute | solution.py:287
  15.2 27.5 %collective-permute-start.3 = (bf16[192,3072]{1,0:T(8,128)(2,1)}, bf16[192,3072]{1,0:T(8,128)(2,1)}, u32[]{:S(2)}, u32[]{:S(2)}) collective-permute-start(bf16[192,3072]{1,0:T(8,128)(2,1)} %get-tuple-element.108.refs_0_), channel_id=1, source_target_pairs={{0,16},{16,0},{1,17},{17,1},{2,18},{18,2},{3,19},{19,3},{4,20},{20... | collective-permute-start | bytes 3538952 | tf_op jit(solution)/shard_map/ppermute | solution.py:297
  16.7 27.2 %collective-permute-start.2 = (bf16[192,3072]{1,0:T(8,128)(2,1)}, bf16[192,3072]{1,0:T(8,128)(2,1)}, u32[]{:S(2)}, u32[]{:S(2)}) collective-permute-start(bf16[192,3072]{1,0:T(8,128)(2,1)} %get-tuple-element.108.refs_0_), channel_id=1, source_target_pairs={{0,2},{2,0},{1,3},{3,1},{4,6},{6,4},{5,7},{7,5},{8,10},{10,8},{9,1... | collective-permute-start | bytes 3538952 | tf_op jit(solution)/shard_map/ppermute | solution.py:296
  18.2 25.7 %copy-start.4 = (bf16[192,3072]{1,0:T(8,128)(2,1)S(1)}, bf16[192,3072]{1,0:T(8,128)(2,1)}, u32[]{:S(2)}) copy-start(bf16[192,3072]{1,0:T(8,128)(2,1)} %get-tuple-element.118.refs_1_) | copy-start | bytes 3538948
  21.2 62.5 %copy-start.1 = (bf16[1536,384]{1,0:T(8,128)(2,1)}, bf16[1536,384]{1,0:T(8,128)(2,1)S(1)}, u32[]{:S(2)}) copy-start(bf16[1536,384]{1,0:T(8,128)(2,1)S(1)} %get-tuple-element.148.refs_19_.refs_10_) | copy-start | bytes 3538948
  43.9 6.8 %collective-permute-start.8 = (bf16[192,3072]{1,0:T(8,128)(2,1)}, bf16[192,3072]{1,0:T(8,128)(2,1)}, u32[]{:S(2)}, u32[]{:S(2)}) collective-permute-start(bf16[192,3072]{1,0:T(8,128)(2,1)} %collective-permute-done.2.refs_4_), channel_id=1, source_target_pairs={{0,1},{1,0},{2,3},{3,2},{4,5},{5,4},{6,7},{7,6},{8,9},{9,8},{10,11... | collective-permute-start | bytes 3538952 | tf_op jit(solution)/shard_map/ppermute | solution.py:304
  43.9 32.8 %collective-permute-start.7 = (bf16[192,3072]{1,0:T(8,128)(2,1)S(1)}, bf16[192,3072]{1,0:T(8,128)(2,1)}, u32[]{:S(2)}, u32[]{:S(2)}) collective-permute-start(bf16[192,3072]{1,0:T(8,128)(2,1)S(1)} %copy-done.4), channel_id=1, source_target_pairs={{0,16},{16,0},{1,17},{17,1},{2,18},{18,2},{3,19},{19,3},{4,20},{20... | collective-permute-start | bytes 3538952 | tf_op jit(solution)/shard_map/ppermute | solution.py:297
  44.4 32.3 %collective-permute-start.6 = (bf16[192,3072]{1,0:T(8,128)(2,1)S(1)}, bf16[192,3072]{1,0:T(8,128)(2,1)}, u32[]{:S(2)}, u32[]{:S(2)}) collective-permute-start(bf16[192,3072]{1,0:T(8,128)(2,1)S(1)} %copy-done.4), channel_id=1, source_target_pairs={{0,2},{2,0},{1,3},{3,1},{4,6},{6,4},{5,7},{7,5},{8,10},{10,8},{9,1... | collective-permute-start | bytes 3538952 | tf_op jit(solution)/shard_map/ppermute | solution.py:296
  48.6 28.0 %collective-permute-start.4 = (bf16[192,3072]{1,0:T(8,128)(2,1)}, bf16[192,3072]{1,0:T(8,128)(2,1)S(1)}, u32[]{:S(2)}, u32[]{:S(2)}) collective-permute-start(bf16[192,3072]{1,0:T(8,128)(2,1)} %broadcast_select_fusion.1), channel_id=1, source_target_pairs={{0,4},{4,0},{8,12},{12,8},{1,5},{5,1},{9,13},{13,9},{2,6},{6,2},{1... | collective-permute-start | bytes 3538952 | tf_op jit(solution)/shard_map/ppermute | solution.py:287
  49.0 27.7 %collective-permute-start.5 = (bf16[1536,384]{1,0:T(8,128)(2,1)}, bf16[1536,384]{1,0:T(8,128)(2,1)}, u32[]{:S(2)}, u32[]{:S(2)}) collective-permute-start(bf16[1536,384]{1,0:T(8,128)(2,1)} %get-tuple-element.106.refs_17_.refs_20_), channel_id=1, source_target_pairs={{4,8},{8,4},{5,9},{9,5},{6,10},{10,6},{7,11},{11,7},{20,24},{24,20... | collective-permute-start | bytes 3538952 | tf_op jit(solution)/shard_map/ppermute | solution.py:293
  50.6 26.1 %collective-permute-start.9 = (bf16[192,3072]{1,0:T(8,128)(2,1)}, bf16[192,3072]{1,0:T(8,128)(2,1)}, u32[]{:S(2)}, u32[]{:S(2)}) collective-permute-start(bf16[192,3072]{1,0:T(8,128)(2,1)} %collective-permute-done.3.refs_8_), channel_id=1, source_target_pairs={{0,1},{1,0},{2,3},{3,2},{4,5},{5,4},{6,7},{7,6},{8,9},{9,8},{10,11... | collective-permute-start | bytes 3538952 | tf_op jit(solution)/shard_map/ppermute | solution.py:304
  76.7 46.4 %copy-start.5 = (bf16[192,3072]{1,0:T(8,128)(2,1)}, bf16[192,3072]{1,0:T(8,128)(2,1)S(1)}, u32[]{:S(2)}) copy-start(bf16[192,3072]{1,0:T(8,128)(2,1)S(1)} %collective-permute-done.4.refs_17_.refs_0_) | copy-start | bytes 3538948
  76.7 8.3 %collective-permute-start.14 = (bf16[192,3072]{1,0:T(8,128)(2,1)}, bf16[192,3072]{1,0:T(8,128)(2,1)S(1)}, u32[]{:S(2)}, u32[]{:S(2)}) collective-permute-start(bf16[192,3072]{1,0:T(8,128)(2,1)} %collective-permute-done.6.refs_5_), channel_id=1, source_target_pairs={{0,1},{1,0},{2,3},{3,2},{4,5},{5,4},{6,7},{7,6},{8,9},{9,8},{10,11... | collective-permute-start | bytes 3538952 | tf_op jit(solution)/shard_map/ppermute | solution.py:304
  78.6 33.9 %collective-permute-start.13 = (bf16[192,3072]{1,0:T(8,128)(2,1)}, bf16[192,3072]{1,0:T(8,128)(2,1)S(1)}, u32[]{:S(2)}, u32[]{:S(2)}) collective-permute-start(bf16[192,3072]{1,0:T(8,128)(2,1)} %collective-permute-done.6.refs_5_), channel_id=1, source_target_pairs={{0,16},{16,0},{1,17},{17,1},{2,18},{18,2},{3,19},{19,3},{4,20},{20... | collective-permute-start | bytes 3538952 | tf_op jit(solution)/shard_map/ppermute | solution.py:297
  80.3 29.7 %collective-permute-start.10 = (bf16[192,3072]{1,0:T(8,128)(2,1)S(1)}, bf16[192,3072]{1,0:T(8,128)(2,1)S(1)}, u32[]{:S(2)}, u32[]{:S(2)}) collective-permute-start(bf16[192,3072]{1,0:T(8,128)(2,1)S(1)} %broadcast_select_fusion), channel_id=1, source_target_pairs={{0,4},{4,0},{8,12},{12,8},{1,5},{5,1},{9,13},{13,9},{2,6},{6,2},{1... | collective-permute-start | bytes 3538952 | tf_op jit(solution)/shard_map/ppermute | solution.py:287
  83.7 26.4 %collective-permute-start.11 = (bf16[1536,384]{1,0:T(8,128)(2,1)S(1)}, bf16[1536,384]{1,0:T(8,128)(2,1)S(1)}, u32[]{:S(2)}, u32[]{:S(2)}) collective-permute-start(bf16[1536,384]{1,0:T(8,128)(2,1)S(1)} %get-tuple-element.148.refs_19_.refs_10_), channel_id=1, source_target_pairs={{4,8},{8,4},{5,9},{9,5},{6,10},{10,6},{7,11},{11,7},{20,24},{24,20... | collective-permute-start | bytes 3538952 | tf_op jit(solution)/shard_map/ppermute | solution.py:293
  84.4 28.1 %collective-permute-start.12 = (bf16[192,3072]{1,0:T(8,128)(2,1)}, bf16[192,3072]{1,0:T(8,128)(2,1)S(1)}, u32[]{:S(2)}, u32[]{:S(2)}) collective-permute-start(bf16[192,3072]{1,0:T(8,128)(2,1)} %collective-permute-done.3.refs_8_), channel_id=1, source_target_pairs={{0,2},{2,0},{1,3},{3,1},{4,6},{6,4},{5,7},{7,5},{8,10},{10,8},{9,1... | collective-permute-start | bytes 3538952 | tf_op jit(solution)/shard_map/ppermute | solution.py:296
  85.0 33.3 %copy-start.7 = (bf16[192,3072]{1,0:T(8,128)(2,1)}, bf16[192,3072]{1,0:T(8,128)(2,1)S(1)}, u32[]{:S(2)}) copy-start(bf16[192,3072]{1,0:T(8,128)(2,1)S(1)} %collective-permute-done.14.refs_7_) | copy-start | bytes 3538948
  85.0 27.5 %collective-permute-start.15 = (bf16[192,3072]{1,0:T(8,128)(2,1)}, bf16[192,3072]{1,0:T(8,128)(2,1)S(1)}, u32[]{:S(2)}, u32[]{:S(2)}) collective-permute-start(bf16[192,3072]{1,0:T(8,128)(2,1)} %collective-permute-done.7.refs_9_), channel_id=1, source_target_pairs={{0,1},{1,0},{2,3},{3,2},{4,5},{5,4},{6,7},{7,6},{8,9},{9,8},{10,11... | collective-permute-start | bytes 3538952 | tf_op jit(solution)/shard_map/ppermute | solution.py:304
  112.5 2.9 %collective-permute-start.20 = (bf16[192,3072]{1,0:T(8,128)(2,1)S(1)}, bf16[192,3072]{1,0:T(8,128)(2,1)S(1)}, u32[]{:S(2)}, u32[]{:S(2)}) collective-permute-start(bf16[192,3072]{1,0:T(8,128)(2,1)S(1)} %collective-permute-done.12.refs_12_), channel_id=1, source_target_pairs={{0,1},{1,0},{2,3},{3,2},{4,5},{5,4},{6,7},{7,6},{8,9},{9,8},{10,11... | collective-permute-start | bytes 3538952 | tf_op jit(solution)/shard_map/ppermute | solution.py:304
  115.5 9.2 %copy-start.11 = (bf16[192,3072]{1,0:T(8,128)(2,1)}, bf16[192,3072]{1,0:T(8,128)(2,1)S(1)}, u32[]{:S(2)}) copy-start(bf16[192,3072]{1,0:T(8,128)(2,1)S(1)} %collective-permute-done.20.refs_14_) | copy-start | bytes 3538948
  115.5 7.6 %collective-permute-start.21 = (bf16[192,3072]{1,0:T(8,128)(2,1)S(1)}, bf16[192,3072]{1,0:T(8,128)(2,1)S(1)}, u32[]{:S(2)}, u32[]{:S(2)}) collective-permute-start(bf16[192,3072]{1,0:T(8,128)(2,1)S(1)} %collective-permute-done.13.refs_13_), channel_id=1, source_target_pairs={{0,1},{1,0},{2,3},{3,2},{4,5},{5,4},{6,7},{7,6},{8,9},{9,8},{10,11... | collective-permute-start | bytes 3538952 | tf_op jit(solution)/shard_map/ppermute | solution.py:304
  118.4 28.4 %collective-permute-start.16 = (bf16[1536,384]{1,0:T(8,128)(2,1)}, bf16[1536,384]{1,0:T(8,128)(2,1)}, u32[]{:S(2)}, u32[]{:S(2)}) collective-permute-start(bf16[1536,384]{1,0:T(8,128)(2,1)} %broadcast_select_fusion.3), channel_id=1, source_target_pairs={{0,4},{4,0},{8,12},{12,8},{1,5},{5,1},{9,13},{13,9},{2,6},{6,2},{1... | collective-permute-start | bytes 3538952 | tf_op jit(solution)/shard_map/ppermute | solution.py:287
  120.1 26.7 %collective-permute-start.17 = (bf16[1536,384]{1,0:T(8,128)(2,1)}, bf16[1536,384]{1,0:T(8,128)(2,1)}, u32[]{:S(2)}, u32[]{:S(2)}) collective-permute-start(bf16[1536,384]{1,0:T(8,128)(2,1)} %collective-permute-done.refs_23_.refs_16_), channel_id=1, source_target_pairs={{4,8},{8,4},{5,9},{9,5},{6,10},{10,6},{7,11},{11,7},{20,24},{24,20... | collective-permute-start | bytes 3538952 | tf_op jit(solution)/shard_map/ppermute | solution.py:293
  122.0 27.9 %collective-permute-start.19 = (bf16[192,3072]{1,0:T(8,128)(2,1)S(1)}, bf16[192,3072]{1,0:T(8,128)(2,1)}, u32[]{:S(2)}, u32[]{:S(2)}) collective-permute-start(bf16[192,3072]{1,0:T(8,128)(2,1)S(1)} %collective-permute-done.4.refs_17_.refs_0_), channel_id=1, source_target_pairs={{0,16},{16,0},{1,17},{17,1},{2,18},{18,2},{3,19},{19,3},{4,20},{20... | collective-permute-start | bytes 3538952 | tf_op jit(solution)/shard_map/ppermute | solution.py:297
  122.5 27.5 %collective-permute-start.18 = (bf16[192,3072]{1,0:T(8,128)(2,1)S(1)}, bf16[192,3072]{1,0:T(8,128)(2,1)S(1)}, u32[]{:S(2)}, u32[]{:S(2)}) collective-permute-start(bf16[192,3072]{1,0:T(8,128)(2,1)S(1)} %collective-permute-done.4.refs_17_.refs_0_), channel_id=1, source_target_pairs={{0,2},{2,0},{1,3},{3,1},{4,6},{6,4},{5,7},{7,5},{8,10},{10,8},{9,1... | collective-permute-start | bytes 3538952 | tf_op jit(solution)/shard_map/ppermute | solution.py:296
  124.1 25.9 %collective-permute-start.26 = (bf16[192,3072]{1,0:T(8,128)(2,1)S(1)}, bf16[192,3072]{1,0:T(8,128)(2,1)}, u32[]{:S(2)}, u32[]{:S(2)}) collective-permute-start(bf16[192,3072]{1,0:T(8,128)(2,1)S(1)} %collective-permute-done.4.refs_17_.refs_0_), channel_id=1, source_target_pairs={{0,1},{1,0},{2,3},{3,2},{4,5},{5,4},{6,7},{7,6},{8,9},{9,8},{10,11... | collective-permute-start | bytes 3538952 | tf_op jit(solution)/shard_map/ppermute | solution.py:304
  124.7 25.3 %copy-start.14 = (bf16[192,3072]{1,0:T(8,128)(2,1)S(1)}, bf16[192,3072]{1,0:T(8,128)(2,1)}, u32[]{:S(2)}) copy-start(bf16[192,3072]{1,0:T(8,128)(2,1)} %copy-done.13) | copy-start | bytes 3538948
  124.7 30.5 %copy-start.2 = (bf16[1536,384]{1,0:T(8,128)(2,1)S(1)}, bf16[1536,384]{1,0:T(8,128)(2,1)}, u32[]{:S(2)}) copy-start(bf16[1536,384]{1,0:T(8,128)(2,1)} %copy-done.1) | copy-start | bytes 3538948
  150.0 6.3 %copy-start.15 = (bf16[192,3072]{1,0:T(8,128)(2,1)}, bf16[192,3072]{1,0:T(8,128)(2,1)S(1)}, u32[]{:S(2)}) copy-start(bf16[192,3072]{1,0:T(8,128)(2,1)S(1)} %collective-permute-done.18.refs_4_) | copy-start | bytes 3538948
  150.0 2.9 %collective-permute-start.27 = (bf16[192,3072]{1,0:T(8,128)(2,1)S(1)}, bf16[192,3072]{1,0:T(8,128)(2,1)S(1)}, u32[]{:S(2)}, u32[]{:S(2)}) collective-permute-start(bf16[192,3072]{1,0:T(8,128)(2,1)S(1)} %copy-done.14), channel_id=1, source_target_pairs={{0,1},{1,0},{2,3},{3,2},{4,5},{5,4},{6,7},{7,6},{8,9},{9,8},{10,11... | collective-permute-start | bytes 3538952 | tf_op jit(solution)/shard_map/ppermute | solution.py:304
  152.9 7.4 %collective-permute-start.28 = (bf16[192,3072]{1,0:T(8,128)(2,1)S(1)}, bf16[192,3072]{1,0:T(8,128)(2,1)S(1)}, u32[]{:S(2)}, u32[]{:S(2)}) collective-permute-start(bf16[192,3072]{1,0:T(8,128)(2,1)S(1)} %collective-permute-done.18.refs_4_), channel_id=1, source_target_pairs={{0,1},{1,0},{2,3},{3,2},{4,5},{5,4},{6,7},{7,6},{8,9},{9,8},{10,11... | collective-permute-start | bytes 3538952 | tf_op jit(solution)/shard_map/ppermute | solution.py:304
  153.1 32.5 %collective-permute-start.25 = (bf16[192,3072]{1,0:T(8,128)(2,1)S(1)}, bf16[192,3072]{1,0:T(8,128)(2,1)}, u32[]{:S(2)}, u32[]{:S(2)}) collective-permute-start(bf16[192,3072]{1,0:T(8,128)(2,1)S(1)} %copy-done.14), channel_id=1, source_target_pairs={{0,16},{16,0},{1,17},{17,1},{2,18},{18,2},{3,19},{19,3},{4,20},{20... | collective-permute-start | bytes 3538952 | tf_op jit(solution)/shard_map/ppermute | solution.py:297
  154.6 30.9 %collective-permute-start.24 = (bf16[192,3072]{1,0:T(8,128)(2,1)S(1)}, bf16[192,3072]{1,0:T(8,128)(2,1)S(1)}, u32[]{:S(2)}, u32[]{:S(2)}) collective-permute-start(bf16[192,3072]{1,0:T(8,128)(2,1)S(1)} %copy-done.14), channel_id=1, source_target_pairs={{0,2},{2,0},{1,3},{3,1},{4,6},{6,4},{5,7},{7,5},{8,10},{10,8},{9,1... | collective-permute-start | bytes 3538952 | tf_op jit(solution)/shard_map/ppermute | solution.py:296
  156.3 29.2 %collective-permute-start.22 = (bf16[1536,384]{1,0:T(8,128)(2,1)}, bf16[1536,384]{1,0:T(8,128)(2,1)S(1)}, u32[]{:S(2)}, u32[]{:S(2)}) collective-permute-start(bf16[1536,384]{1,0:T(8,128)(2,1)} %broadcast_select_fusion.2), channel_id=1, source_target_pairs={{0,4},{4,0},{8,12},{12,8},{1,5},{5,1},{9,13},{13,9},{2,6},{6,2},{1... | collective-permute-start | bytes 3538952 | tf_op jit(solution)/shard_map/ppermute | solution.py:287
  159.4 26.1 %collective-permute-start.23 = (bf16[1536,384]{1,0:T(8,128)(2,1)}, bf16[1536,384]{1,0:T(8,128)(2,1)S(1)}, u32[]{:S(2)}, u32[]{:S(2)}) collective-permute-start(bf16[1536,384]{1,0:T(8,128)(2,1)} %collective-permute-done.16.refs_16_.refs_19_), channel_id=1, source_target_pairs={{4,8},{8,4},{5,9},{9,5},{6,10},{10,6},{7,11},{11,7},{20,24},{24,20... | collective-permute-start | bytes 3538952 | tf_op jit(solution)/shard_map/ppermute | solution.py:293
  160.3 14.2 %copy-start.17 = (bf16[192,3072]{1,0:T(8,128)(2,1)}, bf16[192,3072]{1,0:T(8,128)(2,1)S(1)}, u32[]{:S(2)}) copy-start(bf16[192,3072]{1,0:T(8,128)(2,1)S(1)} %collective-permute-done.28.refs_6_) | copy-start | bytes 3538948
  160.4 25.2 %collective-permute-start.29 = (bf16[192,3072]{1,0:T(8,128)(2,1)}, bf16[192,3072]{1,0:T(8,128)(2,1)S(1)}, u32[]{:S(2)}, u32[]{:S(2)}) collective-permute-start(bf16[192,3072]{1,0:T(8,128)(2,1)} %collective-permute-done.19.refs_0_), channel_id=1, source_target_pairs={{0,1},{1,0},{2,3},{3,2},{4,5},{5,4},{6,7},{7,6},{8,9},{9,8},{10,11... | collective-permute-start | bytes 3538952 | tf_op jit(solution)/shard_map/ppermute | solution.py:304
  185.5 6.2 %copy-start = (bf16[1536,384]{1,0:T(8,128)(2,1)}, bf16[1536,384]{1,0:T(8,128)(2,1)S(1)}, u32[]{:S(2)}) copy-start(bf16[1536,384]{1,0:T(8,128)(2,1)S(1)} %collective-permute-done.22.refs_18_.refs_21_.refs_8_) | copy-start | bytes 3538948
  185.5 6.2 %copy-start.21 = (bf16[1536,384]{1,0:T(8,128)(2,1)}, bf16[1536,384]{1,0:T(8,128)(2,1)S(1)}, u32[]{:S(2)}) copy-start(bf16[1536,384]{1,0:T(8,128)(2,1)S(1)} %collective-permute-done.23.refs_20_) | copy-start | bytes 3538948
  185.6 23.9 %copy-start.18 = (bf16[192,3072]{1,0:T(8,128)(2,1)}, bf16[192,3072]{1,0:T(8,128)(2,1)S(1)}, u32[]{:S(2)}) copy-start(bf16[192,3072]{1,0:T(8,128)(2,1)S(1)} %collective-permute-done.24.refs_5_) | copy-start | bytes 3538948
  185.6 23.9 %copy-start.23 = (bf16[192,3072]{1,0:T(8,128)(2,1)}, bf16[192,3072]{1,0:T(8,128)(2,1)S(1)}, u32[]{:S(2)}) copy-start(bf16[192,3072]{1,0:T(8,128)(2,1)S(1)} %collective-permute-done.29.refs_2_) | copy-start | bytes 3538948
  185.6 4.6 %collective-permute-start.37 = (bf16[192,3072]{1,0:T(8,128)(2,1)S(1)}, bf16[192,3072]{1,0:T(8,128)(2,1)S(1)}, u32[]{:S(2)}, u32[]{:S(2)}) collective-permute-start(bf16[192,3072]{1,0:T(8,128)(2,1)S(1)} %collective-permute-done.24.refs_5_), channel_id=1, source_target_pairs={{0,1},{1,0},{2,3},{3,2},{4,5},{5,4},{6,7},{7,6},{8,9},{9,8},{10,11... | collective-permute-start | bytes 3538952 | tf_op jit(solution)/shard_map/ppermute | solution.py:304
  185.7 32.5 %collective-permute-start.36 = (bf16[192,3072]{1,0:T(8,128)(2,1)S(1)}, bf16[192,3072]{1,0:T(8,128)(2,1)}, u32[]{:S(2)}, u32[]{:S(2)}) collective-permute-start(bf16[192,3072]{1,0:T(8,128)(2,1)S(1)} %collective-permute-done.24.refs_5_), channel_id=1, source_target_pairs={{0,16},{16,0},{1,17},{17,1},{2,18},{18,2},{3,19},{19,3},{4,20},{20... | collective-permute-start | bytes 3538952 | tf_op jit(solution)/shard_map/ppermute | solution.py:297
  186.2 31.9 %collective-permute-start.33 = (bf16[1536,384]{1,0:T(8,128)(2,1)S(1)}, bf16[1536,384]{1,0:T(8,128)(2,1)}, u32[]{:S(2)}, u32[]{:S(2)}) collective-permute-start(bf16[1536,384]{1,0:T(8,128)(2,1)S(1)} %collective-permute-done.23.refs_20_), channel_id=1, source_target_pairs={{4,0},{8,12},{5,1},{9,13},{6,2},{10,14},{7,3},{11,15},{20,16},{24,... | collective-permute-start | bytes 3538952 | tf_op jit(solution)/shard_map/ppermute | solution.py:290
  187.5 30.6 %collective-permute-start.35 = (bf16[192,3072]{1,0:T(8,128)(2,1)}, bf16[192,3072]{1,0:T(8,128)(2,1)}, u32[]{:S(2)}, u32[]{:S(2)}) collective-permute-start(bf16[192,3072]{1,0:T(8,128)(2,1)} %collective-permute-done.19.refs_0_), channel_id=1, source_target_pairs={{0,2},{2,0},{1,3},{3,1},{4,6},{6,4},{5,7},{7,5},{8,10},{10,8},{9,1... | collective-permute-start | bytes 3538952 | tf_op jit(solution)/shard_map/ppermute | solution.py:296
  189.1 29.0 %collective-permute-start.34 = (bf16[1536,384]{1,0:T(8,128)(2,1)S(1)}, bf16[1536,384]{1,0:T(8,128)(2,1)S(1)}, u32[]{:S(2)}, u32[]{:S(2)}) collective-permute-start(bf16[1536,384]{1,0:T(8,128)(2,1)S(1)} %collective-permute-done.22.refs_18_.refs_21_.refs_8_), channel_id=1, source_target_pairs={{4,8},{8,4},{5,9},{9,5},{6,10},{10,6},{7,11},{11,7},{20,24},{24,20... | collective-permute-start | bytes 3538952 | tf_op jit(solution)/shard_map/ppermute | solution.py:293
  190.2 19.3 %copy-start.19 = (bf16[192,3072]{1,0:T(8,128)(2,1)}, bf16[192,3072]{1,0:T(8,128)(2,1)S(1)}, u32[]{:S(2)}) copy-start(bf16[192,3072]{1,0:T(8,128)(2,1)S(1)} %collective-permute-done.37.refs_7_) | copy-start | bytes 3538948
  190.2 27.9 %collective-permute-start.38 = (bf16[192,3072]{1,0:T(8,128)(2,1)}, bf16[192,3072]{1,0:T(8,128)(2,1)}, u32[]{:S(2)}, u32[]{:S(2)}) collective-permute-start(bf16[192,3072]{1,0:T(8,128)(2,1)} %collective-permute-done.25.refs_1_), channel_id=1, source_target_pairs={{0,1},{1,0},{2,3},{3,2},{4,5},{5,4},{6,7},{7,6},{8,9},{9,8},{10,11... | collective-permute-start | bytes 3538952 | tf_op jit(solution)/shard_map/ppermute | solution.py:304
  218.2 23.5 %collective-permute-start.44 = (bf16[192,3072]{1,0:T(8,128)(2,1)}, bf16[192,3072]{1,0:T(8,128)(2,1)S(1)}, u32[]{:S(2)}, u32[]{:S(2)}) collective-permute-start(bf16[192,3072]{1,0:T(8,128)(2,1)} %collective-permute-done.35.refs_4_), channel_id=1, source_target_pairs={{0,1},{1,0},{2,3},{3,2},{4,5},{5,4},{6,7},{7,6},{8,9},{9,8},{10,11... | collective-permute-start | bytes 3538952 | tf_op jit(solution)/shard_map/ppermute | solution.py:401
  218.4 24.6 %collective-permute-start.45 = (bf16[192,3072]{1,0:T(8,128)(2,1)}, bf16[192,3072]{1,0:T(8,128)(2,1)S(1)}, u32[]{:S(2)}, u32[]{:S(2)}) collective-permute-start(bf16[192,3072]{1,0:T(8,128)(2,1)} %collective-permute-done.36.refs_5_), channel_id=1, source_target_pairs={{0,1},{1,0},{2,3},{3,2},{4,5},{5,4},{6,7},{7,6},{8,9},{9,8},{10,11... | collective-permute-start | bytes 3538952 | tf_op jit(solution)/shard_map/ppermute | solution.py:401
  219.9 36.7 %collective-permute-start.32 = (bf16[384,256]{1,0:T(8,128)(2,1)S(1)}, bf16[384,256]{1,0:T(8,128)(2,1)S(1)}, u32[]{:S(2)}, u32[]{:S(2)}) collective-permute-start(bf16[384,256]{1,0:T(8,128)(2,1)S(1)} %get-tuple-element.201), channel_id=1, source_target_pairs={{0,18},{2,16},{16,2},{18,0},{1,19},{3,17},{17,3},{19,1},{4,22},{6,... | collective-permute-start | bytes 589832 | tf_op jit(solution)/shard_map/ppermute | solution.py:327
  221.8 36.8 %collective-permute-start.31 = (bf16[384,256]{1,0:T(8,128)(2,1)S(1)}, bf16[384,256]{1,0:T(8,128)(2,1)S(1)}, u32[]{:S(2)}, u32[]{:S(2)}) collective-permute-start(bf16[384,256]{1,0:T(8,128)(2,1)S(1)} %get-tuple-element.202), channel_id=1, source_target_pairs={{0,16},{2,18},{16,0},{18,2},{1,17},{3,19},{17,1},{19,3},{4,20},{6,... | collective-permute-start | bytes 589832 | tf_op jit(solution)/shard_map/ppermute | solution.py:327
  222.3 36.8 %collective-permute-start.30 = (bf16[384,256]{1,0:T(8,128)(2,1)S(1)}, bf16[384,256]{1,0:T(8,128)(2,1)S(1)}, u32[]{:S(2)}, u32[]{:S(2)}) collective-permute-start(bf16[384,256]{1,0:T(8,128)(2,1)S(1)} %get-tuple-element.203), channel_id=1, source_target_pairs={{0,2},{2,0},{16,18},{18,16},{1,3},{3,1},{17,19},{19,17},{4,6},{6,4... | collective-permute-start | bytes 589832 | tf_op jit(solution)/shard_map/ppermute | solution.py:327
  230.1 10.5 %copy-start.26 = (bf16[768,128]{1,0:T(8,128)(2,1)S(1)}, bf16[768,128]{1,0:T(8,128)(2,1)}, u32[]{:S(2)}) copy-start(bf16[768,128]{1,0:T(8,128)(2,1)} %shard_map.44) | copy-start | bytes 589828
  241.7 18.6 %collective-permute-start.43 = (bf16[384,128]{1,0:T(8,128)(2,1)S(1)}, bf16[384,128]{1,0:T(8,128)(2,1)S(1)}, u32[]{:S(2)}, u32[]{:S(2)}) collective-permute-start(bf16[384,128]{1,0:T(8,128)(2,1)S(1)} %get-tuple-element.211), channel_id=1, source_target_pairs={{4,2},{6,0},{8,14},{10,12},{20,18},{22,16},{24,30},{26,28},{5,3},{... | collective-permute-start | bytes 294920 | tf_op jit(solution)/shard_map/ppermute | solution.py:424
  243.0 18.5 %collective-permute-start.42 = (bf16[384,128]{1,0:T(8,128)(2,1)S(1)}, bf16[384,128]{1,0:T(8,128)(2,1)S(1)}, u32[]{:S(2)}, u32[]{:S(2)}) collective-permute-start(bf16[384,128]{1,0:T(8,128)(2,1)S(1)} %get-tuple-element.212), channel_id=1, source_target_pairs={{4,0},{6,2},{8,12},{10,14},{20,16},{22,18},{24,28},{26,30},{5,1},{... | collective-permute-start | bytes 294920 | tf_op jit(solution)/shard_map/ppermute | solution.py:424
  256.7 6.5 %collective-permute-start.41 = (bf16[384,128]{1,0:T(8,128)(2,1)S(1)}, bf16[384,128]{1,0:T(8,128)(2,1)S(1)}, u32[]{:S(2)}, u32[]{:S(2)}) collective-permute-start(bf16[384,128]{1,0:T(8,128)(2,1)S(1)} %get-tuple-element.205), channel_id=1, source_target_pairs={{0,18},{2,16},{16,2},{18,0},{1,19},{3,17},{17,3},{19,1},{4,22},{6,... | collective-permute-start | bytes 294920 | tf_op jit(solution)/shard_map/ppermute | solution.py:327
  258.6 5.2 %collective-permute-start.40 = (bf16[384,128]{1,0:T(8,128)(2,1)S(1)}, bf16[384,128]{1,0:T(8,128)(2,1)S(1)}, u32[]{:S(2)}, u32[]{:S(2)}) collective-permute-start(bf16[384,128]{1,0:T(8,128)(2,1)S(1)} %get-tuple-element.206), channel_id=1, source_target_pairs={{0,16},{2,18},{16,0},{18,2},{1,17},{3,19},{17,1},{19,3},{4,20},{6,... | collective-permute-start | bytes 294920 | tf_op jit(solution)/shard_map/ppermute | solution.py:327
  259.1 4.8 %collective-permute-start.39 = (bf16[384,128]{1,0:T(8,128)(2,1)S(1)}, bf16[384,128]{1,0:T(8,128)(2,1)S(1)}, u32[]{:S(2)}, u32[]{:S(2)}) collective-permute-start(bf16[384,128]{1,0:T(8,128)(2,1)S(1)} %get-tuple-element.207), channel_id=1, source_target_pairs={{0,2},{2,0},{16,18},{18,16},{1,3},{3,1},{17,19},{19,17},{4,6},{6,4... | collective-permute-start | bytes 294920 | tf_op jit(solution)/shard_map/ppermute | solution.py:327
  260.2 10.3 %collective-permute-start.47 = (bf16[384,128]{1,0:T(8,128)(2,1)S(1)}, bf16[384,128]{1,0:T(8,128)(2,1)S(1)}, u32[]{:S(2)}, u32[]{:S(2)}) collective-permute-start(bf16[384,128]{1,0:T(8,128)(2,1)S(1)} %get-tuple-element.209), channel_id=1, source_target_pairs={{4,18},{6,16},{8,30},{10,28},{20,2},{22,0},{24,14},{26,12},{5,19},... | collective-permute-start | bytes 294920 | tf_op jit(solution)/shard_map/ppermute | solution.py:424
  261.5 10.1 %collective-permute-start.46 = (bf16[384,128]{1,0:T(8,128)(2,1)S(1)}, bf16[384,128]{1,0:T(8,128)(2,1)S(1)}, u32[]{:S(2)}, u32[]{:S(2)}) collective-permute-start(bf16[384,128]{1,0:T(8,128)(2,1)S(1)} %get-tuple-element.210), channel_id=1, source_target_pairs={{4,16},{6,18},{8,28},{10,30},{20,0},{22,2},{24,12},{26,14},{5,17},... | collective-permute-start | bytes 294920 | tf_op jit(solution)/shard_map/ppermute | solution.py:424
  (11 other events, 37.2 us)

commit v5 on v4

--- a/solution.py
+++ b/solution.py
@@ -111,13 +111,14 @@
         mixed_ref[base + begin : base + begin + step, :] = mixed.astype(jnp.bfloat16)
 
 
-def job_kernel(layout, slots, counts, same, columns, finished, role_ref, *refs):
+def job_kernel(layout, slots, ranges, same, added, starts, finished, role_ref, *refs):
     refs = list(refs)
     take = lambda n: [refs.pop(0) for _ in range(n)]
-    images, jobs = len(layout), counts[0]
-    pieces = [[[take(2) for _ in range(n)] for n in places] for places in layout]
+    images, jobs = len(layout), len(added)
+    steps = range(len(slots))
+    pieces = [[[take(2) for _ in place] for place in image] for image in layout]
     weights = [[take(1) * 2 if alike else take(2) for alike in row] for row in same]
-    partials = [None if at is None else take(1)[0] for at in columns]
+    partials = [take(images) if has else None for has in added]
     outs = take(jobs)
     features_ref, weight_ref, total_ref, projected_ref, token_sems, weight_sems, sum_sems = take(7)
     core, inner = role_ref[0], role_ref[1]
@@ -138,20 +139,22 @@
     def start_tokens(image, n):
         cut, begin = slots[n] // 2, slots[n] % 2 * slab
         for place in range(2):
-            split = layout[image][place]
+            split = len(layout[image][place])
             for owner in range(split):
                 row = image * tokens + 2 * place * part
                 if split == 2:
                     row += (1 - core if owner else core) * part
-                rows = pl.ds(pl.multiple_of(row, 32), 2 * part // split)
+                count = 2 * part // split
+                from_rows = pl.ds(layout[image][place][owner][cut], count)
+                rows = pl.ds(pl.multiple_of(row, 32), count)
                 pltpu.make_async_copy(
-                    pieces[image][place][owner][cut].at[:, pl.ds(begin, slab)],
+                    pieces[image][place][owner][cut].at[from_rows, pl.ds(begin, slab)],
                     features_ref.at[rows, pl.ds(n * slab, slab)],
                     token_sems.at[image, n],
                 ).start()
 
     def start_weight(n, j, role):
-        source = weights[n][j][role]
+        source = weights[n][j - ranges[n][0]][role]
         if source.shape[0] == slab:
             pltpu.make_async_copy(source, weight(n, j), weight_sems.at[n, j]).start()
             return
@@ -163,8 +166,8 @@
             ).start()
 
     def start_weights(n):
-        for j in range(counts[n]):
-            if same[n][j]:
+        for j in range(*ranges[n]):
+            if same[n][j - ranges[n][0]]:
                 start_weight(n, j, 0)
                 continue
 
@@ -177,40 +180,42 @@
                 start_weight(n, j, 1)
 
     def partial_copy(image, j):
-        source = partials[j].at[pl.ds(image * tokens, tokens), pl.ds(columns[j], wide)]
+        source = partials[j][image].at[pl.ds(starts[j][image], tokens)]
         return pltpu.make_async_copy(source, total(image, j), sum_sems.at[image, j])
 
-    for n in range(len(slots)):
+    for n in steps:
         start_tokens(0, n)
         start_weights(n)
     for image in range(images):
         for j in range(jobs):
-            if columns[j] is not None:
+            if added[j]:
                 partial_copy(image, j).start()
         if image:
-            for n in range(len(slots)):
+            for n in steps:
                 start_tokens(image, n)
 
     for image in range(images):
-        for n in range(len(slots)):
+        for n in steps:
             pltpu.make_async_copy(
                 features(image, n), features(image, n), token_sems.at[image, n]
             ).wait()
+            low, high = ranges[n]
             if image == 0:
-                for j in range(counts[n]):
+                for j in range(low, high):
                     pltpu.make_async_copy(weight(n, j), weight(n, j), weight_sems.at[n, j]).wait()
             term = jnp.dot(
                 features(image, n)[...],
-                weight_ref[n * slab : (n + 1) * slab, : counts[n] * wide],
+                weight_ref[n * slab : (n + 1) * slab, low * wide : high * wide],
                 preferred_element_type=jnp.float32,
             )
-            for j in range(counts[n]):
-                value = term[:, j * wide : (j + 1) * wide]
-                if n == 0 and columns[j] is not None:
+            for j in range(low, high):
+                value = term[:, (j - low) * wide : (j - low + 1) * wide]
+                mine = [m for m in steps if ranges[m][0] <= j < ranges[m][1]]
+                if n == mine[0] and added[j]:
                     partial_copy(image, j).wait()
-                if n or columns[j] is not None:
+                if n != mine[0] or added[j]:
                     value += total(image, j)[...]
-                if n + 1 < len(slots) and j < counts[n + 1]:
+                if n != mine[-1]:
                     total(image, j)[...] = value
                 elif j < finished:
                     projected_ref[...] = value.astype(jnp.bfloat16)
@@ -219,26 +224,29 @@
                     outs[j][image * tokens : (image + 1) * tokens, :] = value
 
 
-def run_jobs(core, inner, wide, images, slots, weights, partials=None, finished=0):
-    layout = [[len(place) for place in image] for image in images]
-    operands = [x for image in images for place in image for owner in place for x in owner]
+def run_jobs(core, inner, tokens, wide, images, weights, partials, finished=0):
+    images = [
+        [[[x if isinstance(x, tuple) else (x, 0) for x in owner] for owner in place] for place in image]
+        for image in images
+    ]
+    layout = [[[[row for _, row in owner] for owner in place] for place in image] for image in images]
+    operands = [x for image in images for place in image for owner in place for x, _ in owner]
     span = operands[0].shape[1]
     slab = span // 2
-    tokens = sum(owner[0].shape[0] for place in images[0] for owner in place)
-    total = len(images) * tokens
-    counts = [len(row) for row in weights]
-    jobs = counts[0]
-    same = [[not isinstance(w, tuple) for w in row] for row in weights]
-    for row in weights:
+    total, jobs = len(images) * tokens, len(partials)
+    slots = [slot for slot, _, _ in weights]
+    ranges = [(first, first + len(row)) for _, first, row in weights]
+    same = [[not isinstance(w, tuple) for w in row] for _, _, row in weights]
+    for _, _, row in weights:
         for w in row:
             operands += list(w) if isinstance(w, tuple) else [w]
-    partials = partials or [None] * jobs
-    columns = [p and p[1] for p in partials]
-    operands += [p[0] for p in partials if p]
+    added = [p is not None for p in partials]
+    starts = [p and [row for _, row in p] for p in partials]
+    operands += [x for p in partials if p is not None for x, _ in p]
     vmem = pl.BlockSpec(memory_space=pltpu.VMEM)
     depth = len(slots) * slab
     return pl.pallas_call(
-        functools.partial(job_kernel, layout, slots, counts, same, columns, finished),
+        functools.partial(job_kernel, layout, slots, ranges, same, added, starts, finished),
         out_shape=[
             jax.ShapeDtypeStruct((total, wide // 3), jnp.bfloat16)
             if j < finished
@@ -259,7 +267,9 @@
         ],
         compiler_params=pltpu.CompilerParams(vmem_limit_bytes=56 << 20),
         cost_estimate=pl.CostEstimate(
-            flops=2 * total * slab * wide * sum(counts), bytes_accessed=0, transcendentals=0
+            flops=2 * total * slab * wide * sum(len(row) for row in same),
+            bytes_accessed=0,
+            transcendentals=0,
         ),
     )(jnp.stack([core, inner]).astype(jnp.int32), *operands)
 
@@ -311,7 +321,7 @@
         pick(far_inner, beside_plane),
         3 - 3 * (plane // 2),
     )
-    run = functools.partial(run_jobs, core, inner, columns)
+    run = functools.partial(run_jobs, core, inner, seqs * rows, columns)
 
     def exchange(mixed):
         got = []
@@ -336,76 +346,106 @@
     cut0, cut1 = normed
     beside1, across1 = beside(cut0), across(cut0)
     own1, own2 = weight_piece(qkv_weight, 1), weight_piece(qkv_weight, 2)
-    pair1, middle1, beside1, across1, own1, own2, cut0, cut1, tokens = wait(
-        (pair1, middle1, beside1, across1, own1, own2, cut0, cut1, tokens)
-    )
-
-    pair2, middle2 = pair(pick(fold(middle1), cut0)), middle(own1)
+    give = pick(fold(own1), cut0)
+    pair1, middle1, beside1, across1, own1, own2, cut0, cut1, tokens, give = wait(
+        (pair1, middle1, beside1, across1, own1, own2, cut0, cut1, tokens, give)
+    )
+
+    pair2, middle2 = pair(give), middle(pair1)
     beside2, across2 = beside(cut1), across(cut1)
+    give = pick(fold(middle1), cut1)
     far_normed = normalize_part(tokens, ln_gain, part, 1 - core, order)
     far1 = others(beside1, across1)
-    pair2, middle2, beside2, across2, across1, cut1, own2, far_normed, far1 = wait(
-        (pair2, middle2, beside2, across2, across1, cut1, own2, far_normed, far1)
-    )
-
-    pair3, middle3 = pair(pick(fold(own1), cut1)), middle(own2)
+    pair2, middle2, beside2, across2, across1, own1, own2, far_normed, far1, give = wait(
+        (pair2, middle2, beside2, across2, across1, own1, own2, far_normed, far1, give)
+    )
+
+    pair3, middle3 = pair(give), middle(own1)
     beside3, across3 = beside(across1), across(beside2)
+    give = pick(middle2, own1)
     far2 = others(beside2, across2)
-    pair3, middle3, beside3, across3, middle2, pair1, pair2, far2 = wait(
-        (pair3, middle3, beside3, across3, middle2, pair1, pair2, far2)
-    )
-
-    pair4, middle4 = pair(pick(middle2, own1)), middle(pair1)
+    pair3, middle3, beside3, across3, pair1, pair2, own2, far2, give = wait(
+        (pair3, middle3, beside3, across3, pair1, pair2, own2, far2, give)
+    )
+
+    pair4, middle4 = pair(give), middle(own2)
     beside4, across4 = beside(pair2), across(pair2)
+    give = pick(middle3, own2)
+    image0 = ((normed, far_normed), ((beside1, beside2), (far1[0], far2[0])))
+    owns = [own0, (own1, own0), (own2, own1)]
+    mixed10, sum20, sum30 = run(
+        [image0],
+        [(0, 0, owns), (2, 0, [middle1, (middle3, pair1)]), (1, 0, [pair1]), (3, 0, [middle2])],
+        [None] * 3,
+        1,
+    )
     far3 = others(beside3, across3)
-    images = [
-        ((normed, far_normed), ((beside1, beside2), (far1[0], far2[0]))),
-        (((across1, across2), (far1[1], far2[1])), ((beside3, across3), far3)),
-    ]
-    sums = run(
-        images,
-        (0, 2),
-        [[own0, (own1, own0), (own2, own1)], [middle1, (middle2, pair1), (middle3, pair3)]],
-    )
-    pair4, middle4, beside4, across4, own2, pair3, sums = wait(
-        (pair4, middle4, beside4, across4, own2, pair3, sums)
-    )
-
-    pair5, middle5 = pair(pick(middle4, own2)), middle(pair4)
+    lent = jnp.concatenate([pair2, pair3])
+    pair4, middle4, beside4, across4, own2, pair3, lent, mixed10, sum20, sum30, far3, give = wait(
+        (pair4, middle4, beside4, across4, own2, pair3, lent, mixed10, sum20, sum30, far3, give)
+    )
+
+    pair5, middle5 = pair(give), middle(pair4)
     beside5, across5 = beside(pair3), across(pair3)
-    (mixed1,) = run(images, (1, 3), [[pair1], [middle4]], [(sums[0], 0)], 1)
-    far_lent = others(pair2, pair3, beside4, across4)
-    pair5, middle5, beside5, across5, across4, mixed1, far_lent = wait(
-        (pair5, middle5, beside5, across5, across4, mixed1, far_lent)
+    image1 = (((across1, across2), (far1[1], far2[1])), ((beside3, across3), far3))
+    over, near = (middle4, pair2), (pair4, pair3)
+    mixed11, sum21, sum31 = run(
+        [image1],
+        [
+            (0, 0, owns),
+            (2, 0, [middle1, (middle3, pair1), over]),
+            (1, 0, [pair1, near]),
+            (3, 0, [middle2]),
+        ],
+        [None] * 3,
+        1,
+    )
+    sum20, sum30 = run([image0], [(2, 1, [over]), (1, 0, [near])], [[(sum20, 0)], [(sum30, 0)]])
+    far_lent, far4 = others(lent, beside4)
+    pair5, middle5, beside5, across5, across4, mixed11, sum20, sum21, sum30, sum31, far_lent, far4 = wait(
+        (
+            *(pair5, middle5, beside5, across5, across4, mixed11),
+            *(sum20, sum21, sum30, sum31, far_lent, far4),
+        )
     )
 
     pair6, middle6 = outward(middle5), middle(pair5)
     beside6, across6 = beside(across4), across(beside5)
-    far5 = others(beside5, across5)
+    far5, far_across4 = others(beside5, across4)
     mixed2, sum3 = run(
-        images,
-        (1, 3),
-        [[(pair4, pair2), (pair5, pair4)], [(middle5, pair5)]],
-        [(sums[1], 0), (sums[2], 0)],
+        [image0, image1],
+        [(3, 0, [(middle5, pair4)]), (1, 1, [pair5])],
+        [[(sum20, 0), (sum21, 0)], [(sum30, 0), (sum31, 0)]],
         1,
     )
-    early = exchange(jnp.concatenate([mixed1, mixed2], axis=1))
-    lent0 = [
-        (((pair2, pair3), far_lent[:2]), ((beside4, beside5), (far_lent[2], far5[0])))
+    lent0 = (((pair2, pair3), (far_lent, (far_lent, part))), ((beside4, beside5), (far4, far5)))
+    lent_weights = [(0, 0, [pair5]), (1, 0, [middle4]), (2, 0, [own2])]
+    (sum4,) = run([lent0], lent_weights, [None])
+    pair6, middle6, beside6, across6, across5, mixed2, sum3, sum4, far_across4 = wait(
+        (pair6, middle6, beside6, across6, across5, mixed2, sum3, sum4, far_across4)
+    )
+
+    far_across5, *far6 = [
+        lax.ppermute(value, "head", swap) for value in (across5, beside6, across6)
     ]
-    (sum4,) = run(lent0, (0, 1, 2), [[pair5], [middle3], [own2]])
-    pair6, middle6, beside6, across6, sum3, sum4, far5 = wait(
-        (pair6, middle6, beside6, across6, sum3, sum4, far5)
-    )
-
-    far6 = [lax.ppermute(value, "head", swap) for value in (beside6, across6)]
-    (mixed3,) = run(images, (3,), [[(middle6, pair6)]], [(sum3, 0)], 1)
-    late = exchange(mixed3)
-    (mixed4,) = run(lent0, (3,), [[middle6]], [(sum4, 0)], 1)
-    lent1 = [
-        (((across4, across5), (far_lent[3], far5[1])), ((beside6, across6), far6))
-    ]
-    (mixed5,) = run(lent1, (0, 1, 2, 3), [[pair5], [middle3], [own2], [middle6]], None, 1)
+    (mixed3,) = run(
+        [image0, image1, lent0],
+        [(3, 0, [(middle6, pair6)])],
+        [[(sum3, 0), (sum3, seqs * rows), (sum4, 0)]],
+        1,
+    )
+    sent = exchange(
+        jnp.concatenate(
+            [
+                jnp.concatenate([mixed10, mixed11]),
+                mixed2,
+                mixed3[: mixed2.shape[0]],
+            ],
+            axis=1,
+        )
+    )
+    lent1 = (((across4, across5), (far_across4, far_across5)), ((beside6, across6), far6))
+    (mixed4,) = run([lent1], [*lent_weights, (3, 0, [middle6])], [None], 1)
 
     def hand_back(mixed):
         got = []
@@ -424,10 +464,10 @@
                 got.append(lax.ppermute(sent, ("groups", "dp", "seq"), steps))
         return got
 
-    early, late, back = wait((early, late, hand_back((mixed4, mixed5))))
+    back = hand_back((mixed3[mixed2.shape[0] :], mixed4))
     received = jnp.stack([
-        pick(jnp.concatenate([x, y], axis=1), jnp.concatenate([x[:, x.shape[1] // 2 :], y, z], axis=1))
-        for x, y, z in zip(early, late, back)
+        pick(x, jnp.concatenate([x[:, x.shape[1] // heads :], y], axis=1))
+        for x, y in zip(*wait((sent, back)))
     ])
     blocks = []
     for s in range(seqs):

time: 278 us -> 265 us (0.953)
  waiting for transfers between devices: 99.2 us -> 76.8 us
  Pallas kernels: 103 us -> 108 us
    ppermute x5, waiting for transfers between devices: 68.9 us -> 45.5 us  [pair(): return lax.ppermute(value, 'dp', [(0, 1), (1, 0), (2, 3), (3, 2)])]
    ppermute x6, waiting for transfers between devices: 3.83 us -> 18 us  [shared(): beside = lambda value: lax.ppermute(value, 'seq', swap)]
    ppermute x6, waiting for transfers between devices: 12 us -> 1.48 us  [shared(): across = lambda value: lax.ppermute(value, 'groups', swap)]
    ppermute x12 -> x10, waiting for transfers between devices: 5.69 us -> 0.03 us  [others(): got.append(lax.ppermute(value, 'head', swap))]
    pallas_call x7, Pallas kernels: 89.5 us -> 94.8 us  [run_jobs(): pl.pallas_call(functools.partial(job_kernel, layout, slots, ranges, same,...]
    ppermute x6 -> x3, starting transfers between devices: 7.11 us -> 3.55 us  [exchange(): sent = lax.ppermute(sent, ('groups', 'seq'), steps)]
    ppermute x5, starting transfers between devices: 13.3 us -> 16.3 us  [pair(): return lax.ppermute(value, 'dp', [(0, 1), (1, 0), (2, 3), (3, 2)])]
  transfers between devices with their start and end apart: 48 -> 44, of which waited for: 17 -> 11; matrix products, arithmetic and copies ran while one was open for 7% -> 5% of each run, Pallas kernels for 37% -> 39%
where the time goes in v5:
time: 265 us; the launch traced here: 261 us
  Pallas kernels  108 us (41%)
  waiting for transfers between devices  76.8 us (29%)
  starting transfers between devices  50.5 us (19%)
  local copies, waits for them, and re-layouts  16.8 us (6%)
  other arithmetic  7.66 us (3%)
    pallas_call x7, Pallas kernels, run_jobs(): pl.pallas_call(functools.partial(job_kernel, layout, slots, ranges, same,...  94.8 us
    ppermute x5, waiting for transfers between devices, pair(): return lax.ppermute(value, 'dp', [(0, 1), (1, 0), (2, 3), (3, 2)])  45.5 us
    ppermute x6, waiting for transfers between devices, shared(): beside = lambda value: lax.ppermute(value, 'seq', swap)  18 us
    ppermute x5, starting transfers between devices, pair(): return lax.ppermute(value, 'dp', [(0, 1), (1, 0), (2, 3), (3, 2)])  16.3 us
    pallas_call x2, Pallas kernels, normalize_part(): pl.pallas_call(normalize_kernel, out_shape=[jax.ShapeDtypeStruct((part, w...  13.1 us
    ppermute x4, waiting for transfers between devices, hand_back(): got.append(lax.ppermute(sent, ('groups', 'dp', 'seq'), steps))  10.2 us
    ppermute x6, starting transfers between devices, shared(): beside = lambda value: lax.ppermute(value, 'seq', swap)  8.67 us
    ppermute x6, starting transfers between devices, middle(): return lax.ppermute(value, 'dp', [(1, 2), (2, 1)])  8.11 us
  transfers between devices with their start and end apart: 44, of which 11 were waited for; matrix products, arithmetic and copies ran while one was open for 5% of the time, Pallas kernels for 39%

profile of v5, /device:TPU:0, one launch (start us, length us, event | category | flops | bytes accessed | tf_op | source)
XLA Modules:
  0.0 260.6 jit_solution(8641907465171795118)
XLA Ops:
  0.0 2.4 dynamic-slice_bitcast_fusion.1.refs_8_.refs_10_
  2.4 0.7 stack.76.place_ref
  3.1 6.6 %shard_map.37 = (bf16[192,3072]{1,0:T(8,128)(2,1)}, bf16[192,3072]{1,0:T(8,128)(2,1)}) custom-call(s32[5]{0:T(128)} %stack.76.place_ref, bf16[1,384,6144]{2,1,0:T(8,128)(2,1)} %tokens_ref.1, f32[1,6144]{1,0:T(1,128)} %bitcast.50), custom_call_target="tpu_custom_call" | custom-call | flops 9437184 | bytes 4718592 | tf_op jit(solution)/shard_map/pallas_call | solution.py:77
  9.7 2.9 %collective-permute-start.2 = (bf16[192,3072]{1,0:T(8,128)(2,1)}, bf16[192,3072]{1,0:T(8,128)(2,1)}, u32[]{:S(2)}, u32[]{:S(2)}) collective-permute-start(bf16[192,3072]{1,0:T(8,128)(2,1)} %get-tuple-element.110.refs_0_), channel_id=1, source_target_pairs={{0,2},{2,0},{1,3},{3,1},{4,6},{6,4},{5,7},{7,5},{8,10},{10,8},{9,1... | collective-permute-start | bytes 3538952 | tf_op jit(solution)/shard_map/ppermute | solution.py:306
  12.6 1.5 collective-permute-start.3
  14.1 1.6 collective-permute-start
  15.7 1.7 collective-permute-start.1
  17.4 1.9 dynamic-slice_bitcast_fusion
  19.5 0.9 copy-done.8
  20.4 1.1 copy-done.2
  21.4 1.3 broadcast_select_fusion.3
  22.7 16.2 %collective-permute-done.2.refs_4_ = bf16[192,3072]{1,0:T(8,128)(2,1)} collective-permute-done((bf16[192,3072]{1,0:T(8,128)(2,1)}, bf16[192,3072]{1,0:T(8,128)(2,1)}, u32[]{:S(2)}, u32[]{:S(2)}) %collective-permute-start.2) | collective-permute-done | bytes 1179680 | tf_op jit(solution)/shard_map/ppermute | solution.py:306
  38.9 1.5 collective-permute-done.3.refs_0_.refs_8_
  40.3 1.2 collective-permute-done.refs_15_.refs_16_.refs_18_
  41.6 0.6 collective-permute-start.6
  42.5 4.7 %collective-permute-start.4 = (bf16[192,3072]{1,0:T(8,128)(2,1)}, bf16[192,3072]{1,0:T(8,128)(2,1)S(1)}, u32[]{:S(2)}, u32[]{:S(2)}) collective-permute-start(bf16[192,3072]{1,0:T(8,128)(2,1)} %broadcast_select_fusion.3), channel_id=1, source_target_pairs={{0,4},{4,0},{8,12},{12,8},{1,5},{5,1},{9,13},{13,9},{2,6},{6,2},{1... | collective-permute-start | bytes 3538952 | tf_op jit(solution)/shard_map/ppermute | solution.py:297
  47.2 1.7 collective-permute-start.5
  48.9 0.7 stack.78.place_ref
  49.6 1.5 copy.8
  51.1 6.5 %shard_map.38 = (bf16[192,3072]{1,0:T(8,128)(2,1)}, bf16[192,3072]{1,0:T(8,128)(2,1)}) custom-call(s32[5]{0:T(128)} %stack.78.place_ref, bf16[1,384,6144]{2,1,0:T(8,128)(2,1)} %tokens_ref.1, f32[1,6144]{1,0:T(1,128)} %bitcast.51), custom_call_target="tpu_custom_call" | custom-call | flops 9437184 | bytes 4718592 | tf_op jit(solution)/shard_map/pallas_call | solution.py:77
  57.7 15.8 %collective-permute-done.4.refs_17_.refs_9_.refs_0_.refs_16_ = bf16[192,3072]{1,0:T(8,128)(2,1)S(1)} collective-permute-done((bf16[192,3072]{1,0:T(8,128)(2,1)}, bf16[192,3072]{1,0:T(8,128)(2,1)S(1)}, u32[]{:S(2)}, u32[]{:S(2)}) %collective-permute-start.4) | collective-permute-done | bytes 1179680 | tf_op jit(solution)/shard_map/ppermute | solution.py:297
  73.6 1.6 collective-permute-start.13
  75.2 3.7 %collective-permute-start.10 = (bf16[192,3072]{1,0:T(8,128)(2,1)S(1)}, bf16[192,3072]{1,0:T(8,128)(2,1)S(1)}, u32[]{:S(2)}, u32[]{:S(2)}) collective-permute-start(bf16[192,3072]{1,0:T(8,128)(2,1)S(1)} %broadcast_select_fusion.2), channel_id=1, source_target_pairs={{0,4},{4,0},{8,12},{12,8},{1,5},{5,1},{9,13},{13,9},{2,6},{6,2},{1... | collective-permute-start | bytes 3538952 | tf_op jit(solution)/shard_map/ppermute | solution.py:297
  78.9 0.7 collective-permute-start.11
  79.7 1.6 collective-permute-start.12
  81.2 1.2 broadcast_select_fusion.1
  82.4 22.8 %collective-permute-done.10.refs_20_.refs_11_.refs_1_.refs_17_ = bf16[192,3072]{1,0:T(8,128)(2,1)S(1)} collective-permute-done((bf16[192,3072]{1,0:T(8,128)(2,1)S(1)}, bf16[192,3072]{1,0:T(8,128)(2,1)S(1)}, u32[]{:S(2)}, u32[]{:S(2)}) %collective-permute-start.10) | collective-permute-done | bytes 1179680 | tf_op jit(solution)/shard_map/ppermute | solution.py:297
  105.2 1.0 copy-done.19
  106.3 1.5 collective-permute-done.12.refs_4_.refs_12_
  108.4 1.5 collective-permute-start.18
  110.4 2.9 %collective-permute-start.16 = (bf16[1536,384]{1,0:T(8,128)(2,1)}, bf16[1536,384]{1,0:T(8,128)(2,1)S(1)}, u32[]{:S(2)}, u32[]{:S(2)}) collective-permute-start(bf16[1536,384]{1,0:T(8,128)(2,1)} %broadcast_select_fusion.1), channel_id=1, source_target_pairs={{0,4},{4,0},{8,12},{12,8},{1,5},{5,1},{9,13},{13,9},{2,6},{6,2},{1... | collective-permute-start | bytes 3538952 | tf_op jit(solution)/shard_map/ppermute | solution.py:297
  113.3 0.9 collective-permute-start.17
  114.4 1.5 pad_maximum_fusion
  115.9 1.2 broadcast_select_fusion
  117.1 16.8 %shard_map.39 = (bf16[768,128]{1,0:T(8,128)(2,1)}, f32[768,384]{1,0:T(8,128)}, f32[768,384]{1,0:T(8,128)}) custom-call(s32[2]{0:T(128)} %pad_add_fusion.role_ref, bf16[192,3072]{1,0:T(8,128)(2,1)} %get-tuple-element.110.refs_0_, bf16[192,3072]{1,0:T(8,128)(2,1)} %get-tuple-element.115.refs_1_, bf16[192,3072]{1,0:T(8,128)(2,1)} %get-tuple-element.140.refs_2_, ...), custom_call_target="tpu_custom_call" | custom-call | flops 6341787648 | tf_op jit(solution)/shard_map/pallas_call | solution.py:248
  133.9 5.7 %collective-permute-done.16.refs_19_.refs_10_.refs_17_ = bf16[1536,384]{1,0:T(8,128)(2,1)S(1)} collective-permute-done((bf16[1536,384]{1,0:T(8,128)(2,1)}, bf16[1536,384]{1,0:T(8,128)(2,1)S(1)}, u32[]{:S(2)}, u32[]{:S(2)}) %collective-permute-start.16) | collective-permute-done | bytes 1179680 | tf_op jit(solution)/shard_map/ppermute | solution.py:297
  139.7 1.0 copy-done.11
  141.6 1.5 collective-permute-start.25
  143.1 3.4 %collective-permute-start.22 = (bf16[1536,384]{1,0:T(8,128)(2,1)}, bf16[1536,384]{1,0:T(8,128)(2,1)S(1)}, u32[]{:S(2)}, u32[]{:S(2)}) collective-permute-start(bf16[1536,384]{1,0:T(8,128)(2,1)} %broadcast_select_fusion), channel_id=1, source_target_pairs={{0,4},{4,0},{8,12},{12,8},{1,5},{5,1},{9,13},{13,9},{2,6},{6,2},{1... | collective-permute-start | bytes 3538952 | tf_op jit(solution)/shard_map/ppermute | solution.py:297
  146.5 2.1 collective-permute-start.23
  148.7 8.7 %shard_map.41 = (f32[768,384]{1,0:T(8,128)}, f32[768,384]{1,0:T(8,128)}) custom-call(s32[2]{0:T(128)} %pad_add_fusion.role_ref, bf16[192,3072]{1,0:T(8,128)(2,1)} %get-tuple-element.110.refs_0_, bf16[192,3072]{1,0:T(8,128)(2,1)} %get-tuple-element.115.refs_1_, bf16[192,3072]{1,0:T(8,128)(2,1)} %get-tuple-element.140.refs_2_, ...), custom_call_target="tpu_custom_call" | custom-call | flops 1811939328 | tf_op jit(solution)/shard_map/pallas_call | solution.py:248
  157.5 18.6 %shard_map.40 = (bf16[768,128]{1,0:T(8,128)(2,1)}, f32[768,384]{1,0:T(8,128)}, f32[768,384]{1,0:T(8,128)}) custom-call(s32[2]{0:T(128)} %pad_add_fusion.role_ref, bf16[192,3072]{1,0:T(8,128)(2,1)} %collective-permute-done.3.refs_0_.refs_8_, bf16[192,3072]{1,0:T(8,128)(2,1)} %collective-permute-done.7.refs_1_.refs_9_, ...), custom_call_target="tpu_custom_call" | custom-call | flops 8153726976 | tf_op jit(solution)/shard_map/pallas_call | solution.py:248
  177.2 1.3 collective-permute-start.28
  178.5 0.9 collective-permute-start.29
  179.4 1.6 collective-permute-start.30
  181.0 15.9 %shard_map.42 = (bf16[1536,128]{1,0:T(8,128)(2,1)}, f32[1536,384]{1,0:T(8,128)}) custom-call(s32[2]{0:T(128)} %pad_add_fusion.role_ref, bf16[192,3072]{1,0:T(8,128)(2,1)} %get-tuple-element.110.refs_0_, bf16[192,3072]{1,0:T(8,128)(2,1)} %get-tuple-element.115.refs_1_, bf16[192,3072]{1,0:T(8,128)(2,1)} %get-tuple-element.140.refs_2_, ...), custom_call_target="tpu_custom_call" | custom-call | flops 3623878656 | tf_op jit(solution)/shard_map/pallas_call | solution.py:248
  196.9 8.6 %shard_map.43.refs_28_ = f32[768,384]{1,0:T(8,128)} custom-call(s32[2]{0:T(128)} %pad_add_fusion.role_ref, bf16[192,3072]{1,0:T(8,128)(2,1)} %copy-done.4, bf16[192,3072]{1,0:T(8,128)(2,1)} %copy-done.5, bf16[384,3072]{1,0:T(8,128)(2,1)} %copy-done, bf16[384,3072]{1,0:T(8,128)(2,1)} %copy-done, bf16[192,3072]{1,0:T(8,128)(2,1)} %copy-done.11, ...), custom_call_target="tpu_custom_call" | custom-call | flops 2717908992 | tf_op jit(solution)/shard_map/pallas_call | solution.py:248
  205.5 1.6 collective-permute-done.28.refs_25_
  208.1 14.8 %shard_map.44 = bf16[2304,128]{1,0:T(8,128)(2,1)} custom-call(s32[2]{0:T(128)} %pad_add_fusion.role_ref, bf16[192,3072]{1,0:T(8,128)(2,1)} %get-tuple-element.110.refs_0_, bf16[192,3072]{1,0:T(8,128)(2,1)} %get-tuple-element.115.refs_1_, bf16[192,3072]{1,0:T(8,128)(2,1)} %get-tuple-element.140.refs_2_, bf16[192,3072]{1,0:T(8,128)(2,1)} %get-tuple-element.141.refs_3_, ...), custom_call_target="tpu_custom_call" | custom-call | flops 2717908992 | tf_op jit(solution)/shard_map/pallas_call | solution.py:248
  223.0 1.0 slice.55
  224.2 1.0 fusion.4
  225.2 1.5 collective-permute-start.34
  226.7 1.5 collective-permute-start.35
  228.2 1.0 fusion.5
  229.7 1.3 collective-permute-start.37
  231.1 1.3 collective-permute-start.38
  232.4 11.4 %shard_map.45 = bf16[768,128]{1,0:T(8,128)(2,1)} custom-call(s32[2]{0:T(128)} %pad_add_fusion.role_ref, bf16[192,3072]{1,0:T(8,128)(2,1)} %collective-permute-done.19.refs_0_, bf16[192,3072]{1,0:T(8,128)(2,1)} %collective-permute-done.25.refs_1_, bf16[192,3072]{1,0:T(8,128)(2,1)} %collective-permute-done.33.refs_2_, bf16[192,3072]{1,0:T(8,128)(2,1)} %copy-done.21, ...), custom_call_target="tpu_custom_call" | custom-call | flops 3623878656 | tf_op jit(solution)/shard_map/pallas_call | solution.py:248
  243.8 1.0 fusion.6
  244.7 1.3 collective-permute-start.42
  246.0 1.3 collective-permute-start.43
  247.4 8.1 %collective-permute-done.42 = bf16[384,128]{1,0:T(8,128)(2,1)S(1)} collective-permute-done((bf16[384,128]{1,0:T(8,128)(2,1)S(1)}, bf16[384,128]{1,0:T(8,128)(2,1)S(1)}, u32[]{:S(2)}, u32[]{:S(2)}) %collective-permute-start.42) | collective-permute-done | bytes 98336 | tf_op jit(solution)/shard_map/ppermute | solution.py:464
  255.5 2.1 collective-permute-done.43
  257.7 0.9 slice.54
  259.3 1.1 maximum_bitcast_fusion
  (113 shorter events, 6.5 us)
Async XLA Ops:
  9.7 29.2 %collective-permute-start.2 = (bf16[192,3072]{1,0:T(8,128)(2,1)}, bf16[192,3072]{1,0:T(8,128)(2,1)}, u32[]{:S(2)}, u32[]{:S(2)}) collective-permute-start(bf16[192,3072]{1,0:T(8,128)(2,1)} %get-tuple-element.110.refs_0_), channel_id=1, source_target_pairs={{0,2},{2,0},{1,3},{3,1},{4,6},{6,4},{5,7},{7,5},{8,10},{10,8},{9,1... | collective-permute-start | bytes 3538952 | tf_op jit(solution)/shard_map/ppermute | solution.py:306
  12.6 27.7 %collective-permute-start.3 = (bf16[192,3072]{1,0:T(8,128)(2,1)}, bf16[192,3072]{1,0:T(8,128)(2,1)}, u32[]{:S(2)}, u32[]{:S(2)}) collective-permute-start(bf16[192,3072]{1,0:T(8,128)(2,1)} %get-tuple-element.110.refs_0_), channel_id=1, source_target_pairs={{0,16},{16,0},{1,17},{17,1},{2,18},{18,2},{3,19},{19,3},{4,20},{20... | collective-permute-start | bytes 3538952 | tf_op jit(solution)/shard_map/ppermute | solution.py:307
  14.1 27.5 %collective-permute-start = (bf16[1536,384]{1,0:T(8,128)(2,1)}, bf16[1536,384]{1,0:T(8,128)(2,1)}, u32[]{:S(2)}, u32[]{:S(2)}) collective-permute-start(bf16[1536,384]{1,0:T(8,128)(2,1)} %dynamic-slice_bitcast_fusion.1.refs_8_.refs_10_), channel_id=1, source_target_pairs={{0,4},{4,0},{8,12},{12,8},{1,5},{5,1},{9,13},{13,9},{2,6},{6,2},{1... | collective-permute-start | bytes 3538952 | tf_op jit(solution)/shard_map/ppermute | solution.py:297
  15.7 25.9 %collective-permute-start.1 = (bf16[1536,384]{1,0:T(8,128)(2,1)}, bf16[1536,384]{1,0:T(8,128)(2,1)}, u32[]{:S(2)}, u32[]{:S(2)}) collective-permute-start(bf16[1536,384]{1,0:T(8,128)(2,1)} %dynamic-slice_bitcast_fusion.1.refs_8_.refs_10_), channel_id=1, source_target_pairs={{4,8},{8,4},{5,9},{9,5},{6,10},{10,6},{7,11},{11,7},{20,24},{24,20... | collective-permute-start | bytes 3538952 | tf_op jit(solution)/shard_map/ppermute | solution.py:303
  19.3 96.6 %copy-start.1 = (bf16[1536,384]{1,0:T(8,128)(2,1)}, bf16[1536,384]{1,0:T(8,128)(2,1)S(1)}, u32[]{:S(2)}) copy-start(bf16[1536,384]{1,0:T(8,128)(2,1)S(1)} %get-tuple-element.190.refs_11_.refs_10_) | copy-start | bytes 3538948
  19.3 2.1 copy-start.2
  21.4 20.2 %copy-start.3 = (bf16[192,3072]{1,0:T(8,128)(2,1)S(1)}, bf16[192,3072]{1,0:T(8,128)(2,1)}, u32[]{:S(2)}) copy-start(bf16[192,3072]{1,0:T(8,128)(2,1)} %get-tuple-element.115.refs_1_) | copy-start | bytes 3538948
  41.6 7.4 %collective-permute-start.8 = (bf16[192,3072]{1,0:T(8,128)(2,1)}, bf16[192,3072]{1,0:T(8,128)(2,1)}, u32[]{:S(2)}, u32[]{:S(2)}) collective-permute-start(bf16[192,3072]{1,0:T(8,128)(2,1)} %collective-permute-done.2.refs_4_), channel_id=1, source_target_pairs={{0,1},{1,0},{2,3},{3,2},{4,5},{5,4},{6,7},{7,6},{8,9},{9,8},{10,11... | collective-permute-start | bytes 3538952 | tf_op jit(solution)/shard_map/ppermute | solution.py:314
  41.6 31.9 %collective-permute-start.6 = (bf16[192,3072]{1,0:T(8,128)(2,1)S(1)}, bf16[192,3072]{1,0:T(8,128)(2,1)}, u32[]{:S(2)}, u32[]{:S(2)}) collective-permute-start(bf16[192,3072]{1,0:T(8,128)(2,1)S(1)} %copy-done.3), channel_id=1, source_target_pairs={{0,2},{2,0},{1,3},{3,1},{4,6},{6,4},{5,7},{7,5},{8,10},{10,8},{9,1... | collective-permute-start | bytes 3538952 | tf_op jit(solution)/shard_map/ppermute | solution.py:306
  42.2 31.3 %collective-permute-start.7 = (bf16[192,3072]{1,0:T(8,128)(2,1)S(1)}, bf16[192,3072]{1,0:T(8,128)(2,1)}, u32[]{:S(2)}, u32[]{:S(2)}) collective-permute-start(bf16[192,3072]{1,0:T(8,128)(2,1)S(1)} %copy-done.3), channel_id=1, source_target_pairs={{0,16},{16,0},{1,17},{17,1},{2,18},{18,2},{3,19},{19,3},{4,20},{20... | collective-permute-start | bytes 3538952 | tf_op jit(solution)/shard_map/ppermute | solution.py:307
  42.5 31.0 %collective-permute-start.4 = (bf16[192,3072]{1,0:T(8,128)(2,1)}, bf16[192,3072]{1,0:T(8,128)(2,1)S(1)}, u32[]{:S(2)}, u32[]{:S(2)}) collective-permute-start(bf16[192,3072]{1,0:T(8,128)(2,1)} %broadcast_select_fusion.3), channel_id=1, source_target_pairs={{0,4},{4,0},{8,12},{12,8},{1,5},{5,1},{9,13},{13,9},{2,6},{6,2},{1... | collective-permute-start | bytes 3538952 | tf_op jit(solution)/shard_map/ppermute | solution.py:297
  47.2 26.3 %collective-permute-start.5 = (bf16[1536,384]{1,0:T(8,128)(2,1)}, bf16[1536,384]{1,0:T(8,128)(2,1)}, u32[]{:S(2)}, u32[]{:S(2)}) collective-permute-start(bf16[1536,384]{1,0:T(8,128)(2,1)} %collective-permute-done.refs_15_.refs_16_.refs_18_), channel_id=1, source_target_pairs={{4,8},{8,4},{5,9},{9,5},{6,10},{10,6},{7,11},{11,7},{20,24},{24,20... | collective-permute-start | bytes 3538952 | tf_op jit(solution)/shard_map/ppermute | solution.py:303
  48.9 24.6 %collective-permute-start.9 = (bf16[192,3072]{1,0:T(8,128)(2,1)}, bf16[192,3072]{1,0:T(8,128)(2,1)}, u32[]{:S(2)}, u32[]{:S(2)}) collective-permute-start(bf16[192,3072]{1,0:T(8,128)(2,1)} %collective-permute-done.3.refs_0_.refs_8_), channel_id=1, source_target_pairs={{0,1},{1,0},{2,3},{3,2},{4,5},{5,4},{6,7},{7,6},{8,9},{9,8},{10,11... | collective-permute-start | bytes 3538952 | tf_op jit(solution)/shard_map/ppermute | solution.py:314
  57.6 21.3 %copy-start.9 = (bf16[1536,1,384]{2,0,1:T(8,128)(2,1)S(1)}, bf16[1536,1,384]{2,0,1:T(8,128)(2,1)}, u32[]{:S(2)}) copy-start(bf16[1536,1,384]{2,0,1:T(8,128)(2,1)} %copy-done.8) | copy-start | bytes 3538948
  73.5 40.8 %copy-start.4 = (bf16[192,3072]{1,0:T(8,128)(2,1)}, bf16[192,3072]{1,0:T(8,128)(2,1)S(1)}, u32[]{:S(2)}) copy-start(bf16[192,3072]{1,0:T(8,128)(2,1)S(1)} %collective-permute-done.4.refs_17_.refs_9_.refs_0_.refs_16_) | copy-start | bytes 3538948
  73.5 7.7 %collective-permute-start.14 = (bf16[192,3072]{1,0:T(8,128)(2,1)}, bf16[192,3072]{1,0:T(8,128)(2,1)}, u32[]{:S(2)}, u32[]{:S(2)}) collective-permute-start(bf16[192,3072]{1,0:T(8,128)(2,1)} %collective-permute-done.6.refs_5_), channel_id=1, source_target_pairs={{0,1},{1,0},{2,3},{3,2},{4,5},{5,4},{6,7},{7,6},{8,9},{9,8},{10,11... | collective-permute-start | bytes 3538952 | tf_op jit(solution)/shard_map/ppermute | solution.py:314
  73.6 34.2 %collective-permute-start.13 = (bf16[192,3072]{1,0:T(8,128)(2,1)}, bf16[192,3072]{1,0:T(8,128)(2,1)}, u32[]{:S(2)}, u32[]{:S(2)}) collective-permute-start(bf16[192,3072]{1,0:T(8,128)(2,1)} %collective-permute-done.6.refs_5_), channel_id=1, source_target_pairs={{0,16},{16,0},{1,17},{17,1},{2,18},{18,2},{3,19},{19,3},{4,20},{20... | collective-permute-start | bytes 3538952 | tf_op jit(solution)/shard_map/ppermute | solution.py:307
  75.2 30.0 %collective-permute-start.10 = (bf16[192,3072]{1,0:T(8,128)(2,1)S(1)}, bf16[192,3072]{1,0:T(8,128)(2,1)S(1)}, u32[]{:S(2)}, u32[]{:S(2)}) collective-permute-start(bf16[192,3072]{1,0:T(8,128)(2,1)S(1)} %broadcast_select_fusion.2), channel_id=1, source_target_pairs={{0,4},{4,0},{8,12},{12,8},{1,5},{5,1},{9,13},{13,9},{2,6},{6,2},{1... | collective-permute-start | bytes 3538952 | tf_op jit(solution)/shard_map/ppermute | solution.py:297
  78.9 26.3 %collective-permute-start.11 = (bf16[1536,384]{1,0:T(8,128)(2,1)S(1)}, bf16[1536,384]{1,0:T(8,128)(2,1)S(1)}, u32[]{:S(2)}, u32[]{:S(2)}) collective-permute-start(bf16[1536,384]{1,0:T(8,128)(2,1)S(1)} %bitcast.46), channel_id=1, source_target_pairs={{4,8},{8,4},{5,9},{9,5},{6,10},{10,6},{7,11},{11,7},{20,24},{24,20... | collective-permute-start | bytes 3538952 | tf_op jit(solution)/shard_map/ppermute | solution.py:303
  79.7 28.1 %collective-permute-start.12 = (bf16[192,3072]{1,0:T(8,128)(2,1)}, bf16[192,3072]{1,0:T(8,128)(2,1)}, u32[]{:S(2)}, u32[]{:S(2)}) collective-permute-start(bf16[192,3072]{1,0:T(8,128)(2,1)} %collective-permute-done.3.refs_0_.refs_8_), channel_id=1, source_target_pairs={{0,2},{2,0},{1,3},{3,1},{4,6},{6,4},{5,7},{7,5},{8,10},{10,8},{9,1... | collective-permute-start | bytes 3538952 | tf_op jit(solution)/shard_map/ppermute | solution.py:306
  81.2 26.6 %collective-permute-start.15 = (bf16[192,3072]{1,0:T(8,128)(2,1)}, bf16[192,3072]{1,0:T(8,128)(2,1)}, u32[]{:S(2)}, u32[]{:S(2)}) collective-permute-start(bf16[192,3072]{1,0:T(8,128)(2,1)} %collective-permute-done.7.refs_1_.refs_9_), channel_id=1, source_target_pairs={{0,1},{1,0},{2,3},{3,2},{4,5},{5,4},{6,7},{7,6},{8,9},{9,8},{10,11... | collective-permute-start | bytes 3538952 | tf_op jit(solution)/shard_map/ppermute | solution.py:314
  105.2 36.4 %copy-start.5 = (bf16[192,3072]{1,0:T(8,128)(2,1)}, bf16[192,3072]{1,0:T(8,128)(2,1)S(1)}, u32[]{:S(2)}) copy-start(bf16[192,3072]{1,0:T(8,128)(2,1)S(1)} %collective-permute-done.10.refs_20_.refs_11_.refs_1_.refs_17_) | copy-start | bytes 3538948
  107.8 6.5 %collective-permute-start.20 = (bf16[192,3072]{1,0:T(8,128)(2,1)}, bf16[192,3072]{1,0:T(8,128)(2,1)}, u32[]{:S(2)}, u32[]{:S(2)}) collective-permute-start(bf16[192,3072]{1,0:T(8,128)(2,1)} %collective-permute-done.12.refs_4_.refs_12_), channel_id=1, source_target_pairs={{0,1},{1,0},{2,3},{3,2},{4,5},{5,4},{6,7},{7,6},{8,9},{9,8},{10,11... | collective-permute-start | bytes 3538952 | tf_op jit(solution)/shard_map/ppermute | solution.py:314
  108.4 7.5 %copy-start.20 = (bf16[1536,384]{1,0:T(8,128)(2,1)S(1)}, bf16[1536,384]{1,0:T(8,128)(2,1)}, u32[]{:S(2)}) copy-start(bf16[1536,384]{1,0:T(8,128)(2,1)} %copy-done.19) | copy-start | bytes 3538948
  108.4 31.2 %collective-permute-start.18 = (bf16[192,3072]{1,0:T(8,128)(2,1)S(1)}, bf16[192,3072]{1,0:T(8,128)(2,1)S(1)}, u32[]{:S(2)}, u32[]{:S(2)}) collective-permute-start(bf16[192,3072]{1,0:T(8,128)(2,1)S(1)} %collective-permute-done.4.refs_17_.refs_9_.refs_0_.refs_16_), channel_id=1, source_target_pairs={{0,2},{2,0},{1,3},{3,1},{4,6},{6,4},{5,7},{7,5},{8,10},{10,8},{9,1... | collective-permute-start | bytes 3538952 | tf_op jit(solution)/shard_map/ppermute | solution.py:306
  109.9 29.7 %collective-permute-start.19 = (bf16[192,3072]{1,0:T(8,128)(2,1)S(1)}, bf16[192,3072]{1,0:T(8,128)(2,1)}, u32[]{:S(2)}, u32[]{:S(2)}) collective-permute-start(bf16[192,3072]{1,0:T(8,128)(2,1)S(1)} %collective-permute-done.4.refs_17_.refs_9_.refs_0_.refs_16_), channel_id=1, source_target_pairs={{0,16},{16,0},{1,17},{17,1},{2,18},{18,2},{3,19},{19,3},{4,20},{20... | collective-permute-start | bytes 3538952 | tf_op jit(solution)/shard_map/ppermute | solution.py:307
  110.4 29.2 %collective-permute-start.16 = (bf16[1536,384]{1,0:T(8,128)(2,1)}, bf16[1536,384]{1,0:T(8,128)(2,1)S(1)}, u32[]{:S(2)}, u32[]{:S(2)}) collective-permute-start(bf16[1536,384]{1,0:T(8,128)(2,1)} %broadcast_select_fusion.1), channel_id=1, source_target_pairs={{0,4},{4,0},{8,12},{12,8},{1,5},{5,1},{9,13},{13,9},{2,6},{6,2},{1... | collective-permute-start | bytes 3538952 | tf_op jit(solution)/shard_map/ppermute | solution.py:297
  113.3 26.3 %collective-permute-start.17 = (bf16[1536,384]{1,0:T(8,128)(2,1)S(1)}, bf16[1536,384]{1,0:T(8,128)(2,1)S(1)}, u32[]{:S(2)}, u32[]{:S(2)}) collective-permute-start(bf16[1536,384]{1,0:T(8,128)(2,1)S(1)} %get-tuple-element.190.refs_11_.refs_10_), channel_id=1, source_target_pairs={{4,8},{8,4},{5,9},{9,5},{6,10},{10,6},{7,11},{11,7},{20,24},{24,20... | collective-permute-start | bytes 3538952 | tf_op jit(solution)/shard_map/ppermute | solution.py:303
  114.3 25.4 %collective-permute-start.21 = (bf16[192,3072]{1,0:T(8,128)(2,1)}, bf16[192,3072]{1,0:T(8,128)(2,1)S(1)}, u32[]{:S(2)}, u32[]{:S(2)}) collective-permute-start(bf16[192,3072]{1,0:T(8,128)(2,1)} %collective-permute-done.13.refs_5_.refs_13_), channel_id=1, source_target_pairs={{0,1},{1,0},{2,3},{3,2},{4,5},{5,4},{6,7},{7,6},{8,9},{9,8},{10,11... | collective-permute-start | bytes 3538952 | tf_op jit(solution)/shard_map/ppermute | solution.py:314
  139.6 9.1 %copy-start.6 = (bf16[1536,384]{1,0:T(8,128)(2,1)}, bf16[1536,384]{1,0:T(8,128)(2,1)S(1)}, u32[]{:S(2)}) copy-start(bf16[1536,384]{1,0:T(8,128)(2,1)S(1)} %collective-permute-done.17.refs_16_.refs_8_.refs_9_) | copy-start | bytes 3538948
  141.0 7.6 %collective-permute-start.26 = (bf16[384,3072]{1,0:T(8,128)(2,1)}, bf16[384,3072]{1,0:T(8,128)(2,1)S(1)}, u32[]{:S(2)}, u32[]{:S(2)}) collective-permute-start(bf16[384,3072]{1,0:T(8,128)(2,1)} %pad_maximum_fusion), channel_id=1, source_target_pairs={{0,1},{1,0},{2,3},{3,2},{4,5},{5,4},{6,7},{7,6},{8,9},{9,8},{10,11... | collective-permute-start | bytes 7077896 | tf_op jit(solution)/shard_map/ppermute | solution.py:314
  141.1 35.1 %collective-permute-start.24 = (bf16[192,3072]{1,0:T(8,128)(2,1)S(1)}, bf16[192,3072]{1,0:T(8,128)(2,1)S(1)}, u32[]{:S(2)}, u32[]{:S(2)}) collective-permute-start(bf16[192,3072]{1,0:T(8,128)(2,1)S(1)} %collective-permute-done.10.refs_20_.refs_11_.refs_1_.refs_17_), channel_id=1, source_target_pairs={{0,2},{2,0},{1,3},{3,1},{4,6},{6,4},{5,7},{7,5},{8,10},{10,8},{9,1... | collective-permute-start | bytes 3538952 | tf_op jit(solution)/shard_map/ppermute | solution.py:306
  141.6 34.5 %collective-permute-start.25 = (bf16[192,3072]{1,0:T(8,128)(2,1)S(1)}, bf16[192,3072]{1,0:T(8,128)(2,1)}, u32[]{:S(2)}, u32[]{:S(2)}) collective-permute-start(bf16[192,3072]{1,0:T(8,128)(2,1)S(1)} %collective-permute-done.10.refs_20_.refs_11_.refs_1_.refs_17_), channel_id=1, source_target_pairs={{0,16},{16,0},{1,17},{17,1},{2,18},{18,2},{3,19},{19,3},{4,20},{20... | collective-permute-start | bytes 3538952 | tf_op jit(solution)/shard_map/ppermute | solution.py:307
  143.1 33.0 %collective-permute-start.22 = (bf16[1536,384]{1,0:T(8,128)(2,1)}, bf16[1536,384]{1,0:T(8,128)(2,1)S(1)}, u32[]{:S(2)}, u32[]{:S(2)}) collective-permute-start(bf16[1536,384]{1,0:T(8,128)(2,1)} %broadcast_select_fusion), channel_id=1, source_target_pairs={{0,4},{4,0},{8,12},{12,8},{1,5},{5,1},{9,13},{13,9},{2,6},{6,2},{1... | collective-permute-start | bytes 3538952 | tf_op jit(solution)/shard_map/ppermute | solution.py:297
  146.5 29.6 %collective-permute-start.23 = (bf16[1536,384]{1,0:T(8,128)(2,1)}, bf16[1536,384]{1,0:T(8,128)(2,1)}, u32[]{:S(2)}, u32[]{:S(2)}) collective-permute-start(bf16[1536,384]{1,0:T(8,128)(2,1)} %copy-done.10), channel_id=1, source_target_pairs={{4,8},{8,4},{5,9},{9,5},{6,10},{10,6},{7,11},{11,7},{20,24},{24,20... | collective-permute-start | bytes 3538952 | tf_op jit(solution)/shard_map/ppermute | solution.py:303
  148.6 8.8 %copy-start = (bf16[384,3072]{1,0:T(8,128)(2,1)}, bf16[384,3072]{1,0:T(8,128)(2,1)S(1)}, u32[]{:S(2)}) copy-start(bf16[384,3072]{1,0:T(8,128)(2,1)S(1)} %collective-permute-done.26.refs_2_.refs_3_.refs_18_.refs_19_) | copy-start | bytes 7077892
  148.7 27.5 %collective-permute-start.27 = (bf16[192,3072]{1,0:T(8,128)(2,1)}, bf16[192,3072]{1,0:T(8,128)(2,1)S(1)}, u32[]{:S(2)}, u32[]{:S(2)}) collective-permute-start(bf16[192,3072]{1,0:T(8,128)(2,1)} %copy-done.11), channel_id=1, source_target_pairs={{0,1},{1,0},{2,3},{3,2},{4,5},{5,4},{6,7},{7,6},{8,9},{9,8},{10,11... | collective-permute-start | bytes 3538952 | tf_op jit(solution)/shard_map/ppermute | solution.py:314
  176.1 4.9 %copy-start.7 = (bf16[1536,384]{1,0:T(8,128)(2,1)}, bf16[1536,384]{1,0:T(8,128)(2,1)S(1)}, u32[]{:S(2)}) copy-start(bf16[1536,384]{1,0:T(8,128)(2,1)S(1)} %collective-permute-done.22.refs_18_.refs_8_) | copy-start | bytes 3538948
  176.1 20.8 %copy-start.13 = (bf16[192,3072]{1,0:T(8,128)(2,1)}, bf16[192,3072]{1,0:T(8,128)(2,1)S(1)}, u32[]{:S(2)}) copy-start(bf16[192,3072]{1,0:T(8,128)(2,1)S(1)} %collective-permute-done.24.refs_5_.refs_21_) | copy-start | bytes 3538948
  176.1 20.8 %copy-start.14 = (bf16[192,3072]{1,0:T(8,128)(2,1)}, bf16[192,3072]{1,0:T(8,128)(2,1)S(1)}, u32[]{:S(2)}) copy-start(bf16[192,3072]{1,0:T(8,128)(2,1)S(1)} %collective-permute-done.27.refs_6_.refs_22_) | copy-start | bytes 3538948
  176.2 4.8 %collective-permute-start.32 = (bf16[192,3072]{1,0:T(8,128)(2,1)S(1)}, bf16[192,3072]{1,0:T(8,128)(2,1)S(1)}, u32[]{:S(2)}, u32[]{:S(2)}) collective-permute-start(bf16[192,3072]{1,0:T(8,128)(2,1)S(1)} %collective-permute-done.24.refs_5_.refs_21_), channel_id=1, source_target_pairs={{0,1},{1,0},{2,3},{3,2},{4,5},{5,4},{6,7},{7,6},{8,9},{9,8},{10,11... | collective-permute-start | bytes 3538952 | tf_op jit(solution)/shard_map/ppermute | solution.py:314
  176.7 30.7 %collective-permute-start.31 = (bf16[192,3072]{1,0:T(8,128)(2,1)S(1)}, bf16[192,3072]{1,0:T(8,128)(2,1)S(1)}, u32[]{:S(2)}, u32[]{:S(2)}) collective-permute-start(bf16[192,3072]{1,0:T(8,128)(2,1)S(1)} %collective-permute-done.24.refs_5_.refs_21_), channel_id=1, source_target_pairs={{0,16},{16,0},{1,17},{17,1},{2,18},{18,2},{3,19},{19,3},{4,20},{20... | collective-permute-start | bytes 3538952 | tf_op jit(solution)/shard_map/ppermute | solution.py:307
  177.2 29.9 %collective-permute-start.28 = (bf16[1536,384]{1,0:T(8,128)(2,1)}, bf16[1536,384]{1,0:T(8,128)(2,1)}, u32[]{:S(2)}, u32[]{:S(2)}) collective-permute-start(bf16[1536,384]{1,0:T(8,128)(2,1)} %collective-permute-done.23.refs_16_), channel_id=1, source_target_pairs={{4,0},{8,12},{5,1},{9,13},{6,2},{10,14},{7,3},{11,15},{20,16},{24,... | collective-permute-start | bytes 3538952 | tf_op jit(solution)/shard_map/ppermute | solution.py:300
  178.5 28.6 %collective-permute-start.29 = (bf16[1536,384]{1,0:T(8,128)(2,1)S(1)}, bf16[1536,384]{1,0:T(8,128)(2,1)S(1)}, u32[]{:S(2)}, u32[]{:S(2)}) collective-permute-start(bf16[1536,384]{1,0:T(8,128)(2,1)S(1)} %collective-permute-done.22.refs_18_.refs_8_), channel_id=1, source_target_pairs={{4,8},{8,4},{5,9},{9,5},{6,10},{10,6},{7,11},{11,7},{20,24},{24,20... | collective-permute-start | bytes 3538952 | tf_op jit(solution)/shard_map/ppermute | solution.py:303
  179.4 27.9 %collective-permute-start.30 = (bf16[192,3072]{1,0:T(8,128)(2,1)}, bf16[192,3072]{1,0:T(8,128)(2,1)S(1)}, u32[]{:S(2)}, u32[]{:S(2)}) collective-permute-start(bf16[192,3072]{1,0:T(8,128)(2,1)} %collective-permute-done.19.refs_0_), channel_id=1, source_target_pairs={{0,2},{2,0},{1,3},{3,1},{4,6},{6,4},{5,7},{7,5},{8,10},{10,8},{9,1... | collective-permute-start | bytes 3538952 | tf_op jit(solution)/shard_map/ppermute | solution.py:306
  181.0 16.0 %copy-start.15 = (bf16[192,3072]{1,0:T(8,128)(2,1)}, bf16[192,3072]{1,0:T(8,128)(2,1)S(1)}, u32[]{:S(2)}) copy-start(bf16[192,3072]{1,0:T(8,128)(2,1)S(1)} %collective-permute-done.32.refs_7_.refs_23_) | copy-start | bytes 3538948
  181.0 26.4 %collective-permute-start.33 = (bf16[192,3072]{1,0:T(8,128)(2,1)}, bf16[192,3072]{1,0:T(8,128)(2,1)}, u32[]{:S(2)}, u32[]{:S(2)}) collective-permute-start(bf16[192,3072]{1,0:T(8,128)(2,1)} %collective-permute-done.19.refs_0_), channel_id=1, source_target_pairs={{0,1},{1,0},{2,3},{3,2},{4,5},{5,4},{6,7},{7,6},{8,9},{9,8},{10,11... | collective-permute-start | bytes 3538952 | tf_op jit(solution)/shard_map/ppermute | solution.py:314
  207.3 15.6 %copy-start.18 = (bf16[192,3072]{1,0:T(8,128)(2,1)}, bf16[192,3072]{1,0:T(8,128)(2,1)S(1)}, u32[]{:S(2)}) copy-start(bf16[192,3072]{1,0:T(8,128)(2,1)S(1)} %collective-permute-done.30.refs_4_) | copy-start | bytes 3538948
  207.3 15.6 %copy-start.17 = (bf16[192,3072]{1,0:T(8,128)(2,1)}, bf16[192,3072]{1,0:T(8,128)(2,1)S(1)}, u32[]{:S(2)}) copy-start(bf16[192,3072]{1,0:T(8,128)(2,1)S(1)} %collective-permute-done.31.refs_5_) | copy-start | bytes 3538948
  207.4 16.6 %copy-start.24 = (bf16[1536,128]{1,0:T(8,128)(2,1)S(1)}, bf16[1536,128]{1,0:T(8,128)(2,1)}, u32[]{:S(2)}) copy-start(bf16[1536,128]{1,0:T(8,128)(2,1)} %get-tuple-element.192) | copy-start | bytes 1179652
  207.4 16.6 %copy-start.25 = (bf16[768,128]{1,0:T(8,128)(2,1)S(1)}, bf16[768,128]{1,0:T(8,128)(2,1)}, u32[]{:S(2)}) copy-start(bf16[768,128]{1,0:T(8,128)(2,1)} %get-tuple-element.154) | copy-start | bytes 589828
  207.4 16.6 %copy-start.26 = (bf16[768,128]{1,0:T(8,128)(2,1)S(1)}, bf16[768,128]{1,0:T(8,128)(2,1)}, u32[]{:S(2)}) copy-start(bf16[768,128]{1,0:T(8,128)(2,1)} %get-tuple-element.175) | copy-start | bytes 589828
  207.4 21.8 %collective-permute-start.39 = (bf16[192,3072]{1,0:T(8,128)(2,1)}, bf16[192,3072]{1,0:T(8,128)(2,1)S(1)}, u32[]{:S(2)}, u32[]{:S(2)}) collective-permute-start(bf16[192,3072]{1,0:T(8,128)(2,1)} %collective-permute-done.25.refs_1_), channel_id=1, source_target_pairs={{0,1},{1,0},{2,3},{3,2},{4,5},{5,4},{6,7},{7,6},{8,9},{9,8},{10,11... | collective-permute-start | bytes 3538952 | tf_op jit(solution)/shard_map/ppermute | solution.py:429
  207.5 22.3 %collective-permute-start.40 = (bf16[192,3072]{1,0:T(8,128)(2,1)S(1)}, bf16[192,3072]{1,0:T(8,128)(2,1)S(1)}, u32[]{:S(2)}, u32[]{:S(2)}) collective-permute-start(bf16[192,3072]{1,0:T(8,128)(2,1)S(1)} %collective-permute-done.30.refs_4_), channel_id=1, source_target_pairs={{0,1},{1,0},{2,3},{3,2},{4,5},{5,4},{6,7},{7,6},{8,9},{9,8},{10,11... | collective-permute-start | bytes 3538952 | tf_op jit(solution)/shard_map/ppermute | solution.py:429
  208.0 23.1 %collective-permute-start.41 = (bf16[192,3072]{1,0:T(8,128)(2,1)S(1)}, bf16[192,3072]{1,0:T(8,128)(2,1)S(1)}, u32[]{:S(2)}, u32[]{:S(2)}) collective-permute-start(bf16[192,3072]{1,0:T(8,128)(2,1)S(1)} %collective-permute-done.31.refs_5_), channel_id=1, source_target_pairs={{0,1},{1,0},{2,3},{3,2},{4,5},{5,4},{6,7},{7,6},{8,9},{9,8},{10,11... | collective-permute-start | bytes 3538952 | tf_op jit(solution)/shard_map/ppermute | solution.py:429
  225.2 22.2 %collective-permute-start.34 = (bf16[384,384]{1,0:T(8,128)(2,1)}, bf16[384,384]{1,0:T(8,128)(2,1)S(1)}, u32[]{:S(2)}, u32[]{:S(2)}) collective-permute-start(bf16[384,384]{1,0:T(8,128)(2,1)} %get-tuple-element.217), channel_id=1, source_target_pairs={{0,2},{2,0},{16,18},{18,16},{1,3},{3,1},{17,19},{19,17},{4,6},{6,4... | collective-permute-start | bytes 884744 | tf_op jit(solution)/shard_map/ppermute | solution.py:337
  226.7 20.7 %collective-permute-start.35 = (bf16[384,384]{1,0:T(8,128)(2,1)}, bf16[384,384]{1,0:T(8,128)(2,1)S(1)}, u32[]{:S(2)}, u32[]{:S(2)}) collective-permute-start(bf16[384,384]{1,0:T(8,128)(2,1)} %get-tuple-element.216), channel_id=1, source_target_pairs={{0,16},{2,18},{16,0},{18,2},{1,17},{3,19},{17,1},{19,3},{4,20},{6,... | collective-permute-start | bytes 884744 | tf_op jit(solution)/shard_map/ppermute | solution.py:337
  229.2 3.2 %copy-start.21 = (bf16[192,3072]{1,0:T(8,128)(2,1)}, bf16[192,3072]{1,0:T(8,128)(2,1)S(1)}, u32[]{:S(2)}) copy-start(bf16[192,3072]{1,0:T(8,128)(2,1)S(1)} %collective-permute-done.39.refs_3_) | copy-start | bytes 3538948
  229.2 18.3 %collective-permute-start.36 = (bf16[384,384]{1,0:T(8,128)(2,1)}, bf16[384,384]{1,0:T(8,128)(2,1)}, u32[]{:S(2)}, u32[]{:S(2)}) collective-permute-start(bf16[384,384]{1,0:T(8,128)(2,1)} %get-tuple-element.215), channel_id=1, source_target_pairs={{0,18},{2,16},{16,2},{18,0},{1,19},{3,17},{17,3},{19,1},{4,22},{6,... | collective-permute-start | bytes 884744 | tf_op jit(solution)/shard_map/ppermute | solution.py:337
  229.7 2.6 %copy-start.22 = (bf16[192,3072]{1,0:T(8,128)(2,1)}, bf16[192,3072]{1,0:T(8,128)(2,1)S(1)}, u32[]{:S(2)}) copy-start(bf16[192,3072]{1,0:T(8,128)(2,1)S(1)} %collective-permute-done.40.refs_6_) | copy-start | bytes 3538948
  229.7 15.0 %collective-permute-start.37 = (bf16[384,128]{1,0:T(8,128)(2,1)S(1)}, bf16[384,128]{1,0:T(8,128)(2,1)S(1)}, u32[]{:S(2)}, u32[]{:S(2)}) collective-permute-start(bf16[384,128]{1,0:T(8,128)(2,1)S(1)} %get-tuple-element.220), channel_id=1, source_target_pairs={{4,0},{6,2},{8,12},{10,14},{20,16},{22,18},{24,28},{26,30},{5,1},{... | collective-permute-start | bytes 294920 | tf_op jit(solution)/shard_map/ppermute | solution.py:464
  231.1 15.0 %collective-permute-start.38 = (bf16[384,128]{1,0:T(8,128)(2,1)S(1)}, bf16[384,128]{1,0:T(8,128)(2,1)S(1)}, u32[]{:S(2)}, u32[]{:S(2)}) collective-permute-start(bf16[384,128]{1,0:T(8,128)(2,1)S(1)} %get-tuple-element.219), channel_id=1, source_target_pairs={{4,2},{6,0},{8,14},{10,12},{20,18},{22,16},{24,30},{26,28},{5,3},{... | collective-permute-start | bytes 294920 | tf_op jit(solution)/shard_map/ppermute | solution.py:464
  244.7 10.8 %collective-permute-start.42 = (bf16[384,128]{1,0:T(8,128)(2,1)S(1)}, bf16[384,128]{1,0:T(8,128)(2,1)S(1)}, u32[]{:S(2)}, u32[]{:S(2)}) collective-permute-start(bf16[384,128]{1,0:T(8,128)(2,1)S(1)} %get-tuple-element.222), channel_id=1, source_target_pairs={{4,16},{6,18},{8,28},{10,30},{20,0},{22,2},{24,12},{26,14},{5,17},... | collective-permute-start | bytes 294920 | tf_op jit(solution)/shard_map/ppermute | solution.py:464
  246.0 11.6 %collective-permute-start.43 = (bf16[384,128]{1,0:T(8,128)(2,1)S(1)}, bf16[384,128]{1,0:T(8,128)(2,1)S(1)}, u32[]{:S(2)}, u32[]{:S(2)}) collective-permute-start(bf16[384,128]{1,0:T(8,128)(2,1)S(1)} %get-tuple-element.221), channel_id=1, source_target_pairs={{4,18},{6,16},{8,30},{10,28},{20,2},{22,0},{24,14},{26,12},{5,19},... | collective-permute-start | bytes 294920 | tf_op jit(solution)/shard_map/ppermute | solution.py:464
  (7 other events, 9.0 us)
